TPU v7x, 32 devices: a whole 2x2x4 slice. The times are simulated.
32 devices in a mesh: dp: 4 (over y, x), seq: 4 (over z), shard: 2 (over core).
Axes of the slice: x: 2, y: 2, z: 4, core: 2. Of those that a mesh axis runs over, the one named last changes fastest.
Arguments:
- tokens: bfloat16 [8, 4096, 1024], P(('dp', 'shard'), 'seq'), may hold values from -6 to 6
- segments: int32 [8, 4096], P(('dp', 'shard')), may hold values from 0 to 2, as said below
- cotangent: bfloat16 [8, 4096, 1024], P(('dp', 'shard'), 'seq'), may hold values from -6 to 6
- norm_one: float32 [1024], P('shard'), may hold values from 0.5 to 1.5
- in_weight: float32 [1024, 3072], P('shard'), may hold values from -0.1875 to 0.1875
- conv_weight: float32 [3, 1024], P(None, 'shard'), may hold values from -3 to 3
- out_weight: float32 [1024, 1024], P('shard'), may hold values from -0.1875 to 0.1875
- norm_two: float32 [1024], P('shard'), may hold values from 0.5 to 1.5
- gate_weight: float32 [1024, 4608], P('shard'), may hold values from -0.1875 to 0.1875
- up_weight: float32 [1024, 4608], P('shard'), may hold values from -0.1875 to 0.1875
- down_weight: float32 [4608, 1024], P('shard'), may hold values from -0.1875 to 0.1875
- moment_norm_one: float32 [1024], P('shard'), may hold values from -1.5 to 1.5
- moment_in: float32 [1024, 3072], P('shard'), may hold values from -1.5 to 1.5
- moment_conv: float32 [3, 1024], P(None, 'shard'), may hold values from -1.5 to 1.5
- moment_out: float32 [1024, 1024], P('shard'), may hold values from -1.5 to 1.5
- moment_norm_two: float32 [1024], P('shard'), may hold values from -1.5 to 1.5
- moment_gate: float32 [1024, 4608], P('shard'), may hold values from -1.5 to 1.5
- moment_up: float32 [1024, 4608], P('shard'), may hold values from -1.5 to 1.5
- moment_down: float32 [4608, 1024], P('shard'), may hold values from -1.5 to 1.5
- learn_rate: float32 [], replicated, may hold values from 0.01 to 0.1
- step_number: int32 [], replicated, may hold values from 0 to 3999
Outputs:
- block_out: bfloat16 [8, 4096, 1024], P(('dp', 'shard'), 'seq')
- input_grad: bfloat16 [8, 4096, 1024], P(('dp', 'shard'), 'seq')
- grad_norm: float32 [], replicated
- next_moment_norm_one: float32 [1024], P('shard')
- next_moment_in: float32 [1024, 3072], P('shard')
- next_moment_conv: float32 [3, 1024], P(None, 'shard')
- next_moment_out: float32 [1024, 1024], P('shard')
- next_moment_norm_two: float32 [1024], P('shard')
- next_moment_gate: float32 [1024, 4608], P('shard')
- next_moment_up: float32 [1024, 4608], P('shard')
- next_moment_down: float32 [4608, 1024], P('shard')
- next_in_weight: bfloat16 [1024, 3072], replicated
- next_out_weight: bfloat16 [1024, 1024], replicated
- next_gate_weight: bfloat16 [1024, 4608], replicated
- next_up_weight: bfloat16 [1024, 4608], replicated
- next_down_weight: bfloat16 [4608, 1024], replicated
Inputs may be any that keep to these rules, and one draw needn't show every extreme that they name: `segments`: each sequence is packed from three documents: the numbers start at 0, never fall, and rise by one at exactly two positions. The first two documents each have between 1228 and 1638 tokens; the third fills the rest of the sequence.
All inputs are finite; a program needn't handle non-finite values.
Results may differ from a plain program's by a relative error of at most 0.012.
The roundings to bfloat16 on the way count: a program that leaves them out, or rounds other values in their place, can miss the bound.
Values may be sent and summed in bfloat16 or wider, within the bound.
A program may use at most 448 MiB of HBM per device.

v0:
```python
import math

import jax
import jax.numpy as jnp
from jax import lax
from jax.sharding import PartitionSpec as P

WARMUP = 2000


EPSILON = 1e-05
MOMENTUM_BETA = 0.9
WEIGHT_DECAY = 0.1
CLIP_RATIO = 0.25


def from_behind(block, axis, distance):
    devices = range(lax.axis_size(axis))
    route = [(i - distance, i) for i in devices if i - distance in devices]
    return lax.ppermute(block, axis, route)


def rows_dot(left, right):
    return jnp.dot(left, right, preferred_element_type=jnp.float32)


def outer_dot(left, right):
    return lax.dot_general(
        left, right, (((0,), (0,)), ((), ())), preferred_element_type=jnp.float32
    )


def back_dot(left, right):
    return lax.dot_general(
        left, right, (((1,), (1,)), ((), ())), preferred_element_type=jnp.float32
    )


def norm_forward(values, gain):
    scale = lax.rsqrt(jnp.mean(values * values, axis=-1, keepdims=True) + EPSILON)
    return (values * scale * gain, scale)


def norm_backward(values, scale, gain, upstream):
    gain_grad = jnp.sum(upstream * values * scale, axis=0)
    inner = jnp.mean(values * gain * upstream, axis=-1, keepdims=True)
    return (scale * gain * upstream - values * scale * scale * scale * inner, gain_grad)


def segment_window(extended, start, offset, length):
    return lax.dynamic_slice_in_dim(extended, start + 2 + offset, length, 1)


def new_moments(gradients, moments, clip_factor):
    return tuple(
        (
            MOMENTUM_BETA * moment + clip_factor * gradient
            for moment, gradient in zip(moments, gradients)
        )
    )


def new_weights(masters, next_moments, rate_now):
    return tuple(
        (
            (master * (1.0 - rate_now * WEIGHT_DECAY) - rate_now * moment).astype(jnp.bfloat16)
            for master, moment in zip(masters, next_moments)
        )
    )


def local(
    tokens,
    segments,
    cotangent,
    norm_one,
    in_weight,
    conv_weight,
    out_weight,
    norm_two,
    gate_weight,
    up_weight,
    down_weight,
    moment_norm_one,
    moment_in,
    moment_conv,
    moment_out,
    moment_norm_two,
    moment_gate,
    moment_up,
    moment_down,
    learn_rate,
    step_number,
):
    masters = (
        norm_one,
        in_weight,
        conv_weight,
        out_weight,
        norm_two,
        gate_weight,
        up_weight,
        down_weight,
    )
    moments = (
        moment_norm_one,
        moment_in,
        moment_conv,
        moment_out,
        moment_norm_two,
        moment_gate,
        moment_up,
        moment_down,
    )
    whole = (
        lax.all_gather(norm_one.astype(jnp.bfloat16), "shard", axis=0, tiled=True),
        lax.all_gather(in_weight.astype(jnp.bfloat16), "shard", axis=0, tiled=True),
        lax.all_gather(conv_weight.astype(jnp.bfloat16), "shard", axis=1, tiled=True),
        lax.all_gather(out_weight.astype(jnp.bfloat16), "shard", axis=0, tiled=True),
        lax.all_gather(norm_two.astype(jnp.bfloat16), "shard", axis=0, tiled=True),
        lax.all_gather(gate_weight.astype(jnp.bfloat16), "shard", axis=0, tiled=True),
        lax.all_gather(up_weight.astype(jnp.bfloat16), "shard", axis=0, tiled=True),
        lax.all_gather(down_weight.astype(jnp.bfloat16), "shard", axis=0, tiled=True),
    )
    gain_one = whole[0].astype(jnp.float32)
    in_matrix = whole[1]
    conv_taps = whole[2].astype(jnp.float32)
    out_matrix = whole[3]
    gain_two = whole[4].astype(jnp.float32)
    gate_matrix = whole[5]
    up_matrix = whole[6]
    down_matrix = whole[7]
    seq_count, span, model_width = tokens.shape
    row_count = seq_count * span
    hidden_in = tokens.reshape(row_count, model_width).astype(jnp.float32)
    start = lax.axis_index("seq") * span
    padding = jnp.full((seq_count, 2), -1, jnp.int32)
    extended = jnp.concatenate([padding, segments, padding], 1)
    current = segment_window(extended, start, 0, span)
    keep_one = (
        (segment_window(extended, start, -1, span) == current)
        .astype(jnp.float32)
        .reshape(row_count, 1)
    )
    keep_two = (
        (segment_window(extended, start, -2, span) == current)
        .astype(jnp.float32)
        .reshape(row_count, 1)
    )
    next_one = (
        (segment_window(extended, start, 1, span) == current)
        .astype(jnp.float32)
        .reshape(row_count, 1)
    )
    next_two = (
        (segment_window(extended, start, 2, span) == current)
        .astype(jnp.float32)
        .reshape(row_count, 1)
    )
    normed_f, scale_one = norm_forward(hidden_in, gain_one)
    normed_one = normed_f.astype(jnp.bfloat16)
    projected = rows_dot(normed_one, in_matrix)
    gate_b = projected[:, :model_width]
    gate_c = projected[:, model_width : 2 * model_width]
    values = projected[:, 2 * model_width :]
    mixed_in = gate_b * values
    mixed_grid = mixed_in.reshape(seq_count, span, model_width)
    before_edge = from_behind(mixed_grid[:, span - 2 :, :], "seq", 1)
    before = jnp.concatenate([before_edge, mixed_grid], 1)
    before_one = before[:, 1:-1, :].reshape(row_count, model_width)
    before_two = before[:, :-2, :].reshape(row_count, model_width)
    convolved = (
        conv_taps[2] * mixed_in
        + conv_taps[1] * keep_one * before_one
        + conv_taps[0] * keep_two * before_two
    )
    mixer_out = (gate_c * convolved).astype(jnp.bfloat16)
    hidden = hidden_in + rows_dot(mixer_out, out_matrix)
    normed_g, scale_two = norm_forward(hidden, gain_two)
    normed_two = normed_g.astype(jnp.bfloat16)
    gate_pre = rows_dot(normed_two, gate_matrix)
    upward = rows_dot(normed_two, up_matrix)
    sigmoid_gate = jax.nn.sigmoid(gate_pre)
    activated = (gate_pre * sigmoid_gate * upward).astype(jnp.bfloat16)
    block_out = (
        (hidden + rows_dot(activated, down_matrix)).astype(jnp.bfloat16).reshape(tokens.shape)
    )
    cotangent_rows = cotangent.reshape(row_count, model_width)
    down_grad = outer_dot(activated, cotangent_rows)
    act_grad = back_dot(cotangent_rows, down_matrix)
    gate_back = (act_grad * upward * sigmoid_gate * (1.0 + gate_pre * (1.0 - sigmoid_gate))).astype(
        jnp.bfloat16
    )
    up_back = (act_grad * gate_pre * sigmoid_gate).astype(jnp.bfloat16)
    gate_grad = outer_dot(normed_two, gate_back)
    up_grad = outer_dot(normed_two, up_back)
    normed_two_grad = back_dot(gate_back, gate_matrix) + back_dot(up_back, up_matrix)
    hidden_part, gain_two_grad = norm_backward(hidden, scale_two, gain_two, normed_two_grad)
    hidden_grad = cotangent_rows.astype(jnp.float32) + hidden_part
    hidden_low = hidden_grad.astype(jnp.bfloat16)
    out_grad = outer_dot(mixer_out, hidden_low)
    mixer_grad = back_dot(hidden_low, out_matrix)
    gate_c_grad = mixer_grad * convolved
    conv_out_grad = mixer_grad * gate_c
    conv_grid = conv_out_grad.reshape(seq_count, span, model_width)
    after_edge = from_behind(conv_grid[:, :2, :], "seq", -1)
    after = jnp.concatenate([conv_grid, after_edge], 1)
    follow_one = after[:, 1:-1, :].reshape(row_count, model_width)
    follow_two = after[:, 2:, :].reshape(row_count, model_width)
    mixed_grad = (
        conv_taps[2] * conv_out_grad
        + conv_taps[1] * next_one * follow_one
        + conv_taps[0] * next_two * follow_two
    )
    conv_grad = jnp.stack(
        [
            jnp.sum(conv_out_grad * keep_two * before_two, axis=0),
            jnp.sum(conv_out_grad * keep_one * before_one, axis=0),
            jnp.sum(conv_out_grad * mixed_in, axis=0),
        ],
        0,
    )
    proj_back = jnp.concatenate([mixed_grad * values, gate_c_grad, mixed_grad * gate_b], 1).astype(
        jnp.bfloat16
    )
    in_grad = outer_dot(normed_one, proj_back)
    normed_one_grad = back_dot(proj_back, in_matrix)
    input_part, gain_one_grad = norm_backward(hidden_in, scale_one, gain_one, normed_one_grad)
    input_grad = (hidden_grad + input_part).astype(jnp.bfloat16).reshape(tokens.shape)
    shares = (
        lax.psum_scatter(gain_one_grad, "shard", scatter_dimension=0, tiled=True),
        lax.psum_scatter(in_grad, "shard", scatter_dimension=0, tiled=True),
        lax.psum_scatter(conv_grad, "shard", scatter_dimension=1, tiled=True),
        lax.psum_scatter(out_grad, "shard", scatter_dimension=0, tiled=True),
        lax.psum_scatter(gain_two_grad, "shard", scatter_dimension=0, tiled=True),
        lax.psum_scatter(gate_grad, "shard", scatter_dimension=0, tiled=True),
        lax.psum_scatter(up_grad, "shard", scatter_dimension=0, tiled=True),
        lax.psum_scatter(down_grad, "shard", scatter_dimension=0, tiled=True),
    )
    param_count = sum((member.size for member in whole))
    clip_level = CLIP_RATIO * math.sqrt(param_count)
    rate_now = learn_rate * jnp.minimum(1.0, (step_number + 1).astype(jnp.float32) / WARMUP)
    large_places = (1, 3, 5, 6, 7)
    summed = lax.psum(
        (shares[0], shares[1], shares[2], shares[3], shares[4], shares[5], shares[6], shares[7]),
        ("dp", "seq"),
    )
    squares_local = sum((jnp.sum(member * member) for member in summed))
    squares_sum = lax.psum(squares_local, "shard")
    grad_norm = jnp.sqrt(squares_sum)
    clip_factor = clip_level / jnp.maximum(grad_norm, clip_level)
    next_moments = new_moments(summed, moments, clip_factor)
    large_low = new_weights(
        tuple((masters[place] for place in large_places)),
        tuple((next_moments[place] for place in large_places)),
        rate_now,
    )
    weights = (
        lax.all_gather(large_low[0], "shard", axis=0, tiled=True),
        lax.all_gather(large_low[1], "shard", axis=0, tiled=True),
        lax.all_gather(large_low[2], "shard", axis=0, tiled=True),
        lax.all_gather(large_low[3], "shard", axis=0, tiled=True),
        lax.all_gather(large_low[4], "shard", axis=0, tiled=True),
    )
    return (
        block_out,
        input_grad,
        grad_norm,
        next_moments[0],
        next_moments[1],
        next_moments[2],
        next_moments[3],
        next_moments[4],
        next_moments[5],
        next_moments[6],
        next_moments[7],
        weights[0],
        weights[1],
        weights[2],
        weights[3],
        weights[4],
    )


def solution(mesh):
    placed = (
        P(("dp", "shard"), "seq", None),
        P(("dp", "shard"), None),
        P(("dp", "shard"), "seq", None),
        P("shard"),
        P("shard", None),
        P(None, "shard"),
        P("shard", None),
        P("shard"),
        P("shard", None),
        P("shard", None),
        P("shard", None),
        P("shard"),
        P("shard", None),
        P(None, "shard"),
        P("shard", None),
        P("shard"),
        P("shard", None),
        P("shard", None),
        P("shard", None),
        P(),
        P(),
    )
    return jax.shard_map(
        local,
        mesh=mesh,
        in_specs=placed,
        out_specs=(
            P(("dp", "shard"), "seq", None),
            P(("dp", "shard"), "seq", None),
            P(),
            P("shard"),
            P("shard", None),
            P(None, "shard"),
            P("shard", None),
            P("shard"),
            P("shard", None),
            P("shard", None),
            P("shard", None),
            P(),
            P(),
            P(),
            P(),
            P(),
        ),
        check_vma=False,
    )
```

profile of v0, /device:TPU:0, one launch (start us, length us, event | category | flops | bytes accessed | tf_op | source)
XLA Modules:
  0.0 1527.4 jit_solution(2687070820012980385)
XLA Ops:
  13.6 6.4 convert_element_type.105
  20.0 8.0 convert_element_type.106
  28.1 6.9 convert_element_type.108
  42.4 9.5 fusion.36
  71.9 11.3 multiply_convert_fusion.7
  92.9 17.8 %fusion.43 = f32[1024,4608]{1,0:T(8,128)} fusion(bf16[1024,1024]{0,1:T(8,128)(2,1)S(1)} %multiply_convert_fusion.6, bf16[1024,4608]{1,0:T(8,128)(2,1)} %all-gather.17.cloned.1.call-done), kind=kOutput, calls=%fused_computation.104 | convolution fusion | flops 9663676416 | bytes 30408704 | tf_op jit(solution)/shard_map/dot_general | solution.py:24
  110.7 18.1 %fusion.44 = f32[1024,4608]{1,0:T(8,128)} fusion(bf16[1024,1024]{0,1:T(8,128)(2,1)} %copy-done.15, bf16[1024,4608]{1,0:T(8,128)(2,1)} %all-gather.19.cloned.1.call-done), kind=kOutput, calls=%fused_computation.105 | convolution fusion | flops 9663676416 | bytes 30408704 | tf_op jit(solution)/shard_map/dot_general | solution.py:24
  128.8 30.9 %multiply_convert_fusion = (bf16[1024,4608]{1,0:T(8,128)(2,1)}, bf16[1024,4608]{1,0:T(8,128)(2,1)}, bf16[1024,4608]{1,0:T(8,128)(2,1)}) fusion(f32[1024,4608]{1,0:T(8,128)} %fusion.43, f32[1024,4608]{1,0:T(8,128)} %fusion.44, bf16[4608,1024]{1,0:T(8,128)(2,1)} %all-gather.21.cloned.1.call-done, bf16[1,1024,1024]{2,1,0:T(8,128)(2,1)S(1)} %copy-done.13), kind=kOutput, calls=%fused_computation | convolution fusion | flops 9739173888 | bytes 77594624 | tf_op jit(solution)/shard_map/dot_general | solution.py:34
  159.7 14.2 fusion.45
  173.9 16.8 %multiply_reduce_fusion.4 = (f32[1024]{0:T(1024)}, f32[1024]{0:T(1024)S(1)}, f32[1024,1024]{0,1:T(8,128)S(1)}) fusion(f32[1024,1024]{0,1:T(8,128)S(1)} %copy-done.7, f32[1024]{0:T(1024)S(1)} %add_rsqrt_fusion, f32[1024]{0:T(1024)S(1)} %bitcast.109, f32[1024,1024]{0,1:T(8,128)S(1)} %fusion.45, bf16[1024,4608]{1,0:T(8,128)(2,1)} %get-tuple-element.80, ...), kind=kOutput, calls=%fused_computation.51 | convolution fusion | flops 9671014400 | bytes 31473664 | tf_op jit(solution)/shard_map/dot_general | solution.py:34
  198.5 7.4 fusion.33
  206.0 12.7 multiply_reduce_fusion.7
  225.0 9.8 multiply_convert_fusion.5
  237.8 11.6 fusion.23
  249.4 19.2 %fusion.46 = f32[1024,4608]{1,0:T(8,128)} fusion(bf16[1024,1024]{0,1:T(8,128)(2,1)} %copy-done.15, bf16[1024,4608]{1,0:T(8,128)(2,1)} %get-tuple-element.81), kind=kOutput, calls=%fused_computation.107 | convolution fusion | flops 9663676416 | bytes 30408704 | tf_op jit(solution)/shard_map/dot_general | solution.py:28
  268.7 19.4 %fusion.47 = f32[1024,4608]{1,0:T(8,128)} fusion(bf16[1024,1024]{0,1:T(8,128)(2,1)} %copy-done.15, bf16[1024,4608]{1,0:T(8,128)(2,1)} %get-tuple-element.80), kind=kOutput, calls=%fused_computation.108 | convolution fusion | flops 9663676416 | bytes 30408704 | tf_op jit(solution)/shard_map/dot_general | solution.py:28
  288.2 18.4 %fusion.27 = f32[4608,1024]{1,0:T(8,128)} fusion(bf16[1024,4608]{1,0:T(8,128)(2,1)} %get-tuple-element.82, bf16[1,1024,1024]{2,1,0:T(8,128)(2,1)} %param.23), kind=kOutput, calls=%fused_computation.71 | convolution fusion | flops 9663676416 | bytes 30408704 | tf_op jit(solution)/shard_map/dot_general | solution.py:28
  307.9 27.3 %reduce-scatter.15.cloned.1.call-done = f32[512,4608]{1,0:T(8,128)} async-done(((f32[1024,4608]{1,0:T(8,128)}), f32[512,4608]{1,0:T(8,128)}) %reduce-scatter.15.cloned.1.call-update) | async-done | bytes 9437200 | tf_op jit(solution)/shard_map/reduce_scatter | solution.py:237
  335.2 31.8 %reduce-scatter.17.cloned.1.call-done = f32[2304,1024]{1,0:T(8,128)} async-done(((f32[4608,1024]{1,0:T(8,128)}), f32[2304,1024]{1,0:T(8,128)}) %reduce-scatter.17.cloned.1.call-update) | async-done | bytes 9437200 | tf_op jit(solution)/shard_map/reduce_scatter | solution.py:238
  369.7 12.8 fusion.19
  386.2 82.1 %all-reduce.2 = (f32[512]{0:T(512)S(1)}, f32[3,512]{1,0:T(4,128)S(1)}, f32[512]{0:T(512)S(1)}) all-reduce(f32[512]{0:T(512)S(1)} %dynamic-slice.1, f32[3,512]{1,0:T(4,128)S(1)} %copy.62, f32[512]{0:T(512)S(1)} %dynamic-slice.3), channel_id=1, replica_groups=mesh['dp'=4,'seq'=4,'shard'=2] {'dp','seq'}, use_global_device_ids=true, to_apply=%region_6.0 | all-reduce | flops 2560 | bytes 20480 | tf_op jit(solution)/shard_map/psum | solution.py:244
  470.1 878.9 %all-reduce.7.cloned.1.call-done = (f32[512,3072]{1,0:T(8,128)}, f32[512,1024]{1,0:T(8,128)}, f32[512,4608]{1,0:T(8,128)}, f32[512,4608]{1,0:T(8,128)}, f32[2304,1024]{1,0:T(8,128)}) async-done(((f32[512,3072]{1,0:T(8,128)}, f32[512,1024]{1,0:T(8,128)}, f32[512,4608]{1,0:T(8,128)}, f32[512,4608]{1,0:T(8,128)}, f32[2304,1024]{1,0:T(8,128)}), (f32[512,3072]{1,0:T(8,128)}, f32[512,1024]{1,0:T(8,128)}, ...) | async-done | bytes 36700176 | tf_op jit(solution)/shard_map/psum | solution.py:244
  1355.3 6.9 multiply_reduce_fusion.2
  1382.8 12.0 subtract_convert_fusion.3
  1394.9 18.2 %subtract_convert_fusion = (bf16[2304,1024]{1,0:T(8,128)(2,1)}, f32[2304,1024]{1,0:T(8,128)}) fusion(f32[2304,1024]{1,0:T(8,128)} %param.31, f32[]{:T(128)S(6)} %mul.594, f32[]{:T(128)S(6)} %sub.34, f32[2304,1024]{1,0:T(8,128)} %get-tuple-element.62, f32[]{:T(128)S(6)} %div.26, f32[2304,1024]{1,0:T(8,128)} %param.39), kind=kLoop, calls=%fused_computation.4 | loop fusion | flops 16515072 | bytes 42467340 | tf_op jit(solution)/shard_map/convert_element_type | solution.py:66
  1413.2 17.8 %subtract_convert_fusion.1 = (bf16[512,4608]{1,0:T(8,128)(2,1)}, f32[512,4608]{1,0:T(8,128)}) fusion(f32[512,4608]{1,0:T(8,128)} %param.30, f32[]{:T(128)S(6)} %mul.594, f32[]{:T(128)S(6)} %sub.34, f32[512,4608]{1,0:T(8,128)} %get-tuple-element.61, f32[]{:T(128)S(6)} %div.26, f32[512,4608]{1,0:T(8,128)} %param.38), kind=kLoop, calls=%fused_computation.5 | loop fusion | flops 16515072 | bytes 42467340 | tf_op jit(solution)/shard_map/convert_element_type | solution.py:66
  1431.0 16.9 %subtract_convert_fusion.2 = (bf16[512,4608]{1,0:T(8,128)(2,1)}, f32[512,4608]{1,0:T(8,128)}) fusion(f32[512,4608]{1,0:T(8,128)} %param.29, f32[]{:T(128)S(6)} %mul.594, f32[]{:T(128)S(6)} %sub.34, f32[512,4608]{1,0:T(8,128)} %get-tuple-element.60, f32[]{:T(128)S(6)} %div.26, f32[512,4608]{1,0:T(8,128)} %param.37), kind=kLoop, calls=%fused_computation.6 | loop fusion | flops 16515072 | bytes 42467340 | tf_op jit(solution)/shard_map/convert_element_type | solution.py:66
  1448.0 19.5 %fusion.25 = bf16[1,1024,1024]{1,2,0:T(8,128)(2,1)} fusion(f32[1024,1024]{0,1:T(8,128)} %copy-done.6, bf16[1024,4608]{1,0:T(8,128)(2,1)} %get-tuple-element.82, bf16[4608,1024]{1,0:T(8,128)(2,1)} %all-gather.21.cloned.1.call-done), kind=kOutput, calls=%fused_computation.69 | convolution fusion | flops 9665773568 | bytes 25165824 | tf_op jit(solution)/shard_map/dot_general | solution.py:24
  1471.4 7.7 fusion.26
  1494.7 8.0 copy.77
  1502.7 8.0 copy.78
  1510.7 8.5 copy.79
  (200 shorter events, 108.6 us)
Async XLA Ops:
  7.2 35.2 %all-gather.13.cloned.1.call-start = ((), (), s32[]{:S(2)}) async-start(), calls=%async_computation.6 | async-start | bytes 9437184 | tf_op jit(solution)/shard_map/all_gather | solution.py:117
  12.3 71.0 %all-gather.15.cloned.1.call-start = ((), (), s32[]{:S(2)}) async-start(), calls=%async_computation.7 | async-start | bytes 3145728 | tf_op jit(solution)/shard_map/all_gather | solution.py:119
  13.5 78.1 %all-gather.17.cloned.1.call-start = ((), (), s32[]{:S(2)}) async-start(), calls=%async_computation.8 | async-start | bytes 14155776 | tf_op jit(solution)/shard_map/all_gather | solution.py:121
  20.0 90.7 %all-gather.19.cloned.1.call-start = ((), (), s32[]{:S(2)}) async-start(), calls=%async_computation.9 | async-start | bytes 14155776 | tf_op jit(solution)/shard_map/all_gather | solution.py:122
  28.0 100.8 %all-gather.21.cloned.1.call-start = ((), (), s32[]{:S(2)}) async-start(), calls=%async_computation.10 | async-start | bytes 14155776 | tf_op jit(solution)/shard_map/all_gather | solution.py:123
  35.0 272.8 %reduce-scatter.11.cloned.1.call-start = ((), (), s32[]{:S(2)}) async-start(), calls=%async_computation.12 | async-start | bytes 6291456 | tf_op jit(solution)/shard_map/reduce_scatter | solution.py:234
  38.0 45.3 %copy-start.3 = (bf16[1,1024,1024]{1,2,0:T(8,128)(2,1)}, bf16[1,1024,1024]{1,2,0:T(8,128)(2,1)S(1)}, u32[]{:S(2)}) copy-start(bf16[1,1024,1024]{1,2,0:T(8,128)(2,1)S(1)} %copy.47) | copy-start | bytes 6291460
  42.2 29.7 %copy-start.16 = (f32[1,1024]{1,0:T(1,128)}, f32[1,1024]{1,0:T(1,128)S(1)}, u32[]{:S(2)}) copy-start(f32[1,1024]{1,0:T(1,128)S(1)} %get-tuple-element.88) | copy-start | bytes 12292
  42.2 29.7 %copy-start.18 = (f32[1,1024]{1,0:T(1,128)}, f32[1,1024]{1,0:T(1,128)S(1)}, u32[]{:S(2)}) copy-start(f32[1,1024]{1,0:T(1,128)S(1)} %get-tuple-element.89) | copy-start | bytes 12292
  42.2 29.7 %copy-start.20 = (f32[1,1024]{1,0:T(1,128)}, f32[1,1024]{1,0:T(1,128)S(1)}, u32[]{:S(2)}) copy-start(f32[1,1024]{1,0:T(1,128)S(1)} %get-tuple-element.90) | copy-start | bytes 12292
  59.8 12.1 collective-permute-start
  110.7 18.1 %copy-start.13 = (bf16[1,1024,1024]{2,1,0:T(8,128)(2,1)S(1)}, bf16[1,1024,1024]{2,1,0:T(8,128)(2,1)}, u32[]{:S(2)}) copy-start(bf16[1,1024,1024]{2,1,0:T(8,128)(2,1)} %param.23) | copy-start | bytes 6291460
  198.4 109.4 %reduce-scatter.9.cloned.1.call-start = ((), (), s32[]{:S(2)}) async-start(), calls=%async_computation.11 | async-start | bytes 18874368 | tf_op jit(solution)/shard_map/reduce_scatter | solution.py:232
  198.5 26.4 %slice-start = ((s8[12582912]{0:T(1024)(128)(4,1)}), s8[4194304]{0:T(1024)(128)(4,1)S(1)}, s32[]{:S(2)}) async-start(s8[12582912]{0:T(1024)(128)(4,1)} %bitcast.94), calls=%async_computation.23 | async-start | bytes 8388608
  198.5 26.4 %slice-start.1 = ((s8[12582912]{0:T(1024)(128)(4,1)}), s8[4194304]{0:T(1024)(128)(4,1)S(1)}, s32[]{:S(2)}) async-start(s8[12582912]{0:T(1024)(128)(4,1)} %bitcast.94), calls=%async_computation.24 | async-start | bytes 8388608
  205.9 19.0 %slice-start.2 = ((s8[12582912]{0:T(1024)(128)(4,1)}), s8[4194304]{0:T(1024)(128)(4,1)S(1)}, s32[]{:S(2)}) async-start(s8[12582912]{0:T(1024)(128)(4,1)} %bitcast.94), calls=%async_computation.25 | async-start | bytes 8388608
  205.9 19.0 %copy-start.17 = (f32[1,1024]{1,0:T(1,128)S(1)}, f32[1,1024]{1,0:T(1,128)}, u32[]{:S(2)}) copy-start(f32[1,1024]{1,0:T(1,128)} %copy-done.16) | copy-start | bytes 12292
  205.9 19.0 %copy-start.19 = (f32[1,1024]{1,0:T(1,128)S(1)}, f32[1,1024]{1,0:T(1,128)}, u32[]{:S(2)}) copy-start(f32[1,1024]{1,0:T(1,128)} %copy-done.18) | copy-start | bytes 12292
  205.9 19.0 %copy-start.21 = (f32[1,1024]{1,0:T(1,128)S(1)}, f32[1,1024]{1,0:T(1,128)}, u32[]{:S(2)}) copy-start(f32[1,1024]{1,0:T(1,128)} %copy-done.20) | copy-start | bytes 12292
  205.9 19.0 %copy-start.27 = (f32[1,1024]{1,0:T(1,128)S(1)}, f32[1,1024]{1,0:T(1,128)}, u32[]{:S(2)}) copy-start(f32[1,1024]{1,0:T(1,128)} %get-tuple-element.84) | copy-start | bytes 12292
  206.0 19.0 %copy-start.28 = (f32[1,1024]{1,0:T(1,128)S(1)}, f32[1,1024]{1,0:T(1,128)}, u32[]{:S(2)}) copy-start(f32[1,1024]{1,0:T(1,128)} %get-tuple-element.86) | copy-start | bytes 12292
  219.4 5.5 collective-permute-start.1
  249.4 58.5 %reduce-scatter.13.cloned.1.call-start = ((), (), s32[]{:S(2)}) async-start(), calls=%async_computation.13 | async-start | bytes 28311552 | tf_op jit(solution)/shard_map/reduce_scatter | solution.py:236
  268.7 66.6 %reduce-scatter.15.cloned.1.call-start = ((), (), s32[]{:S(2)}) async-start(), calls=%async_computation.14 | async-start | bytes 28311552 | tf_op jit(solution)/shard_map/reduce_scatter | solution.py:237
  288.2 78.9 %reduce-scatter.17.cloned.1.call-start = ((), (), s32[]{:S(2)}) async-start(), calls=%async_computation.15 | async-start | bytes 28311552 | tf_op jit(solution)/shard_map/reduce_scatter | solution.py:238
  306.7 78.5 %reduce-scatter.19.cloned.1.call-start = ((), (), s32[]{:S(2)}) async-start(), calls=%async_computation.21 | async-start | bytes 786432
  307.8 1041.2 %all-reduce.7.cloned.1.call-start = ((), (), s32[]{:S(2)}) async-start(), calls=%async_computation.22 | async-start | bytes 73400320 | tf_op jit(solution)/shard_map/psum | solution.py:244
  367.1 1117.3 %all-gather.25.cloned.1.call-start = ((), (), s32[]{:S(2)}) async-start(), calls=%async_computation.17 | async-start | bytes 3145728 | tf_op jit(solution)/shard_map/all_gather | solution.py:260
  1382.8 101.6 %all-gather.23.cloned.1.call-start = ((), (), s32[]{:S(2)}) async-start(), calls=%async_computation.16 | async-start | bytes 9437184 | tf_op jit(solution)/shard_map/all_gather | solution.py:259
  1394.8 89.6 %all-gather.31.cloned.1.call-start = ((), (), s32[]{:S(2)}) async-start(), calls=%async_computation.20 | async-start | bytes 14155776 | tf_op jit(solution)/shard_map/all_gather | solution.py:263
  1413.1 71.3 %all-gather.29.cloned.1.call-start = ((), (), s32[]{:S(2)}) async-start(), calls=%async_computation.19 | async-start | bytes 14155776 | tf_op jit(solution)/shard_map/all_gather | solution.py:262
  1431.0 56.3 %all-gather.27.cloned.1.call-start = ((), (), s32[]{:S(2)}) async-start(), calls=%async_computation.18 | async-start | bytes 14155776 | tf_op jit(solution)/shard_map/all_gather | solution.py:261
  (33 other events, 220.5 us)
Sparse Core Ops, SparseCore 0:
  12.4 19.4 all-gather.12
  34.1 11.7 all-gather.14
  48.0 23.0 all-gather.16
  73.0 23.0 all-gather.18
  98.0 23.0 all-gather.20
  198.6 12.3 reduce-scatter.10
  249.5 21.8 reduce-scatter.8
  273.8 29.4 reduce-scatter.12
  305.6 29.5 reduce-scatter.14
  337.5 29.5 reduce-scatter.16
  370.0 9.2 reduce-scatter.18
  385.6 963.4 all-reduce.6
  1382.9 9.5 all-gather.24
  1394.9 16.9 all-gather.22
  1414.0 23.0 all-gather.30
  1439.1 23.0 all-gather.28
  1464.2 23.0 all-gather.26
where the time goes:
time: 1530 us
  waiting for transfers between devices  946 us (62%)
  matrix products  226 us (15%)
  other arithmetic  168 us (11%)
  blocking collectives  93.5 us (6%)
  local copies, waits for them, and re-layouts  63.6 us (4%)
  between operations  24 us (2%)
    psum x1, waiting for transfers between devices, local(): lax.psum((shares[0], shares[1], shares[2], shares[3], shares[4], shares[5...  879 us
    dot_general x5, matrix products, back_dot(): lax.dot_general(left, right, (((1,), (1,)), ((), ())), preferred_element_...  82.1 us
    psum x1, blocking collectives, local(): lax.psum((shares[0], shares[1], shares[2], shares[3], shares[4], shares[5...  82.1 us
    dot_general x5, matrix products, outer_dot(): lax.dot_general(left, right, (((0,), (0,)), ((), ())), preferred_element_...  73 us
    dot_general x5, matrix products, rows_dot(): return jnp.dot(left, right, preferred_element_type=jnp.float32)  70.6 us
    convert_element_type x5, other arithmetic, new_weights(): (master * (1.0 - rate_now * WEIGHT_DECAY) - rate_now * moment).astype(jnp...  70.5 us
    unnamed x108, local copies, waits for them, and re-layouts  62.6 us
    reduce_scatter x1, waiting for transfers between devices, local(): lax.psum_scatter(down_grad, 'shard', scatter_dimension=0, tiled=True)  31.8 us
  transfers between devices with their start and end apart: 19, of which 5 were waited for; matrix products, arithmetic and copies ran while one was open for 21% of the time, Pallas kernels for 0%

commit v1 on v0

--- a/solution.py
+++ b/solution.py
@@ -1,8 +1,11 @@
+import functools
 import math
 
 import jax
 import jax.numpy as jnp
 from jax import lax
+from jax.experimental import pallas as pl
+from jax.experimental.pallas import tpu as pltpu
 from jax.sharding import PartitionSpec as P
 
 WARMUP = 2000
@@ -66,6 +69,490 @@
             (master * (1.0 - rate_now * WEIGHT_DECAY) - rate_now * moment).astype(jnp.bfloat16)
             for master, moment in zip(masters, next_moments)
         )
+    )
+
+
+MESH = pl.DeviceIdType.MESH
+ANY = pl.BlockSpec(memory_space=pl.ANY)
+INTO_VMEM = pl.BlockSpec(memory_space=pltpu.VMEM)
+
+
+def finish_kernel(shapes, *refs):
+    count = len(shapes)
+    pieces = refs[:count]
+    small = refs[count]
+    wholes = refs[count + 1 : 2 * count + 1]
+    small_out, square_out = refs[2 * count + 1 : 2 * count + 3]
+    rest = refs[2 * count + 3 :]
+    from_end = rest[:count]
+    from_mid = rest[count : 2 * count]
+    done = rest[2 * count : 3 * count]
+    small_in, square_in = rest[3 * count : 3 * count + 2]
+    send, recv, small_send, small_recv, square_send, square_recv, own_sem = rest[3 * count + 2 :]
+
+    group = lax.axis_index("dp")
+    place = lax.axis_index("seq")
+    core = lax.axis_index("shard")
+    x_bit = lax.rem(group, 2)
+    y_bit = lax.div(group, 2)
+    over_x = (group + 1 - 2 * x_bit, place, core)
+    over_y = (group + 2 - 4 * y_bit, place, core)
+    sibling = (group, place, 1 - core)
+    z_near = (group, place + 1 - 2 * lax.rem(place, 2), core)
+    z_far = (group, 3 - place, core)
+    is_mid = jnp.logical_or(place == 1, place == 2)
+    is_end = jnp.logical_not(is_mid)
+    first_dev, second_dev = (over_x, over_y), (over_y, over_x)
+    first_bit, second_bit = (x_bit, y_bit), (y_bit, x_bit)
+
+    barrier = pltpu.get_barrier_semaphore()
+    for device in (over_x, over_y, sibling, z_near, z_far):
+        pl.semaphore_signal(barrier, inc=1, device_id=device, device_id_type=MESH)
+    pl.semaphore_wait(barrier, 5)
+
+    def remote(source, target, c, k, device):
+        return pltpu.make_async_remote_copy(
+            src_ref=source,
+            dst_ref=target,
+            send_sem=send.at[c, k],
+            recv_sem=recv.at[c, k],
+            device_id=device,
+            device_id_type=MESH,
+        )
+
+    def rows_of(c, h, first, second, owner):
+        unit = shapes[c][0] // 2
+        start = owner * (8 * unit) + ((h * 2 + first) * 2 + second) * unit
+        return pl.ds(pl.multiple_of(start, 16), unit)
+
+    def mine(c, h):
+        unit = shapes[c][0] // 2
+        return done[c].at[pl.ds(h * unit, unit)]
+
+    def add_rows(c, one, two, out, square=False):
+        def body(i, carry):
+            rows = pl.ds(pl.multiple_of(i * 16, 16), 16)
+            total = one[rows, :].astype(jnp.float32) + two[rows, :].astype(jnp.float32)
+            out[rows, :] = total.astype(jnp.bfloat16)
+            return carry
+
+        lax.fori_loop(0, shapes[c][0] // 16, body, 0)
+
+    def add_squares(c):
+        width = shapes[c][1]
+
+        def body(i, total):
+            rows = pl.ds(pl.multiple_of(i * 16, 16), 16)
+            block = done[c][rows, :].astype(jnp.float32)
+            block = block * block
+            block = block[:8] + block[8:]
+            for j in range(width // 128):
+                total = total + block[:, j * 128 : (j + 1) * 128]
+            return total
+
+        square_out[...] += lax.fori_loop(
+            0, shapes[c][0] // 16, body, jnp.zeros((8, 128), jnp.float32)
+        )
+
+    def z_in(c):
+        return remote(pieces[c], from_end[c], c, 0, z_near)
+
+    def z_mid(c):
+        return remote(done[c], from_mid[c], c, 1, z_far)
+
+    def z_out(c):
+        return remote(done[c], done[c], c, 2, z_near)
+
+    def to_second(c, h):
+        rows = rows_of(c, h, first_bit[h], second_bit[h], core)
+        return remote(mine(c, h), wholes[c].at[rows], c, 3 + h, second_dev[h])
+
+    def to_first(c, h):
+        rows = rows_of(c, h, first_bit[h], second_bit[h], core)
+        return remote(mine(c, h), wholes[c].at[rows], c, 5 + h, first_dev[h])
+
+    def pass_first(c, h):
+        rows = rows_of(c, h, first_bit[h], 1 - second_bit[h], core)
+        return remote(wholes[c].at[rows], wholes[c].at[rows], c, 7 + h, first_dev[h])
+
+    def to_sibling(c, h, kind):
+        first = first_bit[h] if kind < 2 else 1 - first_bit[h]
+        second = second_bit[h] if kind % 2 == 0 else 1 - second_bit[h]
+        rows = rows_of(c, h, first, second, core)
+        source = mine(c, h) if kind == 0 else wholes[c].at[rows]
+        return remote(source, wholes[c].at[rows], c, 9 + 2 * kind + h, sibling)
+
+    def keep(c, h):
+        rows = rows_of(c, h, first_bit[h], second_bit[h], core)
+        return pltpu.make_async_copy(mine(c, h), wholes[c].at[rows], own_sem.at[c, h])
+
+    def enter(c):
+        @pl.when(is_end)
+        def _():
+            z_in(c).start()
+
+    def middle_add(c):
+        @pl.when(is_mid)
+        def _():
+            z_in(c).wait_recv()
+            add_rows(c, pieces[c], from_end[c], done[c])
+            z_mid(c).start()
+
+    def middle_close(c):
+        @pl.when(is_mid)
+        def _():
+            z_mid(c).wait()
+            add_rows(c, done[c], from_mid[c], done[c])
+            z_out(c).start()
+
+        @pl.when(is_end)
+        def _():
+            z_out(c).wait_recv()
+
+    def hand_out(c):
+        for h in range(2):
+            to_second(c, h).start()
+            to_first(c, h).start()
+            to_sibling(c, h, 0).start()
+            keep(c, h).start()
+        add_squares(c)
+
+    def forward(c):
+        for h in range(2):
+            to_second(c, h).wait_recv()
+            pass_first(c, h).start()
+            to_sibling(c, h, 1).start()
+
+    def last_hop(c):
+        for h in range(2):
+            to_first(c, h).wait_recv()
+            to_sibling(c, h, 2).start()
+            pass_first(c, h).wait_recv()
+            to_sibling(c, h, 3).start()
+
+    def drain(c):
+        @pl.when(is_end)
+        def _():
+            z_in(c).wait_send()
+
+        @pl.when(is_mid)
+        def _():
+            z_out(c).wait_send()
+
+        for h in range(2):
+            to_second(c, h).wait_send()
+            to_first(c, h).wait_send()
+            pass_first(c, h).wait_send()
+            keep(c, h).wait()
+            for kind in range(4):
+                to_sibling(c, h, kind).wait()
+
+    small_route = (sibling, over_x, over_y, z_near, z_far)
+
+    def small_copy(k):
+        return pltpu.make_async_remote_copy(
+            src_ref=small_out,
+            dst_ref=small_in.at[k],
+            send_sem=small_send.at[k],
+            recv_sem=small_recv.at[k],
+            device_id=small_route[k],
+            device_id_type=MESH,
+        )
+
+    def square_copy(k):
+        return pltpu.make_async_remote_copy(
+            src_ref=square_out,
+            dst_ref=square_in.at[k],
+            send_sem=square_send.at[k],
+            recv_sem=square_recv.at[k],
+            device_id=small_route[k],
+            device_id_type=MESH,
+        )
+
+    small_out[...] = small[...]
+    square_out[...] = jnp.zeros_like(square_out)
+    enter(0)
+    small_copy(0).start()
+    for t in range(count + 3):
+        if t + 1 < count:
+            enter(t + 1)
+        if t < 5:
+            small_copy(t).wait()
+            small_out[...] += small_in[t]
+            if t < 4:
+                small_copy(t + 1).start()
+        if t < count:
+            middle_add(t)
+        if 0 <= t - 1 < count:
+            middle_close(t - 1)
+            hand_out(t - 1)
+        if 0 <= t - 2 < count:
+            forward(t - 2)
+        if t >= count:
+            k = t - count
+            if k >= 1:
+                square_copy(k - 1).wait()
+                square_out[...] += square_in[k - 1]
+            square_copy(k).start()
+        if 0 <= t - 3 < count:
+            last_hop(t - 3)
+    square_copy(2).wait()
+    square_out[...] += square_in[2]
+    for c in range(count):
+        drain(c)
+
+
+def finish(pieces, small):
+    shapes = tuple(piece.shape for piece in pieces)
+    count = len(pieces)
+    semaphore = pltpu.SemaphoreType.DMA
+    outs = pl.pallas_call(
+        functools.partial(finish_kernel, shapes),
+        out_shape=[jax.ShapeDtypeStruct((8 * r, c), jnp.bfloat16) for r, c in shapes]
+        + [
+            jax.ShapeDtypeStruct((8, small.shape[1]), jnp.float32),
+            jax.ShapeDtypeStruct((8, 128), jnp.float32),
+        ],
+        in_specs=[INTO_VMEM] * (count + 1),
+        out_specs=[ANY] * count + [INTO_VMEM] * 2,
+        scratch_shapes=[pltpu.VMEM(shape, jnp.bfloat16) for shape in shapes] * 3
+        + [
+            pltpu.VMEM((5, 8, small.shape[1]), jnp.float32),
+            pltpu.VMEM((3, 8, 128), jnp.float32),
+            semaphore((count, 17)),
+            semaphore((count, 17)),
+            semaphore((5,)),
+            semaphore((5,)),
+            semaphore((3,)),
+            semaphore((3,)),
+            semaphore((count, 2)),
+        ],
+        compiler_params=pltpu.CompilerParams(
+            collective_id=0, has_side_effects=True, vmem_limit_bytes=48 * 1024 * 1024
+        ),
+    )(*pieces, small)
+    return outs[:count], outs[count], outs[count + 1]
+
+
+def swap_first(block, axis_bit):
+    route = ((0, 1), (1, 0), (2, 3), (3, 2)) if axis_bit == 0 else ((0, 2), (2, 0), (1, 3), (3, 1))
+    return lax.ppermute(block, "dp", route)
+
+
+def halve(block, bit, axis_bit):
+    rows = block.shape[0] // 2
+    give = lax.dynamic_slice_in_dim(block, (1 - bit) * rows, rows, 0)
+    keep = lax.dynamic_slice_in_dim(block, bit * rows, rows, 0)
+    got = swap_first(give, axis_bit)
+    return (keep.astype(jnp.float32) + got.astype(jnp.float32)).astype(jnp.bfloat16)
+
+
+def scatter_piece(gradient):
+    core = lax.axis_index("shard")
+    group = lax.axis_index("dp")
+    x_bit, y_bit = lax.rem(group, 2), lax.div(group, 2)
+    rows = gradient.shape[0] // 2
+    give = lax.dynamic_slice_in_dim(gradient, (1 - core) * rows, rows, 0)
+    keep = lax.dynamic_slice_in_dim(gradient, core * rows, rows, 0)
+    got = lax.ppermute(give, "shard", ((0, 1), (1, 0)))
+    half = (keep.astype(jnp.float32) + got.astype(jnp.float32)).astype(jnp.bfloat16)
+    part = half[: rows // 2]
+    other = half[rows // 2 :]
+    part = halve(halve(part, x_bit, 0), y_bit, 1)
+    other = halve(halve(other, y_bit, 1), x_bit, 0)
+    return jnp.concatenate([part, other], 0)
+
+
+def local_fast(
+    tokens,
+    segments,
+    cotangent,
+    norm_one,
+    in_weight,
+    conv_weight,
+    out_weight,
+    norm_two,
+    gate_weight,
+    up_weight,
+    down_weight,
+    moment_norm_one,
+    moment_in,
+    moment_conv,
+    moment_out,
+    moment_norm_two,
+    moment_gate,
+    moment_up,
+    moment_down,
+    learn_rate,
+    step_number,
+):
+    masters = (
+        norm_one,
+        in_weight,
+        conv_weight,
+        out_weight,
+        norm_two,
+        gate_weight,
+        up_weight,
+        down_weight,
+    )
+    moments = (
+        moment_norm_one,
+        moment_in,
+        moment_conv,
+        moment_out,
+        moment_norm_two,
+        moment_gate,
+        moment_up,
+        moment_down,
+    )
+    whole = (
+        lax.all_gather(norm_one.astype(jnp.bfloat16), "shard", axis=0, tiled=True),
+        lax.all_gather(in_weight.astype(jnp.bfloat16), "shard", axis=0, tiled=True),
+        lax.all_gather(conv_weight.astype(jnp.bfloat16), "shard", axis=1, tiled=True),
+        lax.all_gather(out_weight.astype(jnp.bfloat16), "shard", axis=0, tiled=True),
+        lax.all_gather(norm_two.astype(jnp.bfloat16), "shard", axis=0, tiled=True),
+        lax.all_gather(gate_weight.astype(jnp.bfloat16), "shard", axis=0, tiled=True),
+        lax.all_gather(up_weight.astype(jnp.bfloat16), "shard", axis=0, tiled=True),
+        lax.all_gather(down_weight.astype(jnp.bfloat16), "shard", axis=0, tiled=True),
+    )
+    gain_one = whole[0].astype(jnp.float32)
+    in_matrix = whole[1]
+    conv_taps = whole[2].astype(jnp.float32)
+    out_matrix = whole[3]
+    gain_two = whole[4].astype(jnp.float32)
+    gate_matrix = whole[5]
+    up_matrix = whole[6]
+    down_matrix = whole[7]
+    seq_count, span, model_width = tokens.shape
+    row_count = seq_count * span
+    hidden_in = tokens.reshape(row_count, model_width).astype(jnp.float32)
+    start = lax.axis_index("seq") * span
+    padding = jnp.full((seq_count, 2), -1, jnp.int32)
+    extended = jnp.concatenate([padding, segments, padding], 1)
+    current = segment_window(extended, start, 0, span)
+    keep_one = (
+        (segment_window(extended, start, -1, span) == current)
+        .astype(jnp.float32)
+        .reshape(row_count, 1)
+    )
+    keep_two = (
+        (segment_window(extended, start, -2, span) == current)
+        .astype(jnp.float32)
+        .reshape(row_count, 1)
+    )
+    next_one = (
+        (segment_window(extended, start, 1, span) == current)
+        .astype(jnp.float32)
+        .reshape(row_count, 1)
+    )
+    next_two = (
+        (segment_window(extended, start, 2, span) == current)
+        .astype(jnp.float32)
+        .reshape(row_count, 1)
+    )
+    normed_f, scale_one = norm_forward(hidden_in, gain_one)
+    normed_one = normed_f.astype(jnp.bfloat16)
+    projected = rows_dot(normed_one, in_matrix)
+    gate_b = projected[:, :model_width]
+    gate_c = projected[:, model_width : 2 * model_width]
+    values = projected[:, 2 * model_width :]
+    mixed_in = gate_b * values
+    mixed_grid = mixed_in.reshape(seq_count, span, model_width)
+    before_edge = from_behind(mixed_grid[:, span - 2 :, :], "seq", 1)
+    before = jnp.concatenate([before_edge, mixed_grid], 1)
+    before_one = before[:, 1:-1, :].reshape(row_count, model_width)
+    before_two = before[:, :-2, :].reshape(row_count, model_width)
+    convolved = (
+        conv_taps[2] * mixed_in
+        + conv_taps[1] * keep_one * before_one
+        + conv_taps[0] * keep_two * before_two
+    )
+    mixer_out = (gate_c * convolved).astype(jnp.bfloat16)
+    hidden = hidden_in + rows_dot(mixer_out, out_matrix)
+    normed_g, scale_two = norm_forward(hidden, gain_two)
+    normed_two = normed_g.astype(jnp.bfloat16)
+    gate_pre = rows_dot(normed_two, gate_matrix)
+    upward = rows_dot(normed_two, up_matrix)
+    sigmoid_gate = jax.nn.sigmoid(gate_pre)
+    activated = (gate_pre * sigmoid_gate * upward).astype(jnp.bfloat16)
+    block_out = (
+        (hidden + rows_dot(activated, down_matrix)).astype(jnp.bfloat16).reshape(tokens.shape)
+    )
+    cotangent_rows = cotangent.reshape(row_count, model_width)
+    down_grad = outer_dot(activated, cotangent_rows).astype(jnp.bfloat16)
+    act_grad = back_dot(cotangent_rows, down_matrix)
+    gate_back = (act_grad * upward * sigmoid_gate * (1.0 + gate_pre * (1.0 - sigmoid_gate))).astype(
+        jnp.bfloat16
+    )
+    up_back = (act_grad * gate_pre * sigmoid_gate).astype(jnp.bfloat16)
+    gate_grad = outer_dot(normed_two, gate_back).astype(jnp.bfloat16)
+    up_grad = outer_dot(normed_two, up_back).astype(jnp.bfloat16)
+    normed_two_grad = back_dot(gate_back, gate_matrix) + back_dot(up_back, up_matrix)
+    hidden_part, gain_two_grad = norm_backward(hidden, scale_two, gain_two, normed_two_grad)
+    hidden_grad = cotangent_rows.astype(jnp.float32) + hidden_part
+    hidden_low = hidden_grad.astype(jnp.bfloat16)
+    out_grad = outer_dot(mixer_out, hidden_low).astype(jnp.bfloat16)
+    mixer_grad = back_dot(hidden_low, out_matrix)
+    gate_c_grad = mixer_grad * convolved
+    conv_out_grad = mixer_grad * gate_c
+    conv_grid = conv_out_grad.reshape(seq_count, span, model_width)
+    after_edge = from_behind(conv_grid[:, :2, :], "seq", -1)
+    after = jnp.concatenate([conv_grid, after_edge], 1)
+    follow_one = after[:, 1:-1, :].reshape(row_count, model_width)
+    follow_two = after[:, 2:, :].reshape(row_count, model_width)
+    mixed_grad = (
+        conv_taps[2] * conv_out_grad
+        + conv_taps[1] * next_one * follow_one
+        + conv_taps[0] * next_two * follow_two
+    )
+    conv_grad = jnp.stack(
+        [
+            jnp.sum(conv_out_grad * keep_two * before_two, axis=0),
+            jnp.sum(conv_out_grad * keep_one * before_one, axis=0),
+            jnp.sum(conv_out_grad * mixed_in, axis=0),
+        ],
+        0,
+    )
+    proj_back = jnp.concatenate([mixed_grad * values, gate_c_grad, mixed_grad * gate_b], 1).astype(
+        jnp.bfloat16
+    )
+    in_grad = outer_dot(normed_one, proj_back).astype(jnp.bfloat16)
+    normed_one_grad = back_dot(proj_back, in_matrix)
+    input_part, gain_one_grad = norm_backward(hidden_in, scale_one, gain_one, normed_one_grad)
+    input_grad = (hidden_grad + input_part).astype(jnp.bfloat16).reshape(tokens.shape)
+    core = lax.axis_index("shard")
+    pieces = [scatter_piece(g) for g in (out_grad, in_grad, gate_grad, up_grad, down_grad)]
+    small = jnp.concatenate(
+        [gain_one_grad[None], conv_grad, gain_two_grad[None], jnp.zeros((3, model_width))], 0
+    )
+    wholes, small_sum, squares = finish(pieces, small)
+    param_count = sum((member.size for member in whole))
+    clip_level = CLIP_RATIO * math.sqrt(param_count)
+    rate_now = learn_rate * jnp.minimum(1.0, (step_number + 1).astype(jnp.float32) / WARMUP)
+    grad_norm = jnp.sqrt(jnp.sum(squares) + jnp.sum(small_sum * small_sum))
+    clip_factor = clip_level / jnp.maximum(grad_norm, clip_level)
+    large = (3, 1, 5, 6, 7)
+    new_moment = {}
+    new_weight = {}
+    for place, gradient in zip(large, wholes):
+        master, moment = masters[place], moments[place]
+        rows = master.shape[0]
+        base = master * (1.0 - rate_now * WEIGHT_DECAY) - (rate_now * MOMENTUM_BETA) * moment
+        base = lax.all_gather(base.astype(jnp.bfloat16), "shard", axis=0, tiled=True)
+        new_weight[place] = (
+            base.astype(jnp.float32) - (rate_now * clip_factor) * gradient.astype(jnp.float32)
+        ).astype(jnp.bfloat16)
+        own = lax.dynamic_slice_in_dim(gradient, core * rows, rows, 0).astype(jnp.float32)
+        new_moment[place] = MOMENTUM_BETA * moment + clip_factor * own
+    width = model_width // 2
+    small_own = lax.dynamic_slice_in_dim(small_sum, core * width, width, 1)
+    for place, gradient in ((0, small_own[0]), (2, small_own[1:4]), (4, small_own[4])):
+        new_moment[place] = MOMENTUM_BETA * moments[place] + clip_factor * gradient
+    return (
+        (block_out, input_grad, grad_norm)
+        + tuple(new_moment[place] for place in range(8))
+        + tuple(new_weight[place] for place in (1, 3, 5, 6, 7))
     )
 
 
@@ -306,8 +793,9 @@
         P(),
         P(),
     )
+    sizes = (mesh.shape["dp"], mesh.shape["seq"], mesh.shape["shard"])
     return jax.shard_map(
-        local,
+        local_fast if sizes == (4, 4, 2) else local,
         mesh=mesh,
         in_specs=placed,
         out_specs=(

time: 1530 us -> 892 us (0.58)
  waiting for transfers between devices: 946 us -> 118 us
  Pallas kernels: 0 us -> 234 us
  blocking collectives: 93.5 us -> 5.82 us
  other arithmetic: 168 us -> 229 us
  matrix products: 226 us -> 201 us
  starting transfers between devices: 7.14 us -> 28 us
    psum x1 -> x0, waiting for transfers between devices: 879 us -> none  [local(): lax.psum((shares[0], shares[1], shares[2], shares[3], shares[4], shares[5...]
    pallas_call x0 -> x1, Pallas kernels: none -> 234 us  [finish(): pl.pallas_call(functools.partial(finish_kernel, shapes), out_shape=[jax.S...]
    ppermute x0 -> x25, waiting for transfers between devices: none -> 115 us  [the longest x20 115 us: swap_first(): return lax.ppermute(block, 'dp', route)]
    psum x2 -> x0, blocking collectives: 85 us -> none  [the longest x1 82.1 us: local(): lax.psum((shares[0], shares[1], shares[2], shares[3], shares[4], shares[5...]
    reduce_scatter x5 -> x0, waiting for transfers between devices: 59.2 us -> none  [the longest x1 31.8 us: local(): lax.psum_scatter(down_grad, 'shard', scatter_dimension=0, tiled=True)]
    convert_element_type x17 -> x42, other arithmetic: 110 us -> 163 us  [the longest x5 65.1 us: local_fast(): base.astype(jnp.bfloat16)]
    add x3 -> x7, other arithmetic: 2.46 us -> 40.4 us  [the longest x4 37.8 us: local_fast(): new_moment[place] = MOMENTUM_BETA * moment + clip_factor * own]
    unnamed x108 -> x138, local copies, waits for them, and re-layouts: 62.6 us -> 31.4 us
  transfers between devices with their start and end apart: 19 -> 37, of which waited for: 5 -> 13; matrix products, arithmetic and copies ran while one was open for 21% -> 50% of each run, Pallas kernels for 0% -> 26%
where the time goes in v1:
time: 892 us; the launch traced here: 884 us
  Pallas kernels  234 us (26%)
  other arithmetic  229 us (26%)
  matrix products  201 us (23%)
  waiting for transfers between devices  118 us (13%)
  local copies, waits for them, and re-layouts  49.2 us (6%)
  starting transfers between devices  28 us (3%)
  between operations  19.4 us (2%)
    pallas_call x1, Pallas kernels, finish(): pl.pallas_call(functools.partial(finish_kernel, shapes), out_shape=[jax.S...  234 us
    ppermute x20, waiting for transfers between devices, swap_first(): return lax.ppermute(block, 'dp', route)  115 us
    dot_general x5, matrix products, back_dot(): lax.dot_general(left, right, (((1,), (1,)), ((), ())), preferred_element_...  79.9 us
    convert_element_type x5, other arithmetic, local_fast(): base.astype(jnp.bfloat16)  65.1 us
    dot_general x5, matrix products, rows_dot(): return jnp.dot(left, right, preferred_element_type=jnp.float32)  64.9 us
    dot_general x5, matrix products, outer_dot(): lax.dot_general(left, right, (((0,), (0,)), ((), ())), preferred_element_...  55.8 us
    convert_element_type x5, other arithmetic, local_fast(): new_weight[place] = (base.astype(jnp.float32) - rate_now * clip_factor *...  51.6 us
    add x4, other arithmetic, local_fast(): new_moment[place] = MOMENTUM_BETA * moment + clip_factor * own  37.8 us
  transfers between devices with their start and end apart: 37, of which 13 were waited for; matrix products, arithmetic and copies ran while one was open for 50% of the time, Pallas kernels for 26%

profile of v1, /device:TPU:0, one launch (start us, length us, event | category | flops | bytes accessed | tf_op | source)
XLA Modules:
  0.0 883.8 jit_solution(16609387983977640964)
XLA Ops:
  8.5 11.7 %subtract_convert_fusion.7 = (bf16[512,3072]{1,0:T(8,128)(2,1)}, bf16[512,3072]{1,0:T(8,128)(2,1)}) fusion(f32[512,3072]{1,0:T(8,128)} %param.33, f32[512,3072]{1,0:T(8,128)} %param.25, f32[]{:T(128)S(6)} %mul.736, f32[]{:T(128)S(6)} %sub.40), kind=kLoop, calls=%fused_computation.26 | loop fusion | flops 7864320 | bytes 18874376 | tf_op jit(solution)/shard_map/convert_element_type | solution.py:542
  26.1 16.9 %subtract_convert_fusion.5 = (bf16[512,4608]{1,0:T(8,128)(2,1)}, bf16[512,4608]{1,0:T(8,128)(2,1)}) fusion(f32[512,4608]{1,0:T(8,128)} %param.38, f32[512,4608]{1,0:T(8,128)} %param.30, f32[]{:T(128)S(6)} %mul.736, f32[]{:T(128)S(6)} %sub.40), kind=kLoop, calls=%fused_computation.12 | loop fusion | flops 11796480 | bytes 28311560 | tf_op jit(solution)/shard_map/convert_element_type | solution.py:542
  43.0 15.0 %subtract_convert_fusion.6 = (bf16[512,4608]{1,0:T(8,128)(2,1)}, bf16[512,4608]{1,0:T(8,128)(2,1)}) fusion(f32[512,4608]{1,0:T(8,128)} %param.37, f32[512,4608]{1,0:T(8,128)} %param.29, f32[]{:T(128)S(6)} %mul.736, f32[]{:T(128)S(6)} %sub.40), kind=kLoop, calls=%fused_computation.13 | loop fusion | flops 11796480 | bytes 28311560 | tf_op jit(solution)/shard_map/convert_element_type | solution.py:542
  58.1 17.3 %subtract_convert_fusion.4 = (bf16[2304,1024]{1,0:T(8,128)(2,1)}, bf16[2304,1024]{1,0:T(8,128)(2,1)}) fusion(f32[2304,1024]{1,0:T(8,128)} %param.39, f32[2304,1024]{1,0:T(8,128)} %param.31, f32[]{:T(128)S(6)} %mul.736, f32[]{:T(128)S(6)} %sub.40), kind=kLoop, calls=%fused_computation.11 | loop fusion | flops 11796480 | bytes 28311560 | tf_op jit(solution)/shard_map/convert_element_type | solution.py:542
  86.6 9.5 %fusion.33 = f32[1024,3072]{1,0:T(8,128)S(1)} fusion(bf16[1024,3072]{1,0:T(8,128)(2,1)} %all-gather.13.cloned.1.call-done, bf16[1,1024,1024]{1,2,0:T(8,128)(2,1)S(1)} %copy.47, f32[1024]{0:T(1024)S(1)} %bitcast.118, f32[1024]{0:T(1024)S(1)} %add_rsqrt_fusion.1), kind=kOutput, calls=%fused_computation.110 | convolution fusion | flops 6446645248 | bytes 20979712 | tf_op jit(solution)/shard_map/dot_general | solution.py:27
  115.3 14.0 %multiply_convert_fusion.7 = (bf16[1024,1024]{1,0:T(8,128)(2,1)}, f32[1024,1024]{1,0:T(8,128)}) fusion(f32[1024,3072]{1,0:T(8,128)} %copy-done, f32[1,1024,1024]{2,1,0:T(8,128)} %copy-done.1, f32[1,2,1024]{2,1,0:T(2,128)S(1)} %collective-permute-done, f32[1024]{0:T(1024)S(1)} %bitcast.105, f32[1024]{0:T(1024)S(1)} %bitcast.116, f32[1024]{0:T(1024)S(1)} %bitcast.107, ...), kind=kLoop, calls=%fused_computation.72 | loop fusion | flops 12582912 | bytes 23097344 | tf_op jit(solution)/shard_map/convert_element_type | solution.py:471
  137.9 17.1 %fusion.48 = f32[1024,4608]{1,0:T(8,128)} fusion(bf16[1024,1024]{0,1:T(8,128)(2,1)S(1)} %multiply_convert_fusion.6, bf16[1024,4608]{1,0:T(8,128)(2,1)} %all-gather.19.cloned.1.call-done), kind=kOutput, calls=%fused_computation.172 | convolution fusion | flops 9663676416 | bytes 30408704 | tf_op jit(solution)/shard_map/dot_general | solution.py:27
  155.0 17.6 %fusion.47 = f32[1024,4608]{1,0:T(8,128)} fusion(bf16[1024,1024]{0,1:T(8,128)(2,1)} %copy-done.22, bf16[1024,4608]{1,0:T(8,128)(2,1)} %all-gather.17.cloned.1.call-done), kind=kOutput, calls=%fused_computation.171 | convolution fusion | flops 9663676416 | bytes 30408704 | tf_op jit(solution)/shard_map/dot_general | solution.py:27
  172.6 33.5 %multiply_convert_fusion = (bf16[1024,4608]{1,0:T(8,128)(2,1)}, bf16[1024,4608]{1,0:T(8,128)(2,1)}, bf16[1024,4608]{1,0:T(8,128)(2,1)}) fusion(f32[1024,4608]{1,0:T(8,128)} %fusion.47, f32[1024,4608]{1,0:T(8,128)} %fusion.48, bf16[4608,1024]{1,0:T(8,128)(2,1)} %all-gather.21.cloned.1.call-done, bf16[1,1024,1024]{2,1,0:T(8,128)(2,1)S(1)} %copy-done.21), kind=kOutput, calls=%fused_computation.3 | convolution fusion | flops 9739173888 | bytes 77594624 | tf_op jit(solution)/shard_map/dot_general | solution.py:37
  206.1 17.3 %convolution_convert_fusion = bf16[1024,4608]{1,0:T(8,128)(2,1)} fusion(bf16[1024,1024]{0,1:T(8,128)(2,1)S(1)} %copy-done.23, bf16[1024,4608]{1,0:T(8,128)(2,1)} %get-tuple-element.74), kind=kOutput, calls=%fused_computation.8 | convolution fusion | flops 9668395008 | bytes 20971520 | tf_op jit(solution)/shard_map/dot_general | solution.py:31
  223.4 12.1 %convolution_convert_fusion.1 = bf16[1024,4608]{1,0:T(8,128)(2,1)} fusion(bf16[1024,1024]{0,1:T(8,128)(2,1)S(1)} %copy-done.23, bf16[1024,4608]{1,0:T(8,128)(2,1)S(1)} %copy-done.54), kind=kOutput, calls=%fused_computation.9 | convolution fusion | flops 9668395008 | bytes 20971520 | tf_op jit(solution)/shard_map/dot_general | solution.py:31
  235.5 14.2 %fusion.49 = f32[1024,1024]{0,1:T(8,128)S(1)} fusion(bf16[1024,4608]{1,0:T(8,128)(2,1)} %get-tuple-element.75, bf16[1024,4608]{1,0:T(8,128)(2,1)} %all-gather.17.cloned.1.call-done), kind=kOutput, calls=%fused_computation.173 | convolution fusion | flops 9663676416 | bytes 23068672 | tf_op jit(solution)/shard_map/dot_general | solution.py:37
  249.8 16.1 %multiply_reduce_fusion = (f32[1024]{0:T(1024)S(1)}, f32[1024]{0:T(1024)S(1)}, f32[1024,1024]{0,1:T(8,128)S(1)}) fusion(f32[1024,1024]{0,1:T(8,128)S(1)} %copy-done.8, f32[1024]{0:T(1024)S(1)} %copy-done.31, f32[1024]{0:T(1024)S(1)} %bitcast.110, f32[1024,1024]{0,1:T(8,128)S(1)} %fusion.49, bf16[1024,4608]{1,0:T(8,128)(2,1)} %get-tuple-element.74, ...), kind=kOutput, calls=%fused_computation.60 | convolution fusion | flops 9671014400 | bytes 31473664 | tf_op jit(solution)/shard_map/dot_general | solution.py:37
  277.9 6.7 multiply_reduce_fusion.2
  286.7 13.9 %convolution_convert_fusion.2 = bf16[4608,1024]{1,0:T(8,128)(2,1)S(1)} fusion(bf16[1024,4608]{1,0:T(8,128)(2,1)} %get-tuple-element.76, bf16[1,1024,1024]{2,1,0:T(8,128)(2,1)} %param.23), kind=kOutput, calls=%fused_computation.10 | convolution fusion | flops 9668395008 | bytes 20971520 | tf_op jit(solution)/shard_map/dot_general | solution.py:31
  314.8 15.9 %fusion.24 = bf16[1,1024,1024]{1,2,0:T(8,128)(2,1)S(1)} fusion(f32[1024,1024]{0,1:T(8,128)} %copy-done.7, bf16[1024,4608]{1,0:T(8,128)(2,1)} %get-tuple-element.76, bf16[4608,1024]{1,0:T(8,128)(2,1)} %all-gather.21.cloned.1.call-done), kind=kOutput, calls=%fused_computation.83 | convolution fusion | flops 9665773568 | bytes 25165824 | tf_op jit(solution)/shard_map/dot_general | solution.py:27
  333.3 10.8 %multiply_convert_fusion.5 = (bf16[1024,1024]{1,0:T(8,128)(2,1)}, f32[1024,1024]{1,0:T(8,128)S(1)}) fusion(f32[1024,3072]{1,0:T(8,128)} %copy-done, f32[1,2,1024]{2,1,0:T(2,128)S(1)} %collective-permute-done.1, f32[1,1024,1024]{2,1,0:T(8,128)} %bitcast.98, f32[1024]{0:T(1024)S(1)} %bitcast.126, f32[1024]{0:T(1024)S(1)} %bitcast.117, f32[1024]{0:T(1024)S(1)} %bitcast.125, ...), kind=kLoop, calls=%fused_computation.66 | loop fusion | flops 11534336 | bytes 18903040 | tf_op jit(solution)/shard_map/convert.5
  347.6 8.8 convolution_convert_fusion.3
  358.5 11.6 %fusion.19 = (f32[1024]{0:T(1024)S(1)}, f32[1024]{0:T(1024)S(1)}, f32[1024,1024]{0,1:T(8,128)S(1)}) fusion(bf16[1,1024,1024]{1,2,0:T(8,128)(2,1)S(1)} %copy-done.4, f32[1024]{0:T(1024)S(1)} %copy-done.41, f32[1024]{0:T(1024)S(1)} %bitcast.120, bf16[1024,3072]{1,0:T(8,128)(2,1)} %all-gather.13.cloned.1.call-done, ...), kind=kOutput, calls=%fused_computation.53 | convolution fusion | flops 6468663296 | bytes 18890752 | tf_op jit(solution)/shard_map/dot_general | solution.py:37
  397.9 15.7 %collective-permute-done.8 = bf16[128,3072]{1,0:T(8,128)(2,1)S(1)} collective-permute-done((bf16[128,3072]{1,0:T(8,128)(2,1)S(1)}, bf16[128,3072]{1,0:T(8,128)(2,1)S(1)}, u32[]{:S(2)}, u32[]{:S(2)}) %collective-permute-start.8) | collective-permute-done | bytes 786464 | tf_op jit(solution)/shard_map/ppermute | solution.py:339
  416.5 6.4 collective-permute-done.9
  450.5 10.3 %collective-permute-done.23 = bf16[576,1024]{1,0:T(8,128)(2,1)} collective-permute-done((bf16[576,1024]{1,0:T(8,128)(2,1)}, bf16[576,1024]{1,0:T(8,128)(2,1)}, u32[]{:S(2)}, u32[]{:S(2)}) %collective-permute-start.23) | collective-permute-done | bytes 1179680 | tf_op jit(solution)/shard_map/ppermute | solution.py:339
  466.5 19.6 %collective-permute-done.18 = bf16[128,4608]{1,0:T(8,128)(2,1)} collective-permute-done((bf16[128,4608]{1,0:T(8,128)(2,1)}, bf16[128,4608]{1,0:T(8,128)(2,1)}, u32[]{:S(2)}, u32[]{:S(2)}) %collective-permute-start.18) | collective-permute-done | bytes 1179680 | tf_op jit(solution)/shard_map/ppermute | solution.py:339
  491.6 19.7 %collective-permute-done.13 = bf16[128,4608]{1,0:T(8,128)(2,1)S(1)} collective-permute-done((bf16[128,4608]{1,0:T(8,128)(2,1)S(1)}, bf16[128,4608]{1,0:T(8,128)(2,1)S(1)}, u32[]{:S(2)}, u32[]{:S(2)}) %collective-permute-start.13) | collective-permute-done | bytes 1179680 | tf_op jit(solution)/shard_map/ppermute | solution.py:339
  514.6 23.9 %collective-permute-done.19 = bf16[64,4608]{1,0:T(8,128)(2,1)S(1)} collective-permute-done((bf16[64,4608]{1,0:T(8,128)(2,1)S(1)}, bf16[64,4608]{1,0:T(8,128)(2,1)S(1)}, u32[]{:S(2)}, u32[]{:S(2)}) %collective-permute-start.19) | collective-permute-done | bytes 589856 | tf_op jit(solution)/shard_map/ppermute | solution.py:339
  548.6 233.5 %shard_map.324 = (bf16[1024,1024]{1,0:T(8,128)(2,1)}, bf16[1024,3072]{1,0:T(8,128)(2,1)}, bf16[1024,4608]{1,0:T(8,128)(2,1)}, bf16[1024,4608]{1,0:T(8,128)(2,1)}...) custom-call(bf16[128,1024]{1,0:T(8,128)(2,1)S(1)} %pad_maximum_fusion.9.refs_0_, ...), custom_call_target="tpu_custom_call" | custom-call | tf_op jit(solution)/shard_map/pallas_call | solution.py:309
  784.8 11.5 %multiply_add_fusion = f32[2304,1024]{1,0:T(8,128)} fusion(f32[2304,1024]{1,0:T(8,128)} %param.39, bf16[4608,1024]{1,0:T(8,128)(2,1)} %get-tuple-element.29, s32[]{:T(128)S(6)} %select_n.126, f32[]{:T(128)S(6)} %div.40), kind=kLoop, calls=%fused_computation.14 | loop fusion | flops 9437184 | bytes 23592968 | tf_op jit(solution)/shard_map/add | solution.py:547
  805.0 13.2 %subtract_convert_fusion = bf16[4608,1024]{1,0:T(8,128)(2,1)} fusion(bf16[4608,1024]{1,0:T(8,128)(2,1)} %get-tuple-element.29, bf16[4608,1024]{1,0:T(8,128)(2,1)} %all-gather.31.cloned.1.call-done, f32[]{:T(128)S(6)} %mul.739), kind=kLoop, calls=%fused_computation | loop fusion | flops 23592960 | bytes 28311556 | tf_op jit(solution)/shard_map/convert_element_type | solution.py:545
  823.4 12.1 %subtract_convert_fusion.1 = bf16[1024,4608]{1,0:T(8,128)(2,1)} fusion(bf16[1024,4608]{1,0:T(8,128)(2,1)} %get-tuple-element.28, bf16[1024,4608]{1,0:T(8,128)(2,1)} %all-gather.29.cloned.1.call-done, f32[]{:T(128)S(6)} %mul.739), kind=kLoop, calls=%fused_computation.1 | loop fusion | flops 23592960 | bytes 28311556 | tf_op jit(solution)/shard_map/convert_element_type | solution.py:545
  835.5 12.1 %subtract_convert_fusion.2 = bf16[1024,4608]{1,0:T(8,128)(2,1)} fusion(bf16[1024,4608]{1,0:T(8,128)(2,1)} %get-tuple-element.27, bf16[1024,4608]{1,0:T(8,128)(2,1)} %all-gather.27.cloned.1.call-done, f32[]{:T(128)S(6)} %mul.739), kind=kLoop, calls=%fused_computation.2 | loop fusion | flops 23592960 | bytes 28311556 | tf_op jit(solution)/shard_map/convert_element_type | solution.py:545
  847.7 17.8 %multiply_add_fusion.1 = (f32[512,4608]{1,0:T(8,128)}, f32[512,4608]{1,0:T(8,128)}) fusion(f32[512,4608]{1,0:T(8,128)} %param.38, bf16[1024,4608]{1,0:T(8,128)(2,1)} %get-tuple-element.28, s32[]{:T(128)S(6)} %select_n.55, f32[]{:T(128)S(6)} %div.40, bf16[1024,4608]{1,0:T(8,128)(2,1)} %get-tuple-element.27, f32[512,4608]{1,0:T(8,128)} %param.37), kind=kLoop, calls=%fused_computation.15 | loop fusion | flops 18874368 | bytes 47185928 | tf_op jit(solution)/shard_map/add | solution.py:547
  865.4 10.2 %subtract_convert_fusion.3 = bf16[1024,3072]{1,0:T(8,128)(2,1)} fusion(bf16[1024,3072]{1,0:T(8,128)(2,1)} %get-tuple-element.25, bf16[1024,3072]{1,0:T(8,128)(2,1)} %all-gather.23.cloned.1.call-done, f32[]{:T(128)S(6)} %mul.739), kind=kLoop, calls=%fused_computation.7 | loop fusion | flops 15728640 | bytes 18874372 | tf_op jit(solution)/shard_map/convert_element_type | solution.py:545
  (318 shorter events, 178.4 us)
Async XLA Ops:
  7.2 79.4 %all-gather.13.cloned.1.call-start = ((), (), s32[]{:S(2)}) async-start(), calls=%async_computation | async-start | bytes 9437184 | tf_op jit(solution)/shard_map/all_gather | solution.py:411
  20.2 109.2 %all-gather.15.cloned.1.call-start = ((), (), s32[]{:S(2)}) async-start(), calls=%async_computation.1 | async-start | bytes 3145728 | tf_op jit(solution)/shard_map/all_gather | solution.py:413
  26.0 110.6 %all-gather.19.cloned.1.call-start = ((), (), s32[]{:S(2)}) async-start(), calls=%async_computation.3 | async-start | bytes 14155776 | tf_op jit(solution)/shard_map/all_gather | solution.py:416
  43.0 112.0 %all-gather.17.cloned.1.call-start = ((), (), s32[]{:S(2)}) async-start(), calls=%async_computation.2 | async-start | bytes 14155776 | tf_op jit(solution)/shard_map/all_gather | solution.py:415
  58.0 114.6 %all-gather.21.cloned.1.call-start = ((), (), s32[]{:S(2)}) async-start(), calls=%async_computation.4 | async-start | bytes 14155776 | tf_op jit(solution)/shard_map/all_gather | solution.py:417
  75.4 729.5 %all-gather.31.cloned.1.call-start = ((), (), s32[]{:S(2)}) async-start(), calls=%async_computation.9 | async-start | bytes 14155776 | tf_op jit(solution)/shard_map/all_gather | solution.py:542
  76.0 742.2 %all-gather.25.cloned.1.call-start = ((), (), s32[]{:S(2)}) async-start(), calls=%async_computation.6 | async-start | bytes 3145728 | tf_op jit(solution)/shard_map/all_gather | solution.py:542
  76.8 746.6 %all-gather.29.cloned.1.call-start = ((), (), s32[]{:S(2)}) async-start(), calls=%async_computation.8 | async-start | bytes 14155776 | tf_op jit(solution)/shard_map/all_gather | solution.py:542
  77.5 758.0 %all-gather.27.cloned.1.call-start = ((), (), s32[]{:S(2)}) async-start(), calls=%async_computation.7 | async-start | bytes 14155776 | tf_op jit(solution)/shard_map/all_gather | solution.py:542
  78.3 787.2 %all-gather.23.cloned.1.call-start = ((), (), s32[]{:S(2)}) async-start(), calls=%async_computation.5 | async-start | bytes 9437184 | tf_op jit(solution)/shard_map/all_gather | solution.py:542
  103.8 11.5 %collective-permute-start = (f32[1,2,1024]{2,1,0:T(2,128)S(1)}, f32[1,2,1024]{2,1,0:T(2,128)S(1)}, u32[]{:S(2)}, u32[]{:S(2)}) collective-permute-start(f32[1,2,1024]{2,1,0:T(2,128)S(1)} %slice.108), channel_id=1, source_target_pairs={{0,2},{2,4},{4,6},{1,3},{3,5},{5,7},{8,10},{10,12},{12,14},{9,11},... | collective-permute-start | bytes 24584 | tf_op jit(solution)/shard_map/ppermute | solution.py:23
  285.4 47.9 %collective-permute-start.1 = (f32[1,2,1024]{2,1,0:T(2,128)S(1)}, f32[1,2,1024]{2,1,0:T(2,128)S(1)}, u32[]{:S(2)}, u32[]{:S(2)}) collective-permute-start(f32[1,2,1024]{2,1,0:T(2,128)S(1)} %slice.112), channel_id=1, source_target_pairs={{2,0},{4,2},{6,4},{3,1},{5,3},{7,5},{10,8},{12,10},{14,12},{11,9},... | collective-permute-start | bytes 24584 | tf_op jit(solution)/shard_map/ppermute | solution.py:23
  307.2 116.4 %collective-permute-start.22 = (bf16[2304,1024]{1,0:T(8,128)(2,1)}, bf16[2304,1024]{1,0:T(8,128)(2,1)}, u32[]{:S(2)}, u32[]{:S(2)}) collective-permute-start(bf16[2304,1024]{1,0:T(8,128)(2,1)} %constant_dynamic-slice_fusion.5), channel_id=1, source_target_pairs={{0,1},{1,0},{2,3},{3,2},{4,5},{5,4},{6,7},{7,6},{8,9},{9,8},{10,11... | collective-permute-start | bytes 14155784 | tf_op jit(solution)/shard_map/ppermute | solution.py:357
  310.0 124.7 %collective-permute-start.17 = (bf16[512,4608]{1,0:T(8,128)(2,1)}, bf16[512,4608]{1,0:T(8,128)(2,1)}, u32[]{:S(2)}, u32[]{:S(2)}) collective-permute-start(bf16[512,4608]{1,0:T(8,128)(2,1)} %constant_dynamic-slice_fusion.10), channel_id=1, source_target_pairs={{0,1},{1,0},{2,3},{3,2},{4,5},{5,4},{6,7},{7,6},{8,9},{9,8},{10,11... | collective-permute-start | bytes 14155784 | tf_op jit(solution)/shard_map/ppermute | solution.py:357
  314.1 130.1 %collective-permute-start.12 = (bf16[512,4608]{1,0:T(8,128)(2,1)}, bf16[512,4608]{1,0:T(8,128)(2,1)}, u32[]{:S(2)}, u32[]{:S(2)}) collective-permute-start(bf16[512,4608]{1,0:T(8,128)(2,1)} %constant_dynamic-slice_fusion.15), channel_id=1, source_target_pairs={{0,1},{1,0},{2,3},{3,2},{4,5},{5,4},{6,7},{7,6},{8,9},{9,8},{10,11... | collective-permute-start | bytes 14155784 | tf_op jit(solution)/shard_map/ppermute | solution.py:357
  314.2 55.9 %collective-permute-start.2 = (bf16[512,1024]{1,0:T(8,128)(2,1)S(1)}, bf16[512,1024]{1,0:T(8,128)(2,1)}, u32[]{:S(2)}, u32[]{:S(2)}) collective-permute-start(bf16[512,1024]{1,0:T(8,128)(2,1)S(1)} %constant_dynamic-slice_fusion.25), channel_id=1, source_target_pairs={{0,1},{1,0},{2,3},{3,2},{4,5},{5,4},{6,7},{7,6},{8,9},{9,8},{10,11... | collective-permute-start | bytes 3145736 | tf_op jit(solution)/shard_map/ppermute | solution.py:357
  358.4 31.9 %collective-permute-start.7 = (bf16[512,3072]{1,0:T(8,128)(2,1)}, bf16[512,3072]{1,0:T(8,128)(2,1)}, u32[]{:S(2)}, u32[]{:S(2)}) collective-permute-start(bf16[512,3072]{1,0:T(8,128)(2,1)} %constant_dynamic-slice_fusion.20), channel_id=1, source_target_pairs={{0,1},{1,0},{2,3},{3,2},{4,5},{5,4},{6,7},{7,6},{8,9},{9,8},{10,11... | collective-permute-start | bytes 9437192 | tf_op jit(solution)/shard_map/ppermute | solution.py:357
  396.0 17.6 %collective-permute-start.8 = (bf16[128,3072]{1,0:T(8,128)(2,1)S(1)}, bf16[128,3072]{1,0:T(8,128)(2,1)S(1)}, u32[]{:S(2)}, u32[]{:S(2)}) collective-permute-start(bf16[128,3072]{1,0:T(8,128)(2,1)S(1)} %constant_dynamic-slice_fusion.19), channel_id=1, source_target_pairs={{0,8},{8,0},{16,24},{24,16},{1,9},{9,1},{17,25},{25,17},{2,10},{10... | collective-permute-start | bytes 2359304 | tf_op jit(solution)/shard_map/ppermute | solution.py:339
  397.0 18.4 %collective-permute-start.10 = (bf16[128,3072]{1,0:T(8,128)(2,1)S(1)}, bf16[128,3072]{1,0:T(8,128)(2,1)S(1)}, u32[]{:S(2)}, u32[]{:S(2)}) collective-permute-start(bf16[128,3072]{1,0:T(8,128)(2,1)S(1)} %constant_dynamic-slice_fusion.17), channel_id=1, source_target_pairs={{0,16},{16,0},{8,24},{24,8},{1,17},{17,1},{9,25},{25,9},{2,18},{18... | collective-permute-start | bytes 2359304 | tf_op jit(solution)/shard_map/ppermute | solution.py:339
  413.8 9.1 %collective-permute-start.9 = (bf16[64,3072]{1,0:T(8,128)(2,1)S(1)}, bf16[64,3072]{1,0:T(8,128)(2,1)S(1)}, u32[]{:S(2)}, u32[]{:S(2)}) collective-permute-start(bf16[64,3072]{1,0:T(8,128)(2,1)S(1)} %constant_dynamic-slice_fusion.18), channel_id=1, source_target_pairs={{0,16},{16,0},{8,24},{24,8},{1,17},{17,1},{9,25},{25,9},{2,18},{18... | collective-permute-start | bytes 1179656 | tf_op jit(solution)/shard_map/ppermute | solution.py:339
  431.6 29.2 %collective-permute-start.23 = (bf16[576,1024]{1,0:T(8,128)(2,1)}, bf16[576,1024]{1,0:T(8,128)(2,1)}, u32[]{:S(2)}, u32[]{:S(2)}) collective-permute-start(bf16[576,1024]{1,0:T(8,128)(2,1)} %constant_dynamic-slice_fusion.4), channel_id=1, source_target_pairs={{0,8},{8,0},{16,24},{24,16},{1,9},{9,1},{17,25},{25,17},{2,10},{10... | collective-permute-start | bytes 3538952 | tf_op jit(solution)/shard_map/ppermute | solution.py:339
  433.6 30.6 %collective-permute-start.25 = (bf16[576,1024]{1,0:T(8,128)(2,1)}, bf16[576,1024]{1,0:T(8,128)(2,1)}, u32[]{:S(2)}, u32[]{:S(2)}) collective-permute-start(bf16[576,1024]{1,0:T(8,128)(2,1)} %constant_dynamic-slice_fusion.2), channel_id=1, source_target_pairs={{0,16},{16,0},{8,24},{24,8},{1,17},{17,1},{9,25},{25,9},{2,18},{18... | collective-permute-start | bytes 3538952 | tf_op jit(solution)/shard_map/ppermute | solution.py:339
  441.0 45.1 %collective-permute-start.18 = (bf16[128,4608]{1,0:T(8,128)(2,1)}, bf16[128,4608]{1,0:T(8,128)(2,1)}, u32[]{:S(2)}, u32[]{:S(2)}) collective-permute-start(bf16[128,4608]{1,0:T(8,128)(2,1)} %constant_dynamic-slice_fusion.9), channel_id=1, source_target_pairs={{0,8},{8,0},{16,24},{24,16},{1,9},{9,1},{17,25},{25,17},{2,10},{10... | collective-permute-start | bytes 3538952 | tf_op jit(solution)/shard_map/ppermute | solution.py:339
  443.7 44.9 %collective-permute-start.20 = (bf16[128,4608]{1,0:T(8,128)(2,1)}, bf16[128,4608]{1,0:T(8,128)(2,1)}, u32[]{:S(2)}, u32[]{:S(2)}) collective-permute-start(bf16[128,4608]{1,0:T(8,128)(2,1)} %constant_dynamic-slice_fusion.7), channel_id=1, source_target_pairs={{0,16},{16,0},{8,24},{24,8},{1,17},{17,1},{9,25},{25,9},{2,18},{18... | collective-permute-start | bytes 3538952 | tf_op jit(solution)/shard_map/ppermute | solution.py:339
  449.5 61.8 %collective-permute-start.13 = (bf16[128,4608]{1,0:T(8,128)(2,1)S(1)}, bf16[128,4608]{1,0:T(8,128)(2,1)S(1)}, u32[]{:S(2)}, u32[]{:S(2)}) collective-permute-start(bf16[128,4608]{1,0:T(8,128)(2,1)S(1)} %constant_dynamic-slice_fusion.14), channel_id=1, source_target_pairs={{0,8},{8,0},{16,24},{24,16},{1,9},{9,1},{17,25},{25,17},{2,10},{10... | collective-permute-start | bytes 3538952 | tf_op jit(solution)/shard_map/ppermute | solution.py:339
  460.8 52.4 %collective-permute-start.15 = (bf16[128,4608]{1,0:T(8,128)(2,1)S(1)}, bf16[128,4608]{1,0:T(8,128)(2,1)S(1)}, u32[]{:S(2)}, u32[]{:S(2)}) collective-permute-start(bf16[128,4608]{1,0:T(8,128)(2,1)S(1)} %constant_dynamic-slice_fusion.12), channel_id=1, source_target_pairs={{0,16},{16,0},{8,24},{24,8},{1,17},{17,1},{9,25},{25,9},{2,18},{18... | collective-permute-start | bytes 3538952 | tf_op jit(solution)/shard_map/ppermute | solution.py:339
  464.2 75.8 %collective-permute-start.24 = (bf16[288,1024]{1,0:T(8,128)(2,1)S(1)}, bf16[288,1024]{1,0:T(8,128)(2,1)S(1)}, u32[]{:S(2)}, u32[]{:S(2)}) collective-permute-start(bf16[288,1024]{1,0:T(8,128)(2,1)S(1)} %constant_dynamic-slice_fusion.3), channel_id=1, source_target_pairs={{0,16},{16,0},{8,24},{24,8},{1,17},{17,1},{9,25},{25,9},{2,18},{18... | collective-permute-start | bytes 1769480 | tf_op jit(solution)/shard_map/ppermute | solution.py:339
  486.1 54.1 %collective-permute-start.26 = (bf16[288,1024]{1,0:T(8,128)(2,1)S(1)}, bf16[288,1024]{1,0:T(8,128)(2,1)S(1)}, u32[]{:S(2)}, u32[]{:S(2)}) collective-permute-start(bf16[288,1024]{1,0:T(8,128)(2,1)S(1)} %constant_dynamic-slice_fusion.1), channel_id=1, source_target_pairs={{0,8},{8,0},{16,24},{24,16},{1,9},{9,1},{17,25},{25,17},{2,10},{10... | collective-permute-start | bytes 1769480 | tf_op jit(solution)/shard_map/ppermute | solution.py:339
  488.6 49.9 %collective-permute-start.19 = (bf16[64,4608]{1,0:T(8,128)(2,1)S(1)}, bf16[64,4608]{1,0:T(8,128)(2,1)S(1)}, u32[]{:S(2)}, u32[]{:S(2)}) collective-permute-start(bf16[64,4608]{1,0:T(8,128)(2,1)S(1)} %constant_dynamic-slice_fusion.8), channel_id=1, source_target_pairs={{0,16},{16,0},{8,24},{24,8},{1,17},{17,1},{9,25},{25,9},{2,18},{18... | collective-permute-start | bytes 1769480 | tf_op jit(solution)/shard_map/ppermute | solution.py:339
  511.3 28.5 %collective-permute-start.21 = (bf16[64,4608]{1,0:T(8,128)(2,1)S(1)}, bf16[64,4608]{1,0:T(8,128)(2,1)S(1)}, u32[]{:S(2)}, u32[]{:S(2)}) collective-permute-start(bf16[64,4608]{1,0:T(8,128)(2,1)S(1)} %constant_dynamic-slice_fusion.6), channel_id=1, source_target_pairs={{0,8},{8,0},{16,24},{24,16},{1,9},{9,1},{17,25},{25,17},{2,10},{10... | collective-permute-start | bytes 1769480 | tf_op jit(solution)/shard_map/ppermute | solution.py:339
  513.3 33.6 %collective-permute-start.14 = (bf16[64,4608]{1,0:T(8,128)(2,1)S(1)}, bf16[64,4608]{1,0:T(8,128)(2,1)S(1)}, u32[]{:S(2)}, u32[]{:S(2)}) collective-permute-start(bf16[64,4608]{1,0:T(8,128)(2,1)S(1)} %constant_dynamic-slice_fusion.13), channel_id=1, source_target_pairs={{0,16},{16,0},{8,24},{24,8},{1,17},{17,1},{9,25},{25,9},{2,18},{18... | collective-permute-start | bytes 1769480 | tf_op jit(solution)/shard_map/ppermute | solution.py:339
  538.5 9.9 %collective-permute-start.16 = (bf16[64,4608]{1,0:T(8,128)(2,1)S(1)}, bf16[64,4608]{1,0:T(8,128)(2,1)S(1)}, u32[]{:S(2)}, u32[]{:S(2)}) collective-permute-start(bf16[64,4608]{1,0:T(8,128)(2,1)S(1)} %constant_dynamic-slice_fusion.11), channel_id=1, source_target_pairs={{0,8},{8,0},{16,24},{24,16},{1,9},{9,1},{17,25},{25,17},{2,10},{10... | collective-permute-start | bytes 1769480 | tf_op jit(solution)/shard_map/ppermute | solution.py:339
  (71 other events, 744.4 us)
Sparse Core Ops, SparseCore 0:
  20.3 19.4 all-gather.12
  42.0 11.7 all-gather.14
  55.9 23.0 all-gather.18
  80.9 23.0 all-gather.16
  105.9 23.0 all-gather.20
  130.4 23.0 all-gather.30
  155.0 11.7 all-gather.24
  168.3 23.0 all-gather.28
  193.5 23.0 all-gather.26
  217.9 17.9 all-gather.22

commit v2 on v1

--- a/solution.py
+++ b/solution.py
@@ -16,6 +16,8 @@
 WEIGHT_DECAY = 0.1
 CLIP_RATIO = 0.25
 
+FEED_PARTS = 3
+
 
 def from_behind(block, axis, distance):
     devices = range(lax.axis_size(axis))
@@ -75,20 +77,45 @@
 MESH = pl.DeviceIdType.MESH
 ANY = pl.BlockSpec(memory_space=pl.ANY)
 INTO_VMEM = pl.BlockSpec(memory_space=pltpu.VMEM)
-
-
-def finish_kernel(shapes, *refs):
-    count = len(shapes)
-    pieces = refs[:count]
-    small = refs[count]
-    wholes = refs[count + 1 : 2 * count + 1]
-    small_out, square_out = refs[2 * count + 1 : 2 * count + 3]
-    rest = refs[2 * count + 3 :]
-    from_end = rest[:count]
-    from_mid = rest[count : 2 * count]
+ROWS_DOT = (((1,), (0,)), ((), ()))
+BACK_DOT = (((1,), (1,)), ((), ()))
+KEEP_SLOTS, GOT_SLOTS, GIVE_SLOTS = 5, 3, 2
+
+
+def kernel_dot(left, right, dims=ROWS_DOT):
+    return lax.dot_general(left, right, dims, preferred_element_type=jnp.float32)
+
+
+def finish_kernel(chunks, parts, wholes_count, unused, *refs):
+    count = len(chunks)
+    out_keep, out_give, in_keep, in_give = refs[:4]
+    n2t, et, gate_back, up_back, act, small = refs[4:10]
+    refs = refs[10 + unused :]
+    whole_refs = refs[:wholes_count]
+    small_out, square_out = refs[wholes_count : wholes_count + 2]
+    rest = refs[wholes_count + 2 :]
+    plain = sum(1 for chunk in chunks if chunk[0] != "feed")
+    plain_keep, plain_got = rest[:plain], rest[plain : 2 * plain]
+    rest = rest[2 * plain :]
+    keep_ring, got_ring, give_ring, tiles = rest[:4]
+    rest = rest[4:]
+    first_in = rest[:count]
+    pieces = rest[count : 2 * count]
     done = rest[2 * count : 3 * count]
-    small_in, square_in = rest[3 * count : 3 * count + 2]
-    send, recv, small_send, small_recv, square_send, square_recv, own_sem = rest[3 * count + 2 :]
+    from_mid = rest[3 * count : 4 * count]
+    small_in, square_in = rest[4 * count : 4 * count + 2]
+    (
+        send,
+        recv,
+        small_send,
+        small_recv,
+        square_send,
+        square_recv,
+        own_sem,
+        load_sem,
+        tile_sem,
+        credit,
+    ) = rest[4 * count + 2 :]
 
     group = lax.axis_index("dp")
     place = lax.axis_index("seq")
@@ -110,6 +137,21 @@
         pl.semaphore_signal(barrier, inc=1, device_id=device, device_id_type=MESH)
     pl.semaphore_wait(barrier, 5)
 
+    def unit_of(c):
+        return chunks[c][2] // 8
+
+    def feed_index(c):
+        return c - plain
+
+    def is_feed(c):
+        return chunks[c][0] == "feed"
+
+    def keep_of(c):
+        return keep_ring.at[feed_index(c) % KEEP_SLOTS] if is_feed(c) else plain_keep[c]
+
+    def got_of(c):
+        return got_ring.at[feed_index(c) % GOT_SLOTS] if is_feed(c) else plain_got[c]
+
     def remote(source, target, c, k, device):
         return pltpu.make_async_remote_copy(
             src_ref=source,
@@ -120,30 +162,43 @@
             device_id_type=MESH,
         )
 
+    def aligned(start, size):
+        return pl.ds(pl.multiple_of(start, 16), size)
+
     def rows_of(c, h, first, second, owner):
-        unit = shapes[c][0] // 2
-        start = owner * (8 * unit) + ((h * 2 + first) * 2 + second) * unit
-        return pl.ds(pl.multiple_of(start, 16), unit)
+        unit = unit_of(c)
+        _, _, _, _, base, stride = chunks[c][:6]
+        return aligned(base + owner * stride + ((h * 2 + first) * 2 + second) * unit, unit)
+
+    def local_rows(c, h, first, second=None):
+        unit = unit_of(c)
+        if second is None:
+            return aligned((h * 2 + first) * 2 * unit, 2 * unit)
+        return aligned(((h * 2 + first) * 2 + second) * unit, unit)
+
+    def whole_of(c):
+        return whole_refs[chunks[c][3 + 0]]
 
     def mine(c, h):
-        unit = shapes[c][0] // 2
+        unit = unit_of(c)
         return done[c].at[pl.ds(h * unit, unit)]
 
-    def add_rows(c, one, two, out, square=False):
+    def add_into(target, target_row, one, one_row, two, two_row, rows):
         def body(i, carry):
-            rows = pl.ds(pl.multiple_of(i * 16, 16), 16)
-            total = one[rows, :].astype(jnp.float32) + two[rows, :].astype(jnp.float32)
-            out[rows, :] = total.astype(jnp.bfloat16)
+            at = lambda start: aligned(start + i * 16, 16)
+            total = one[at(one_row), :].astype(jnp.float32) + two[at(two_row), :].astype(
+                jnp.float32
+            )
+            target[at(target_row), :] = total.astype(jnp.bfloat16)
             return carry
 
-        lax.fori_loop(0, shapes[c][0] // 16, body, 0)
+        lax.fori_loop(0, rows // 16, body, 0)
 
     def add_squares(c):
-        width = shapes[c][1]
+        width = chunks[c][7]
 
         def body(i, total):
-            rows = pl.ds(pl.multiple_of(i * 16, 16), 16)
-            block = done[c][rows, :].astype(jnp.float32)
+            block = done[c][aligned(i * 16, 16), :].astype(jnp.float32)
             block = block * block
             block = block[:8] + block[8:]
             for j in range(width // 128):
@@ -151,70 +206,153 @@
             return total
 
         square_out[...] += lax.fori_loop(
-            0, shapes[c][0] // 16, body, jnp.zeros((8, 128), jnp.float32)
+            0, 2 * unit_of(c) // 16, body, jnp.zeros((8, 128), jnp.float32)
         )
 
+    def over_core(c):
+        if is_feed(c):
+            return remote(give_ring.at[feed_index(c) % GIVE_SLOTS], got_of(c), c, 0, sibling)
+        name, start, rows = chunks[c][0], chunks[c][6], chunks[c][2]
+        source = out_give if name == "out" else in_give
+        return remote(source.at[pl.ds(start, rows)], got_of(c), c, 0, sibling)
+
+    def load_keep(c):
+        name, start, rows = chunks[c][0], chunks[c][6], chunks[c][2]
+        source = out_keep if name == "out" else in_keep
+        return pltpu.make_async_copy(source.at[pl.ds(start, rows)], plain_keep[c], load_sem.at[c])
+
+    def over_first(c, h):
+        unit = unit_of(c)
+        source = keep_of(c).at[local_rows(c, h, 1 - first_bit[h])]
+        return remote(source, first_in[c].at[pl.ds(h * 2 * unit, 2 * unit)], c, 1 + h, first_dev[h])
+
+    def over_second(c, h):
+        unit = unit_of(c)
+        source = keep_of(c).at[local_rows(c, h, first_bit[h], 1 - second_bit[h])]
+        return remote(source, pieces[c].at[pl.ds(h * unit, unit)], c, 3 + h, second_dev[h])
+
     def z_in(c):
-        return remote(pieces[c], from_end[c], c, 0, z_near)
+        return remote(pieces[c], done[c], c, 5, z_near)
 
     def z_mid(c):
-        return remote(done[c], from_mid[c], c, 1, z_far)
+        return remote(done[c], from_mid[c], c, 6, z_far)
 
     def z_out(c):
-        return remote(done[c], done[c], c, 2, z_near)
+        return remote(done[c], done[c], c, 7, z_near)
 
     def to_second(c, h):
         rows = rows_of(c, h, first_bit[h], second_bit[h], core)
-        return remote(mine(c, h), wholes[c].at[rows], c, 3 + h, second_dev[h])
+        return remote(mine(c, h), whole_of(c).at[rows], c, 8 + h, second_dev[h])
 
     def to_first(c, h):
         rows = rows_of(c, h, first_bit[h], second_bit[h], core)
-        return remote(mine(c, h), wholes[c].at[rows], c, 5 + h, first_dev[h])
+        return remote(mine(c, h), whole_of(c).at[rows], c, 10 + h, first_dev[h])
 
     def pass_first(c, h):
         rows = rows_of(c, h, first_bit[h], 1 - second_bit[h], core)
-        return remote(wholes[c].at[rows], wholes[c].at[rows], c, 7 + h, first_dev[h])
+        return remote(whole_of(c).at[rows], whole_of(c).at[rows], c, 12 + h, first_dev[h])
 
     def to_sibling(c, h, kind):
         first = first_bit[h] if kind < 2 else 1 - first_bit[h]
         second = second_bit[h] if kind % 2 == 0 else 1 - second_bit[h]
         rows = rows_of(c, h, first, second, core)
-        source = mine(c, h) if kind == 0 else wholes[c].at[rows]
-        return remote(source, wholes[c].at[rows], c, 9 + 2 * kind + h, sibling)
-
-    def keep(c, h):
+        source = mine(c, h) if kind == 0 else whole_of(c).at[rows]
+        return remote(source, whole_of(c).at[rows], c, 14 + 2 * kind + h, sibling)
+
+    def own_copy(c, h):
         rows = rows_of(c, h, first_bit[h], second_bit[h], core)
-        return pltpu.make_async_copy(mine(c, h), wholes[c].at[rows], own_sem.at[c, h])
-
-    def enter(c):
+        return pltpu.make_async_copy(mine(c, h), whole_of(c).at[rows], own_sem.at[c, h])
+
+    def load_tile(c, half):
+        part, kind = chunks[c][1]
+        cols = tiles.shape[2]
+        source = (gate_back, up_back, act)[kind]
+        return pltpu.make_async_copy(
+            source.at[:, pl.ds((half * parts + part) * cols, cols)], tiles.at[half], tile_sem.at[half]
+        )
+
+    def produce(c):
+        if not is_feed(c):
+            over_core(c).start()
+            load_keep(c).start()
+            return
+        index = feed_index(c)
+        kind = chunks[c][1][1]
+        keep, give = keep_of(c), give_ring.at[index % GIVE_SLOTS]
+        rows = n2t.shape[0] // 2
+        for half in range(2):
+            load_tile(c, half).wait()
+
+        @pl.loop(0, 2)
+        def _(r):
+            target = aligned(r * rows, rows)
+            for ref, side in ((keep, core), (give, 1 - core)):
+                if kind < 2:
+                    block = kernel_dot(n2t[aligned(side * rows, rows), :], tiles[r])
+                else:
+                    block = kernel_dot(et[target, :], tiles[side])
+                ref[target, :] = block.astype(jnp.bfloat16)
+
+        if c + 1 < count:
+            for half in range(2):
+                load_tile(c + 1, half).start()
+        if index >= GOT_SLOTS:
+            pl.semaphore_wait(credit, 1)
+        over_core(c).start()
+
+    def sum_core(c):
+        if not is_feed(c):
+            load_keep(c).wait()
+        over_core(c).wait()
+        add_into(keep_of(c), 0, keep_of(c), 0, got_of(c), 0, chunks[c][2])
+        if is_feed(c) and c + GOT_SLOTS < count:
+            pl.semaphore_signal(credit, inc=1, device_id=sibling, device_id_type=MESH)
+        for h in range(2):
+            over_first(c, h).start()
+
+    def sum_first(c):
+        unit = unit_of(c)
+        for h in range(2):
+            over_first(c, h).wait()
+            row = (h * 2 + first_bit[h]) * 2 * unit
+            add_into(keep_of(c), row, keep_of(c), row, first_in[c], h * 2 * unit, 2 * unit)
+            over_second(c, h).start()
+
+    def sum_second(c):
+        unit = unit_of(c)
+        for h in range(2):
+            over_second(c, h).wait()
+            row = ((h * 2 + first_bit[h]) * 2 + second_bit[h]) * unit
+            add_into(pieces[c], h * unit, pieces[c], h * unit, keep_of(c), row, unit)
+
         @pl.when(is_end)
         def _():
             z_in(c).start()
 
-    def middle_add(c):
+    def sum_end(c):
         @pl.when(is_mid)
         def _():
             z_in(c).wait_recv()
-            add_rows(c, pieces[c], from_end[c], done[c])
+            add_into(done[c], 0, pieces[c], 0, done[c], 0, 2 * unit_of(c))
             z_mid(c).start()
 
-    def middle_close(c):
+    def sum_middle(c):
         @pl.when(is_mid)
         def _():
             z_mid(c).wait()
-            add_rows(c, done[c], from_mid[c], done[c])
+            add_into(done[c], 0, done[c], 0, from_mid[c], 0, 2 * unit_of(c))
             z_out(c).start()
 
         @pl.when(is_end)
         def _():
+            z_in(c).wait_send()
             z_out(c).wait_recv()
 
-    def hand_out(c):
         for h in range(2):
             to_second(c, h).start()
             to_first(c, h).start()
             to_sibling(c, h, 0).start()
-            keep(c, h).start()
+            own_copy(c, h).start()
         add_squares(c)
 
     def forward(c):
@@ -231,10 +369,6 @@
             to_sibling(c, h, 3).start()
 
     def drain(c):
-        @pl.when(is_end)
-        def _():
-            z_in(c).wait_send()
-
         @pl.when(is_mid)
         def _():
             z_out(c).wait_send()
@@ -243,7 +377,7 @@
             to_second(c, h).wait_send()
             to_first(c, h).wait_send()
             pass_first(c, h).wait_send()
-            keep(c, h).wait()
+            own_copy(c, h).wait()
             for kind in range(4):
                 to_sibling(c, h, kind).wait()
 
@@ -271,96 +405,582 @@
 
     small_out[...] = small[...]
     square_out[...] = jnp.zeros_like(square_out)
-    enter(0)
+    for half in range(2):
+        load_tile(plain, half).start()
     small_copy(0).start()
-    for t in range(count + 3):
-        if t + 1 < count:
-            enter(t + 1)
+
+    def at(step, action):
+        if 0 <= step < count:
+            action(step)
+
+    squares_from = count + 3
+    for t in range(count + 7):
+        at(t, produce)
         if t < 5:
             small_copy(t).wait()
             small_out[...] += small_in[t]
             if t < 4:
                 small_copy(t + 1).start()
-        if t < count:
-            middle_add(t)
-        if 0 <= t - 1 < count:
-            middle_close(t - 1)
-            hand_out(t - 1)
-        if 0 <= t - 2 < count:
-            forward(t - 2)
-        if t >= count:
-            k = t - count
+        at(t - 1, sum_first)
+        at(t - 2, sum_second)
+        at(t - 3, sum_middle)
+        if squares_from <= t < squares_from + 4:
+            k = t - squares_from
             if k >= 1:
                 square_copy(k - 1).wait()
                 square_out[...] += square_in[k - 1]
-            square_copy(k).start()
-        if 0 <= t - 3 < count:
-            last_hop(t - 3)
-    square_copy(2).wait()
-    square_out[...] += square_in[2]
+            if k < 3:
+                square_copy(k).start()
+        at(t - 5, last_hop)
+        at(t, sum_core)
+        at(t - 2, sum_end)
+        at(t - 4, forward)
     for c in range(count):
         drain(c)
 
 
-def finish(pieces, small):
-    shapes = tuple(piece.shape for piece in pieces)
-    count = len(pieces)
+def finish(out_sides, in_sides, n2t, et, gate_back, up_back, act, parts, small, order):
+    width = n2t.shape[0]
+    half = width // 2
+    cols = gate_back.shape[1] // (2 * parts)
+    in_cols = in_sides[0].shape[1]
+    chunks = [("out", None, half, 0, 0, half, 0, width)]
+    chunks += [("in", None, half // 2, 1, t * half // 2, half, t * half // 2, in_cols) for t in range(2)]
+    for part in range(parts):
+        for kind in range(3):
+            first = (part * 3 + kind) * 2 * width
+            chunks.append(("feed", (part, kind), width, 2, first, width, 0, cols))
+    count, plain = len(chunks), 3
+    low = jnp.bfloat16
     semaphore = pltpu.SemaphoreType.DMA
+    wholes = [(width, width), (width, in_cols), (parts * 3 * 2 * width, cols)]
+    eighths = [(chunk[2] // 8, chunk[7]) for chunk in chunks]
+    plain_shapes = [(chunk[2], chunk[7]) for chunk in chunks[:plain]]
+    pair = [pltpu.VMEM((2 * rows, c), low) for rows, c in eighths]
     outs = pl.pallas_call(
-        functools.partial(finish_kernel, shapes),
-        out_shape=[jax.ShapeDtypeStruct((8 * r, c), jnp.bfloat16) for r, c in shapes]
+        functools.partial(finish_kernel, tuple(chunks), parts, len(wholes), len(order)),
+        out_shape=[jax.ShapeDtypeStruct(shape, low) for shape in wholes]
         + [
             jax.ShapeDtypeStruct((8, small.shape[1]), jnp.float32),
             jax.ShapeDtypeStruct((8, 128), jnp.float32),
         ],
-        in_specs=[INTO_VMEM] * (count + 1),
-        out_specs=[ANY] * count + [INTO_VMEM] * 2,
-        scratch_shapes=[pltpu.VMEM(shape, jnp.bfloat16) for shape in shapes] * 3
+        in_specs=[ANY] * 4 + [INTO_VMEM] * 2 + [ANY] * 3 + [INTO_VMEM] + [ANY] * len(order),
+        out_specs=[ANY] * len(wholes) + [INTO_VMEM] * 2,
+        scratch_shapes=[pltpu.VMEM(shape, low) for shape in plain_shapes] * 2
+        + [
+            pltpu.VMEM((KEEP_SLOTS, width, cols), low),
+            pltpu.VMEM((GOT_SLOTS, width, cols), low),
+            pltpu.VMEM((GIVE_SLOTS, width, cols), low),
+            pltpu.VMEM((2, act.shape[0], cols), low),
+        ]
+        + [pltpu.VMEM((4 * rows, c), low) for rows, c in eighths]
+        + pair * 3
         + [
             pltpu.VMEM((5, 8, small.shape[1]), jnp.float32),
             pltpu.VMEM((3, 8, 128), jnp.float32),
-            semaphore((count, 17)),
-            semaphore((count, 17)),
+            semaphore((count, 22)),
+            semaphore((count, 22)),
             semaphore((5,)),
             semaphore((5,)),
             semaphore((3,)),
             semaphore((3,)),
             semaphore((count, 2)),
+            semaphore((plain,)),
+            semaphore((2,)),
+            pltpu.SemaphoreType.REGULAR,
         ],
         compiler_params=pltpu.CompilerParams(
-            collective_id=0, has_side_effects=True, vmem_limit_bytes=48 * 1024 * 1024
+            collective_id=0, has_side_effects=True, vmem_limit_bytes=62 * 1024 * 1024
         ),
-    )(*pieces, small)
-    return outs[:count], outs[count], outs[count + 1]
-
-
-def swap_first(block, axis_bit):
-    route = ((0, 1), (1, 0), (2, 3), (3, 2)) if axis_bit == 0 else ((0, 2), (2, 0), (1, 3), (3, 1))
-    return lax.ppermute(block, "dp", route)
-
-
-def halve(block, bit, axis_bit):
-    rows = block.shape[0] // 2
-    give = lax.dynamic_slice_in_dim(block, (1 - bit) * rows, rows, 0)
-    keep = lax.dynamic_slice_in_dim(block, bit * rows, rows, 0)
-    got = swap_first(give, axis_bit)
-    return (keep.astype(jnp.float32) + got.astype(jnp.float32)).astype(jnp.bfloat16)
-
-
-def scatter_piece(gradient):
+    )(*out_sides, *in_sides, n2t, et, gate_back, up_back, act, small, *order)
+    return outs[: len(wholes)], outs[-2], outs[-1]
+
+
+def feed_kernel(step, n2, e, wg, wu, wd, out, back, act, gate_back, up_back):
+    @pl.when(pl.program_id(0) == 0)
+    def _():
+        out[...] = jnp.zeros_like(out)
+        back[...] = jnp.zeros_like(back)
+
+    @pl.loop(0, n2.shape[0] // step)
+    def _(t):
+        rows = pl.ds(pl.multiple_of(t * step, step), step)
+        gate = kernel_dot(n2[rows, :], wg[...])
+        up = kernel_dot(n2[rows, :], wu[...])
+        grad = kernel_dot(e[rows, :], wd[...], BACK_DOT)
+        sigmoid = 0.5 * jnp.tanh(0.5 * gate) + 0.5
+        silu = gate * sigmoid
+        low_act = (silu * up).astype(jnp.bfloat16)
+        low_up = (grad * silu).astype(jnp.bfloat16)
+        low_gate = (grad * up * (sigmoid + silu * (1.0 - sigmoid))).astype(jnp.bfloat16)
+        act[rows, :] = low_act
+        gate_back[rows, :] = low_gate
+        up_back[rows, :] = low_up
+        out[rows, :] += kernel_dot(low_act, wd[...])
+        back[rows, :] += kernel_dot(low_gate, wg[...], BACK_DOT) + kernel_dot(
+            low_up, wu[...], BACK_DOT
+        )
+
+
+def feed(n2, e, gate_matrix, up_matrix, down_matrix, tiles):
+    rows, width = n2.shape
+    cols = gate_matrix.shape[1] // tiles
+    whole = pl.BlockSpec((rows, width), lambda i: (0, 0), pipeline_mode=pl.Buffered(1))
+    tile = pl.BlockSpec((rows, cols), lambda i: (0, i))
+    return pl.pallas_call(
+        functools.partial(feed_kernel, rows // 2),
+        grid=(tiles,),
+        in_specs=[whole, whole]
+        + [pl.BlockSpec((width, cols), lambda i: (0, i))] * 2
+        + [pl.BlockSpec((cols, width), lambda i: (i, 0))],
+        out_specs=[whole, whole, tile, tile, tile],
+        out_shape=[jax.ShapeDtypeStruct((rows, width), jnp.float32)] * 2
+        + [jax.ShapeDtypeStruct((rows, tiles * cols), jnp.bfloat16)] * 3,
+        cost_estimate=pl.CostEstimate(
+            flops=12 * rows * width * cols * tiles,
+            bytes_accessed=70 * 1024 * 1024,
+            transcendentals=rows * cols * tiles,
+        ),
+        compiler_params=pltpu.CompilerParams(vmem_limit_bytes=56 * 1024 * 1024),
+    )(n2, e, gate_matrix, up_matrix, down_matrix)
+
+
+CORE_ROUTE = ((0, 1), (1, 0))
+
+
+def over_core(give):
+    return lax.ppermute(give, "shard", CORE_ROUTE)
+
+
+def scale_of(values):
+    return lax.rsqrt(jnp.mean(values * values, axis=-1, keepdims=True) + EPSILON)
+
+
+def shifted(values, edge, distance):
+    rows = values.shape[0]
+    moved = pltpu.roll(values, (-distance) % rows, 0)
+    index = lax.broadcasted_iota(jnp.int32, values.shape, 0)
+    if distance < 0:
+        for row in range(-distance):
+            moved = jnp.where(index == row, edge[8 + distance + row : 9 + distance + row, :], moved)
+    else:
+        for row in range(distance):
+            moved = jnp.where(index == rows - distance + row, edge[row : row + 1, :], moved)
+    return moved
+
+
+def mixer_kernel(
+    x_ref, edge_ref, masks, gain_one, gain_two, taps, w_in, w_out, proj, conv, hid, n1t, zt, n2, n2t, carry
+):
+    width = x_ref.shape[1]
+    low = jnp.bfloat16
+
+    def project(values, first, count):
+        return kernel_dot(values, w_in[:, first * width : (first + count) * width])
+
+    def normed(values):
+        return (values * scale_of(values) * gain_one[...]).astype(low)
+
+    @pl.when(pl.program_id(0) == 0)
+    def _():
+        edge = normed(edge_ref[...].astype(jnp.float32))
+        mixed = project(edge, 0, 1) * project(edge, 2, 1)
+        carry[...] = mixed[8:, :]
+
+    x = x_ref[...].astype(jnp.float32)
+    first = normed(x)
+    n1t[...] = first.T
+    gate_b, gate_c, values = project(first, 0, 1), project(first, 1, 1), project(first, 2, 1)
+    proj[:, :width] = gate_b
+    proj[:, width : 2 * width] = gate_c
+    proj[:, 2 * width :] = values
+    mixed = gate_b * values
+    edge = carry[...]
+    convolved = (
+        taps[2:3, :] * mixed
+        + taps[1:2, :] * masks[:, 0:1] * shifted(mixed, edge, -1)
+        + taps[0:1, :] * masks[:, 1:2] * shifted(mixed, edge, -2)
+    )
+    carry[...] = mixed[mixed.shape[0] - 8 :, :]
+    conv[...] = convolved
+    mixer_out = (gate_c * convolved).astype(low)
+    zt[...] = mixer_out.T
+    hidden = x + kernel_dot(mixer_out, w_out[...])
+    hid[...] = hidden
+    second = (hidden * scale_of(hidden) * gain_two[...]).astype(low)
+    n2[...] = second
+    n2t[...] = second.T
+
+
+def resident(shape):
+    return pl.BlockSpec(shape, lambda i: (0,) * len(shape), pipeline_mode=pl.Buffered(1))
+
+
+def mixer(x, edge, masks, gain_one, gain_two, taps, w_in, w_out):
+    rows, width = x.shape
+    step = rows // 4
+    tile = lambda cols: pl.BlockSpec((step, cols), lambda i: (i, 0))
+    turned = pl.BlockSpec((width, step), lambda i: (0, i))
+    low, full = jnp.bfloat16, jnp.float32
+    shape = jax.ShapeDtypeStruct
+    return pl.pallas_call(
+        mixer_kernel,
+        grid=(4,),
+        in_specs=[
+            tile(width),
+            resident(edge.shape),
+            tile(masks.shape[1]),
+            resident(gain_one.shape),
+            resident(gain_two.shape),
+            resident(taps.shape),
+            resident(w_in.shape),
+            resident(w_out.shape),
+        ],
+        out_specs=[tile(3 * width), tile(width), tile(width), turned, turned, tile(width), turned],
+        out_shape=[
+            shape((rows, 3 * width), full),
+            shape((rows, width), full),
+            shape((rows, width), full),
+            shape((width, rows), low),
+            shape((width, rows), low),
+            shape((rows, width), low),
+            shape((width, rows), low),
+        ],
+        scratch_shapes=[pltpu.VMEM((8, width), full)],
+        compiler_params=pltpu.CompilerParams(vmem_limit_bytes=56 * 1024 * 1024),
+        cost_estimate=pl.CostEstimate(
+            flops=8 * rows * width * width, bytes_accessed=48 * rows * width, transcendentals=0
+        ),
+    )(x, edge, masks, gain_one, gain_two, taps, w_in, w_out)
+
+
+def out_back_kernel(parts, *refs):
+    h_ref, c_ref, gc_ref, e_ref, gain_two, w_out, zt = refs[:7]
+    outs, backs = refs[7 : 7 + parts], refs[7 + parts : 7 + 2 * parts]
+    block_out, hidden_grad, gc_grad, conv_grad, gain_grad, keep, give, total = refs[-8:]
+    step = pl.program_id(0)
     core = lax.axis_index("shard")
-    group = lax.axis_index("dp")
-    x_bit, y_bit = lax.rem(group, 2), lax.div(group, 2)
-    rows = gradient.shape[0] // 2
-    give = lax.dynamic_slice_in_dim(gradient, (1 - core) * rows, rows, 0)
-    keep = lax.dynamic_slice_in_dim(gradient, core * rows, rows, 0)
-    got = lax.ppermute(give, "shard", ((0, 1), (1, 0)))
-    half = (keep.astype(jnp.float32) + got.astype(jnp.float32)).astype(jnp.bfloat16)
-    part = half[: rows // 2]
-    other = half[rows // 2 :]
-    part = halve(halve(part, x_bit, 0), y_bit, 1)
-    other = halve(halve(other, y_bit, 1), x_bit, 0)
-    return jnp.concatenate([part, other], 0)
+    hidden = h_ref[...]
+    gain = gain_two[...]
+    summed = hidden
+    for ref in outs:
+        summed = summed + ref[...]
+    block_out[...] = summed.astype(jnp.bfloat16)
+    upstream = backs[0][...]
+    for ref in backs[1:]:
+        upstream = upstream + ref[...]
+    scale = scale_of(hidden)
+    inner = jnp.mean(hidden * gain * upstream, axis=-1, keepdims=True)
+    grad = (
+        e_ref[...].astype(jnp.float32)
+        + scale * gain * upstream
+        - hidden * (scale * scale * scale * inner)
+    )
+    hidden_grad[...] = grad
+    low = grad.astype(jnp.bfloat16)
+    share = jnp.sum(upstream * hidden * scale, axis=0, keepdims=True)
+    mixer_grad = kernel_dot(low, w_out[...], BACK_DOT)
+    gc_grad[...] = (mixer_grad * c_ref[...]).astype(jnp.bfloat16)
+    conv_grad[...] = mixer_grad * gc_ref[...]
+
+    @pl.when(step == 0)
+    def _():
+        total[...] = jnp.zeros_like(total)
+        gain_grad[...] = jnp.zeros_like(gain_grad)
+
+    gain_grad[0:1, :] += share
+    total[...] += kernel_dot(zt[...], low)
+
+    @pl.when(step == pl.num_programs(0) - 1)
+    def _():
+        rows = total.shape[0] // 2
+        for target, side in ((keep, core), (give, 1 - core)):
+            target[...] = total[pl.ds(pl.multiple_of(side * rows, rows), rows), :].astype(
+                jnp.bfloat16
+            )
+
+
+def skip_last(kernel, inputs, extra):
+    def wrapped(*refs):
+        return kernel(*refs[:inputs], *refs[inputs + extra :])
+
+    return wrapped
+
+
+def out_back(hidden, convolved, proj, e, gain_two, w_out, zt, outs, backs, order):
+    rows, width = hidden.shape
+    step = rows // 4
+    tile = pl.BlockSpec((step, width), lambda i: (i, 0))
+    low, full = jnp.bfloat16, jnp.float32
+    shape = jax.ShapeDtypeStruct
+    inputs = 7 + len(outs) + len(backs)
+    return pl.pallas_call(
+        skip_last(functools.partial(out_back_kernel, len(outs)), inputs, len(order)),
+        grid=(4,),
+        in_specs=[
+            tile,
+            tile,
+            pl.BlockSpec((step, width), lambda i: (i, 1)),
+            tile,
+            resident(gain_two.shape),
+            resident(w_out.shape),
+            pl.BlockSpec((width, step), lambda i: (0, i)),
+        ]
+        + [tile] * (len(outs) + len(backs))
+        + [ANY] * len(order),
+        out_specs=[tile] * 4 + [resident((8, width))] + [resident((width // 2, width))] * 2,
+        out_shape=[
+            shape((rows, width), low),
+            shape((rows, width), full),
+            shape((rows, width), low),
+            shape((rows, width), full),
+            shape((8, width), full),
+            shape((width // 2, width), low),
+            shape((width // 2, width), low),
+        ],
+        scratch_shapes=[pltpu.VMEM((width, width), full)],
+        compiler_params=pltpu.CompilerParams(vmem_limit_bytes=56 * 1024 * 1024),
+        cost_estimate=pl.CostEstimate(
+            flops=4 * rows * width * width, bytes_accessed=48 * rows * width, transcendentals=0
+        ),
+    )(hidden, convolved, proj, e, gain_two, w_out, zt, *outs, *backs, *order)
+
+
+def conv_back_kernel(
+    dc_ref, dgc, gb_ref, v_ref, masks, edge_ref, taps, n1t, dp_ref, taps_grad, keep, give, carry, all_dp
+):
+    step = pl.program_id(0)
+    last = pl.num_programs(0) - 1
+    core = lax.axis_index("shard")
+    rows, width = dc_ref.shape
+    low = jnp.bfloat16
+
+    @pl.when(step == 0)
+    def _():
+        carry[...] = edge_ref[...]
+        taps_grad[...] = jnp.zeros_like(taps_grad)
+
+    grad = dc_ref[...]
+    edge = carry[...]
+    next_one = masks[:, 2:3] * shifted(grad, edge, 1)
+    next_two = masks[:, 3:4] * shifted(grad, edge, 2)
+    carry[...] = grad[:8, :]
+    gate_b, values = gb_ref[...], v_ref[...]
+    mixed = gate_b * values
+    for row, term in ((0, next_two), (1, next_one), (2, grad)):
+        taps_grad[row : row + 1, :] += jnp.sum(term * mixed, axis=0, keepdims=True)
+    mixed_grad = taps[2:3, :] * grad + taps[1:2, :] * next_one + taps[0:1, :] * next_two
+    place = pl.ds(pl.multiple_of((last - step) * rows, rows), rows)
+    for k, block in enumerate(
+        ((mixed_grad * values).astype(low), dgc[...], (mixed_grad * gate_b).astype(low))
+    ):
+        dp_ref[:, k * width : (k + 1) * width] = block
+        all_dp[place, k * width : (k + 1) * width] = block
+
+    @pl.when(step == last)
+    def _():
+        half = width // 2
+        for target, side in ((keep, core), (give, 1 - core)):
+            left = n1t[pl.ds(pl.multiple_of(side * half, half), half), :]
+            for k in range(3):
+                cols = slice(k * width, (k + 1) * width)
+                target[:, cols] = kernel_dot(left, all_dp[:, cols]).astype(low)
+
+
+def conv_back(conv_grad, gc_grad, proj, masks, edge, taps, n1t, order):
+    rows, width = conv_grad.shape
+    step = rows // 4
+    tile = lambda cols, k=0: pl.BlockSpec((step, cols), lambda i: (3 - i, k))
+    low, full = jnp.bfloat16, jnp.float32
+    shape = jax.ShapeDtypeStruct
+    return pl.pallas_call(
+        skip_last(conv_back_kernel, 8, len(order)),
+        grid=(4,),
+        in_specs=[
+            tile(width),
+            tile(width),
+            tile(width, 0),
+            tile(width, 2),
+            tile(masks.shape[1]),
+            resident(edge.shape),
+            resident(taps.shape),
+            resident(n1t.shape),
+        ]
+        + [ANY] * len(order),
+        out_specs=[tile(3 * width), resident((8, width))] + [resident((width // 2, 3 * width))] * 2,
+        out_shape=[
+            shape((rows, 3 * width), low),
+            shape((8, width), full),
+            shape((width // 2, 3 * width), low),
+            shape((width // 2, 3 * width), low),
+        ],
+        scratch_shapes=[pltpu.VMEM((8, width), full), pltpu.VMEM((rows, 3 * width), low)],
+        compiler_params=pltpu.CompilerParams(vmem_limit_bytes=56 * 1024 * 1024),
+        cost_estimate=pl.CostEstimate(
+            flops=6 * rows * width * width, bytes_accessed=32 * rows * width, transcendentals=0
+        ),
+    )(conv_grad, gc_grad, proj, proj, masks, edge, taps, n1t, *order)
+
+
+def in_back_kernel(dp_ref, w_in, x_ref, grad_ref, gain_one, input_grad, gain_grad):
+    upstream = kernel_dot(dp_ref[...], w_in[...], BACK_DOT)
+    x = x_ref[...].astype(jnp.float32)
+    gain = gain_one[...]
+    scale = scale_of(x)
+    inner = jnp.mean(x * gain * upstream, axis=-1, keepdims=True)
+    input_grad[...] = (
+        grad_ref[...] + scale * gain * upstream - x * (scale * scale * scale * inner)
+    ).astype(jnp.bfloat16)
+
+    @pl.when(pl.program_id(0) == 0)
+    def _():
+        gain_grad[...] = jnp.zeros_like(gain_grad)
+
+    gain_grad[0:1, :] += jnp.sum(upstream * x * scale, axis=0, keepdims=True)
+
+
+def in_back(dp, w_in, x, hidden_grad, gain_one, order):
+    rows, width = x.shape
+    step = rows // 4
+    tile = lambda cols: pl.BlockSpec((step, cols), lambda i: (i, 0))
+    return pl.pallas_call(
+        skip_last(in_back_kernel, 5, len(order)),
+        grid=(4,),
+        in_specs=[
+            tile(3 * width),
+            resident(w_in.shape),
+            tile(width),
+            tile(width),
+            resident(gain_one.shape),
+        ]
+        + [ANY] * len(order),
+        out_specs=[tile(width), resident((8, width))],
+        out_shape=[
+            jax.ShapeDtypeStruct((rows, width), jnp.bfloat16),
+            jax.ShapeDtypeStruct((8, width), jnp.float32),
+        ],
+        compiler_params=pltpu.CompilerParams(vmem_limit_bytes=56 * 1024 * 1024),
+        cost_estimate=pl.CostEstimate(
+            flops=6 * rows * width * width, bytes_accessed=20 * rows * width, transcendentals=0
+        ),
+    )(dp, w_in, x, hidden_grad, gain_one, *order)
+
+
+def base_kernel(rate, master, moment, base):
+    base[...] = (
+        master[...] * (1.0 - rate[0] * WEIGHT_DECAY) - (rate[0] * MOMENTUM_BETA) * moment[...]
+    ).astype(jnp.bfloat16)
+
+
+def base_of(rate, master, moment, order):
+    rows, cols = master.shape
+    step = rows // 4
+    tile = pl.BlockSpec((step, cols), lambda i: (i, 0))
+    return pl.pallas_call(
+        skip_last(base_kernel, 3, len(order)),
+        grid=(4,),
+        in_specs=[pl.BlockSpec(memory_space=pltpu.SMEM), tile, tile] + [ANY] * len(order),
+        out_specs=tile,
+        out_shape=jax.ShapeDtypeStruct((rows, cols), jnp.bfloat16),
+        compiler_params=pltpu.CompilerParams(vmem_limit_bytes=40 * 1024 * 1024),
+        cost_estimate=pl.CostEstimate(
+            flops=3 * rows * cols, bytes_accessed=10 * rows * cols, transcendentals=0
+        ),
+    )(rate, master, moment, *order)
+
+
+def update_kernel(bits, scalars, *refs):
+    core = bits[2]
+    clip, scale = scalars[0], scalars[1]
+    count = len(refs) // 7
+    for n in range(count):
+        own, other, base_own, base_other, moment = refs[5 * n : 5 * n + 5]
+        weight, new_moment = refs[5 * count + 2 * n : 5 * count + 2 * n + 2]
+        rows = own.shape[0]
+        gradient = own[...].astype(jnp.float32)
+        new_moment[...] = MOMENTUM_BETA * moment[...] + clip * gradient
+        mine = pl.ds(pl.multiple_of(core * rows, rows), rows)
+        theirs = pl.ds(pl.multiple_of((1 - core) * rows, rows), rows)
+        weight[mine, :] = (base_own[...].astype(jnp.float32) - scale * gradient).astype(jnp.bfloat16)
+        weight[theirs, :] = (
+            base_other[...].astype(jnp.float32) - scale * other[...].astype(jnp.float32)
+        ).astype(jnp.bfloat16)
+
+
+def update_rows(bits, scalars, grid, block, matrices):
+    width = block[1]
+    in_specs, out_specs, out_shape, operands = [], [], [], []
+    total = 0
+    for gradient, source, column, base, base_other, moment in matrices:
+        in_specs += [
+            pl.BlockSpec(block, lambda *a, source=source: source(a[-1][2], *a[:-1])),
+            pl.BlockSpec(block, lambda *a, source=source: source(1 - a[-1][2], *a[:-1])),
+        ]
+        in_specs += [pl.BlockSpec(block, lambda *a, column=column: (0, column(*a[:-1])))] * 3
+        out_specs += [
+            pl.BlockSpec((2 * block[0], width), lambda *a, column=column: (0, column(*a[:-1]))),
+            pl.BlockSpec(block, lambda *a, column=column: (0, column(*a[:-1]))),
+        ]
+        rows, cols = moment.shape
+        total += rows * cols
+        out_shape += [
+            jax.ShapeDtypeStruct((2 * rows, cols), jnp.bfloat16),
+            jax.ShapeDtypeStruct((rows, cols), jnp.float32),
+        ]
+        operands += [gradient, gradient, base, base_other, moment]
+    in_specs = [pl.BlockSpec(memory_space=pltpu.SMEM)] + in_specs
+    return pl.pallas_call(
+        update_kernel,
+        grid_spec=pltpu.PrefetchScalarGridSpec(
+            num_scalar_prefetch=1, grid=grid, in_specs=in_specs, out_specs=out_specs
+        ),
+        out_shape=out_shape,
+        compiler_params=pltpu.CompilerParams(vmem_limit_bytes=48 * 1024 * 1024),
+        cost_estimate=pl.CostEstimate(flops=8 * total, bytes_accessed=20 * total, transcendentals=0),
+    )(bits, scalars, *operands)
+
+
+def update_down_kernel(bits, scalars, own, other, base_own, base_other, moment, weight, new_moment):
+    core = bits[2]
+    clip, scale = scalars[0], scalars[1]
+    gradient = own[...].astype(jnp.float32).T
+    new_moment[...] = MOMENTUM_BETA * moment[...] + clip * gradient
+    weight[core] = (base_own[...].astype(jnp.float32) - scale * gradient).astype(jnp.bfloat16)
+    gradient = other[...].astype(jnp.float32).T
+    weight[1 - core] = (base_other[...].astype(jnp.float32) - scale * gradient).astype(jnp.bfloat16)
+
+
+def update_down(bits, scalars, gradient, parts, base, base_other, moment):
+    rows, width = moment.shape
+    cols = gradient.shape[1]
+    subs = 2
+    step = cols // subs
+    row = pl.BlockSpec((step, width), lambda k, t, b: (k * subs + t, 0))
+    weight, new_moment = pl.pallas_call(
+        update_down_kernel,
+        grid_spec=pltpu.PrefetchScalarGridSpec(
+            num_scalar_prefetch=1,
+            grid=(parts, subs),
+            in_specs=[
+                pl.BlockSpec(memory_space=pltpu.SMEM),
+                pl.BlockSpec((width, step), lambda k, t, b: ((k * 3 + 2) * 2 + b[2], t)),
+                pl.BlockSpec((width, step), lambda k, t, b: ((k * 3 + 2) * 2 + 1 - b[2], t)),
+                row,
+                row,
+                row,
+            ],
+            out_specs=[pl.BlockSpec((2, step, width), lambda k, t, b: (0, k * subs + t, 0)), row],
+        ),
+        out_shape=[
+            jax.ShapeDtypeStruct((2, rows, width), jnp.bfloat16),
+            jax.ShapeDtypeStruct((rows, width), jnp.float32),
+        ],
+        compiler_params=pltpu.CompilerParams(vmem_limit_bytes=48 * 1024 * 1024),
+        cost_estimate=pl.CostEstimate(
+            flops=8 * rows * width, bytes_accessed=20 * rows * width, transcendentals=0
+        ),
+    )(bits, scalars, gradient, gradient, base, base_other, moment)
+    return weight.reshape(2 * rows, width), new_moment
 
 
 def local_fast(
@@ -426,127 +1046,121 @@
     down_matrix = whole[7]
     seq_count, span, model_width = tokens.shape
     row_count = seq_count * span
-    hidden_in = tokens.reshape(row_count, model_width).astype(jnp.float32)
+    x = tokens.reshape(row_count, model_width)
+    e = cotangent.reshape(row_count, model_width)
+    core = lax.axis_index("shard")
+    group = lax.axis_index("dp")
+    bits = jnp.stack([lax.rem(group, 2), lax.div(group, 2), core]).astype(jnp.int32)
     start = lax.axis_index("seq") * span
     padding = jnp.full((seq_count, 2), -1, jnp.int32)
     extended = jnp.concatenate([padding, segments, padding], 1)
     current = segment_window(extended, start, 0, span)
-    keep_one = (
-        (segment_window(extended, start, -1, span) == current)
-        .astype(jnp.float32)
-        .reshape(row_count, 1)
-    )
-    keep_two = (
-        (segment_window(extended, start, -2, span) == current)
-        .astype(jnp.float32)
-        .reshape(row_count, 1)
-    )
-    next_one = (
-        (segment_window(extended, start, 1, span) == current)
-        .astype(jnp.float32)
-        .reshape(row_count, 1)
-    )
-    next_two = (
-        (segment_window(extended, start, 2, span) == current)
-        .astype(jnp.float32)
-        .reshape(row_count, 1)
-    )
-    normed_f, scale_one = norm_forward(hidden_in, gain_one)
-    normed_one = normed_f.astype(jnp.bfloat16)
-    projected = rows_dot(normed_one, in_matrix)
-    gate_b = projected[:, :model_width]
-    gate_c = projected[:, model_width : 2 * model_width]
-    values = projected[:, 2 * model_width :]
-    mixed_in = gate_b * values
-    mixed_grid = mixed_in.reshape(seq_count, span, model_width)
-    before_edge = from_behind(mixed_grid[:, span - 2 :, :], "seq", 1)
-    before = jnp.concatenate([before_edge, mixed_grid], 1)
-    before_one = before[:, 1:-1, :].reshape(row_count, model_width)
-    before_two = before[:, :-2, :].reshape(row_count, model_width)
-    convolved = (
-        conv_taps[2] * mixed_in
-        + conv_taps[1] * keep_one * before_one
-        + conv_taps[0] * keep_two * before_two
-    )
-    mixer_out = (gate_c * convolved).astype(jnp.bfloat16)
-    hidden = hidden_in + rows_dot(mixer_out, out_matrix)
-    normed_g, scale_two = norm_forward(hidden, gain_two)
-    normed_two = normed_g.astype(jnp.bfloat16)
-    gate_pre = rows_dot(normed_two, gate_matrix)
-    upward = rows_dot(normed_two, up_matrix)
-    sigmoid_gate = jax.nn.sigmoid(gate_pre)
-    activated = (gate_pre * sigmoid_gate * upward).astype(jnp.bfloat16)
-    block_out = (
-        (hidden + rows_dot(activated, down_matrix)).astype(jnp.bfloat16).reshape(tokens.shape)
-    )
-    cotangent_rows = cotangent.reshape(row_count, model_width)
-    down_grad = outer_dot(activated, cotangent_rows).astype(jnp.bfloat16)
-    act_grad = back_dot(cotangent_rows, down_matrix)
-    gate_back = (act_grad * upward * sigmoid_gate * (1.0 + gate_pre * (1.0 - sigmoid_gate))).astype(
-        jnp.bfloat16
-    )
-    up_back = (act_grad * gate_pre * sigmoid_gate).astype(jnp.bfloat16)
-    gate_grad = outer_dot(normed_two, gate_back).astype(jnp.bfloat16)
-    up_grad = outer_dot(normed_two, up_back).astype(jnp.bfloat16)
-    normed_two_grad = back_dot(gate_back, gate_matrix) + back_dot(up_back, up_matrix)
-    hidden_part, gain_two_grad = norm_backward(hidden, scale_two, gain_two, normed_two_grad)
-    hidden_grad = cotangent_rows.astype(jnp.float32) + hidden_part
-    hidden_low = hidden_grad.astype(jnp.bfloat16)
-    out_grad = outer_dot(mixer_out, hidden_low).astype(jnp.bfloat16)
-    mixer_grad = back_dot(hidden_low, out_matrix)
-    gate_c_grad = mixer_grad * convolved
-    conv_out_grad = mixer_grad * gate_c
-    conv_grid = conv_out_grad.reshape(seq_count, span, model_width)
-    after_edge = from_behind(conv_grid[:, :2, :], "seq", -1)
-    after = jnp.concatenate([conv_grid, after_edge], 1)
-    follow_one = after[:, 1:-1, :].reshape(row_count, model_width)
-    follow_two = after[:, 2:, :].reshape(row_count, model_width)
-    mixed_grad = (
-        conv_taps[2] * conv_out_grad
-        + conv_taps[1] * next_one * follow_one
-        + conv_taps[0] * next_two * follow_two
-    )
-    conv_grad = jnp.stack(
+    masks = jnp.stack(
         [
-            jnp.sum(conv_out_grad * keep_two * before_two, axis=0),
-            jnp.sum(conv_out_grad * keep_one * before_one, axis=0),
-            jnp.sum(conv_out_grad * mixed_in, axis=0),
+            (segment_window(extended, start, offset, span) == current).reshape(row_count)
+            for offset in (-1, -2, 1, 2)
         ],
-        0,
-    )
-    proj_back = jnp.concatenate([mixed_grad * values, gate_c_grad, mixed_grad * gate_b], 1).astype(
-        jnp.bfloat16
-    )
-    in_grad = outer_dot(normed_one, proj_back).astype(jnp.bfloat16)
-    normed_one_grad = back_dot(proj_back, in_matrix)
-    input_part, gain_one_grad = norm_backward(hidden_in, scale_one, gain_one, normed_one_grad)
-    input_grad = (hidden_grad + input_part).astype(jnp.bfloat16).reshape(tokens.shape)
-    core = lax.axis_index("shard")
-    pieces = [scatter_piece(g) for g in (out_grad, in_grad, gate_grad, up_grad, down_grad)]
+        1,
+    ).astype(jnp.float32)
+    edge = from_behind(x[row_count - 16 :, :], "seq", 1)
+    gain_one_row, gain_two_row = gain_one[None], gain_two[None]
+    proj, convolved, hidden, n1t, zt, n2, n2t = mixer(
+        x, edge, masks, gain_one_row, gain_two_row, conv_taps, in_matrix, out_matrix
+    )
+    et = e.T
+    feed_out, feed_back, act, gate_back, up_back = feed(
+        n2, e, gate_matrix, up_matrix, down_matrix, 2 * FEED_PARTS
+    )
+    block_out, hidden_grad, gc_grad, conv_out_grad, gain_two_grad, out_keep, out_give = out_back(
+        hidden,
+        convolved,
+        proj,
+        e,
+        gain_two_row,
+        out_matrix,
+        zt,
+        [feed_out],
+        [feed_back],
+        [],
+    )
+    after_edge = from_behind(conv_out_grad[:8, :], "seq", -1)
+    proj_back, taps_grad, in_keep, in_give = conv_back(
+        conv_out_grad, gc_grad, proj, masks, after_edge, conv_taps, n1t, []
+    )
+    input_grad, gain_one_grad = in_back(
+        proj_back, in_matrix, x, hidden_grad, gain_one_row, []
+    )
+    rate_now = learn_rate * jnp.minimum(1.0, (step_number + 1).astype(jnp.float32) / WARMUP)
+    rate = rate_now.reshape(1)
+    base, base_other = {}, {}
+    for place in (5, 6, 7, 1, 3):
+        base[place] = base_of(rate, masters[place], moments[place], [proj_back])
+        base_other[place] = over_core(base[place])
+    input_grad = input_grad.reshape(tokens.shape)
+    block_out = block_out.reshape(tokens.shape)
     small = jnp.concatenate(
-        [gain_one_grad[None], conv_grad, gain_two_grad[None], jnp.zeros((3, model_width))], 0
-    )
-    wholes, small_sum, squares = finish(pieces, small)
+        [gain_one_grad[:1], taps_grad[:3], gain_two_grad[:1], jnp.zeros((3, model_width))], 0
+    )
+    hidden_units = gate_matrix.shape[1]
+    cols = hidden_units // (2 * FEED_PARTS)
+    wholes, small_sum, squares = finish(
+        (out_keep, out_give),
+        (in_keep, in_give),
+        n2t,
+        et,
+        gate_back,
+        up_back,
+        act,
+        FEED_PARTS,
+        small,
+        [base[place] for place in (5, 6, 7, 1, 3)],
+    )
     param_count = sum((member.size for member in whole))
     clip_level = CLIP_RATIO * math.sqrt(param_count)
-    rate_now = learn_rate * jnp.minimum(1.0, (step_number + 1).astype(jnp.float32) / WARMUP)
     grad_norm = jnp.sqrt(jnp.sum(squares) + jnp.sum(small_sum * small_sum))
     clip_factor = clip_level / jnp.maximum(grad_norm, clip_level)
-    large = (3, 1, 5, 6, 7)
-    new_moment = {}
-    new_weight = {}
-    for place, gradient in zip(large, wholes):
-        master, moment = masters[place], moments[place]
-        rows = master.shape[0]
-        base = master * (1.0 - rate_now * WEIGHT_DECAY) - (rate_now * MOMENTUM_BETA) * moment
-        base = lax.all_gather(base.astype(jnp.bfloat16), "shard", axis=0, tiled=True)
-        new_weight[place] = (
-            base.astype(jnp.float32) - (rate_now * clip_factor) * gradient.astype(jnp.float32)
-        ).astype(jnp.bfloat16)
-        own = lax.dynamic_slice_in_dim(gradient, core * rows, rows, 0).astype(jnp.float32)
-        new_moment[place] = MOMENTUM_BETA * moment + clip_factor * own
-    width = model_width // 2
-    small_own = lax.dynamic_slice_in_dim(small_sum, core * width, width, 1)
+    scalars = jnp.stack([clip_factor, rate_now * clip_factor])
+    half = model_width // 2
+    narrow = cols // 2
+
+    def feed_matrix(place, kind):
+        return (
+            wholes[2],
+            lambda side, k, i, t: ((k * 3 + kind) * 4 + side * 2 + i, t),
+            lambda k, i, t: (i * FEED_PARTS + k) * 2 + t,
+            base[place],
+            base_other[place],
+            moments[place],
+        )
+
+    def plain_matrix(place, gradient):
+        return (
+            gradient,
+            lambda side, t: (side, t),
+            lambda t: t,
+            base[place],
+            base_other[place],
+            moments[place],
+        )
+
+    new_weight, new_moment = {}, {}
+    new_weight[3], new_moment[3] = update_rows(
+        bits, scalars, (2,), (half, half), [plain_matrix(3, wholes[0])]
+    )
+    new_weight[5], new_moment[5], new_weight[6], new_moment[6] = update_rows(
+        bits,
+        scalars,
+        (FEED_PARTS, 2, 2),
+        (half, narrow),
+        [feed_matrix(5, 0), feed_matrix(6, 1)],
+    )
+    new_weight[7], new_moment[7] = update_down(
+        bits, scalars, wholes[2], FEED_PARTS, base[7], base_other[7], moments[7]
+    )
+    new_weight[1], new_moment[1] = update_rows(
+        bits, scalars, (6,), (half, half), [plain_matrix(1, wholes[1])]
+    )
+    small_own = lax.dynamic_slice_in_dim(small_sum, core * half, half, 1)
     for place, gradient in ((0, small_own[0]), (2, small_own[1:4]), (4, small_own[4])):
         new_moment[place] = MOMENTUM_BETA * moments[place] + clip_factor * gradient
     return (

time: 892 us -> 718 us (0.80)
  Pallas kernels: 234 us -> 576 us
  matrix products: 201 us -> 0 us
  other arithmetic: 229 us -> 36.3 us
  waiting for transfers between devices: 118 us -> 50.5 us
  local copies, waits for them, and re-layouts: 49.2 us -> 19 us
  starting transfers between devices: 28 us -> 8.52 us
    pallas_call x1 -> x15, Pallas kernels: 234 us -> 576 us  [the longest x1 333 us: finish(): pl.pallas_call(functools.partial(finish_kernel, tuple(chunks), parts, len...]
    dot_general x15 -> x0, matrix products: 201 us -> none  [the longest x5 79.9 us: back_dot(): lax.dot_general(left, right, (((1,), (1,)), ((), ())), preferred_element_...]
    convert_element_type x39 -> x7, other arithmetic: 163 us -> 28.6 us  [the longest x1 6.79 us: local_fast(): down_weight.astype(jnp.bfloat16)]
    ppermute x25 -> x5, waiting for transfers between devices: 115 us -> 0.01 us  [over_core(): return lax.ppermute(give, 'shard', CORE_ROUTE)]
    add x5 -> x0, other arithmetic: 39.1 us -> none  [the longest x4 37.8 us: local_fast(): new_moment[place] = MOMENTUM_BETA * moment + clip_factor * own]
    all_gather x1, waiting for transfers between devices: 0.01 us -> 25 us  [local_fast(): lax.all_gather(down_weight.astype(jnp.bfloat16), 'shard', axis=0, tiled=T...]
    all_gather x1, waiting for transfers between devices: 0.02 us -> 22.4 us  [local_fast(): lax.all_gather(up_weight.astype(jnp.bfloat16), 'shard', axis=0, tiled=True)]
    ppermute x25 -> x5, starting transfers between devices: 21.4 us -> 1.15 us  [over_core(): return lax.ppermute(give, 'shard', CORE_ROUTE)]
  transfers between devices with their start and end apart: 37 -> 12, of which waited for: 13 -> 3; matrix products, arithmetic and copies ran while one was open for 50% -> 5% of each run, Pallas kernels for 26% -> 60%
where the time goes in v2:
time: 718 us; the launch traced here: 714 us
  Pallas kernels  576 us (80%)
  waiting for transfers between devices  50.5 us (7%)
  other arithmetic  36.3 us (5%)
  local copies, waits for them, and re-layouts  19 us (3%)
  between operations  18 us (3%)
  starting transfers between devices  8.52 us (1%)
    pallas_call x1, Pallas kernels, finish(): pl.pallas_call(functools.partial(finish_kernel, tuple(chunks), parts, len...  333 us
    pallas_call x1, Pallas kernels, feed(): pl.pallas_call(functools.partial(feed_kernel, rows // 2), grid=(tiles,),...  71.2 us
    pallas_call x3, Pallas kernels, update_rows(): pl.pallas_call(update_kernel, grid_spec=pltpu.PrefetchScalarGridSpec(num_...  49.1 us
    pallas_call x5, Pallas kernels, base_of(): pl.pallas_call(skip_last(base_kernel, 3, len(order)), grid=(4,), in_specs...  32.2 us
    all_gather x1, waiting for transfers between devices, local_fast(): lax.all_gather(down_weight.astype(jnp.bfloat16), 'shard', axis=0, tiled=T...  25 us
    all_gather x1, waiting for transfers between devices, local_fast(): lax.all_gather(up_weight.astype(jnp.bfloat16), 'shard', axis=0, tiled=True)  22.4 us
    pallas_call x1, Pallas kernels, mixer(): pl.pallas_call(mixer_kernel, grid=(4,), in_specs=[tile(width), resident(e...  20.7 us
    pallas_call x1, Pallas kernels, conv_back(): pl.pallas_call(skip_last(conv_back_kernel, 8, len(order)), grid=(4,), in_...  19.5 us
  transfers between devices with their start and end apart: 12, of which 3 were waited for; matrix products, arithmetic and copies ran while one was open for 5% of the time, Pallas kernels for 60%

profile of v2, /device:TPU:0, one launch (start us, length us, event | category | flops | bytes accessed | tf_op | source)
XLA Modules:
  0.0 714.0 jit_solution(12745909551469114473)
XLA Ops:
  7.2 2.7 convert_element_type.41
  10.0 4.9 convert_element_type.40
  15.0 6.4 convert_element_type.42
  21.5 6.4 convert_element_type.43
  27.9 6.8 convert_element_type.44
  35.6 5.7 collective-permute-start
  42.8 1.8 all-gather
  45.1 1.8 all-gather.1
  47.5 2.0 all_gather.26
  50.7 20.7 %shard_map.324 = (f32[1024,3072]{1,0:T(8,128)}, f32[1024,1024]{1,0:T(8,128)}, f32[1024,1024]{1,0:T(8,128)}, bf16[1024,1024]{1,0:T(8,128)(2,1)}, bf16[1024,1024]{...) custom-call(bf16[1024,1024]{1,0:T(8,128)(2,1)} %bitcast.39, bf16[16,1024]{1,0:T(8,128)(2,1)} %copy-done.17, ...), custom_call_target="tpu_custom_call" | custom-call | flops 8589934592 | bytes 50331648 | tf_op jit(solution)/shard_map/pallas_call | solution.py:626
  71.4 22.4 %all-gather.14.cloned.1.call-done.wu = bf16[1024,4608]{1,0:T(8,128)(2,1)} async-done(((bf16[512,4608]{1,0:T(8,128)(2,1)}), bf16[1024,4608]{1,0:T(8,128)(2,1)}) %all-gather.14.cloned.1.call-update) | async-done | bytes 9437200 | tf_op jit(solution)/shard_map/all_gather | solution.py:1036
  93.8 25.0 %all-gather.16.cloned.1.call-done.wd = bf16[4608,1024]{1,0:T(8,128)(2,1)} async-done(((bf16[2304,1024]{1,0:T(8,128)(2,1)}), bf16[4608,1024]{1,0:T(8,128)(2,1)}) %all-gather.16.cloned.1.call-update) | async-done | bytes 9437200 | tf_op jit(solution)/shard_map/all_gather | solution.py:1037
  118.8 71.2 %shard_map.325 = (f32[1024,1024]{1,0:T(8,128)}, f32[1024,1024]{1,0:T(8,128)}, bf16[1024,4608]{1,0:T(8,128)(2,1)}, bf16[1024,4608]{1,0:T(8,128)(2,1)}, bf16[1024,4608]{1,0:T(8,128)(2,1)}) custom-call(bf16[1024,1024]{1,0:T(8,128)(2,1)} %get-tuple-element.60.n2, bf16[1024,1024]{1,0:T(8,128)(2,1)} %bitcast.32, ...), custom_call_target="tpu_custom_call" | custom-call | flops 57982058496 | bytes 73400320 | tf_op jit(solution)/shard_map/pallas_call | solution.py:530
  190.0 18.1 %shard_map.326 = (bf16[1024,1024]{1,0:T(8,128)(2,1)}, f32[1024,1024]{1,0:T(8,128)}, bf16[1024,1024]{1,0:T(8,128)(2,1)}, f32[1024,1024]{1,0:T(8,128)}, f32[8,1024...) custom-call(f32[1024,1024]{1,0:T(8,128)} %get-tuple-element.56.refs_0_, ...), custom_call_target="tpu_custom_call" | custom-call | flops 4294967296 | bytes 50331648 | tf_op jit(solution)/shard_map/pallas_call | solution.py:717
  211.7 3.0 collective-permute-done.1.refs_5_
  215.3 19.5 %shard_map.327 = (bf16[1024,3072]{1,0:T(8,128)(2,1)}, f32[8,1024]{1,0:T(8,128)}, bf16[512,3072]{1,0:T(8,128)(2,1)}, bf16[512,3072]{1,0:T(8,128)(2,1)}) custom-call(f32[1024,1024]{1,0:T(8,128)} %get-tuple-element.64.refs_0_, bf16[1024,1024]{1,0:T(8,128)(2,1)} %get-tuple-element.65.refs_1_, f32[1024,3072]{1,0:T(8,128)} %get-tuple-element.58.refs_2_.refs_3_, ...), custom_call_target="tpu_custom_call" | custom-call | flops 6442450944 | bytes 33554432 | tf_op jit(solution)/shard_map/pallas_call | solution.py:796
  234.8 2.8 copy-done
  237.6 8.7 %shard_map.331.refs_12_.base_own = bf16[2304,1024]{1,0:T(8,128)(2,1)} custom-call(f32[1]{0:T(128)} %bitcast.14.refs_0_, f32[2304,1024]{1,0:T(8,128)} %refs_1_.7, f32[2304,1024]{1,0:T(8,128)} %moment.1, bf16[1024,3072]{1,0:T(8,128)(2,1)S(1)} %copy-done), custom_call_target="tpu_custom_call" | custom-call | flops 7077888 | bytes 23592960 | tf_op jit(solution)/shard_map/pallas_call | solution.py:879
  246.3 9.0 %shard_map.329.refs_10_.refs_2_ = bf16[512,4608]{1,0:T(8,128)(2,1)} custom-call(f32[1]{0:T(128)} %bitcast.14.refs_0_, f32[512,4608]{1,0:T(8,128)} %refs_1_.5, f32[512,4608]{1,0:T(8,128)} %refs_4_.5, bf16[1024,3072]{1,0:T(8,128)(2,1)S(1)} %copy-done), custom_call_target="tpu_custom_call" | custom-call | flops 7077888 | bytes 23592960 | tf_op jit(solution)/shard_map/pallas_call | solution.py:879
  255.3 8.9 %shard_map.330.refs_11_.refs_7_ = bf16[512,4608]{1,0:T(8,128)(2,1)} custom-call(f32[1]{0:T(128)} %bitcast.14.refs_0_, f32[512,4608]{1,0:T(8,128)} %refs_1_.6, f32[512,4608]{1,0:T(8,128)} %refs_9_.1, bf16[1024,3072]{1,0:T(8,128)(2,1)S(1)} %copy-done), custom_call_target="tpu_custom_call" | custom-call | flops 7077888 | bytes 23592960 | tf_op jit(solution)/shard_map/pallas_call | solution.py:879
  264.8 5.3 shard_map.332.refs_13_.refs_2_
  270.5 2.5 copy.48
  274.0 2.8 copy-done.1
  276.8 1.6 copy-done.5
  278.4 1.6 copy-done.6
  280.4 14.5 %shard_map.328 = (bf16[1024,1024]{1,0:T(8,128)(2,1)}, f32[8,1024]{1,0:T(8,128)}) custom-call(bf16[1024,3072]{1,0:T(8,128)(2,1)} %get-tuple-element.67.refs_0_.refs_3_, bf16[1024,3072]{1,0:T(8,128)(2,1)} %all-gather.8.cloned.1.call-done.w_in.refs_1_, bf16[1024,1024]{1,0:T(8,128)(2,1)} %bitcast.40, f32[1024,1024]{1,0:T(8,128)} %get-tuple-element.68.refs_3_, ...), custom_call_target="tpu_custom_call" | custom-call | flops 6442450944 | bytes 20971520 | tf_op jit(solution)/shard_map/pallas_call | solution.py:846
  296.4 333.1 %shard_map.334 = (bf16[1024,1024]{1,0:T(8,128)(2,1)}, bf16[1024,3072]{1,0:T(8,128)(2,1)}, bf16[18432,768]{1,0:T(8,128)(2,1)}, f32[8,1024]{1,0:T(8,128)}, f32[8,128]{1,0:T(8,128)}) custom-call(bf16[512,1024]{1,0:T(8,128)(2,1)} %get-tuple-element.70.refs_0_, bf16[512,1024]{1,0:T(8,128)(2,1)} %get-tuple-element.71.refs_1_, ...), custom_call_target="tpu_custom_call" | custom-call | tf_op jit(solution)/shard_map/pallas_call | solution.py:460
  637.7 1.6 copy-done.4
  639.3 4.4 shard_map.336
  643.6 12.6 %shard_map.335 = (bf16[1024,3072]{1,0:T(8,128)(2,1)}, f32[512,3072]{1,0:T(8,128)}) custom-call(s32[3]{0:T(128)S(1)} %pad_add_fusion.1.bits, f32[2]{0:T(128)S(1)} %pad_maximum_fusion.scalars, bf16[1024,3072]{1,0:T(8,128)(2,1)} %get-tuple-element.83.refs_0_.refs_1_, bf16[1024,3072]{1,0:T(8,128)(2,1)} %get-tuple-element.83.refs_0_.refs_1_, ...), custom_call_target="tpu_custom_call" | custom-call | flops 12582912 | bytes 31457280 | tf_op jit(solution)/shard_map/pallas_call | solution.py:932
  656.2 17.8 %shard_map.338 = (bf16[2,2304,1024]{2,1,0:T(8,128)(2,1)}, f32[2304,1024]{1,0:T(8,128)}) custom-call(s32[3]{0:T(128)S(1)} %pad_add_fusion.1.bits, f32[2]{0:T(128)S(1)} %pad_maximum_fusion.scalars, bf16[18432,768]{1,0:T(8,128)(2,1)} %get-tuple-element.87.refs_0_.refs_1_.refs_5_.refs_6_.own.other, ...), custom_call_target="tpu_custom_call" | custom-call | flops 18874368 | bytes 47185920 | tf_op jit(solution)/shard_map/pallas_call | solution.py:959
  674.1 32.1 %shard_map.337 = (bf16[1024,4608]{1,0:T(8,128)(2,1)}, f32[512,4608]{1,0:T(8,128)}, bf16[1024,4608]{1,0:T(8,128)(2,1)}, f32[512,4608]{1,0:T(8,128)}) custom-call(s32[3]{0:T(128)S(1)} %pad_add_fusion.1.bits, f32[2]{0:T(128)S(1)} %pad_maximum_fusion.scalars, bf16[18432,768]{1,0:T(8,128)(2,1)} %get-tuple-element.87.refs_0_.refs_1_.refs_5_.refs_6_.own.other, ...), custom_call_target="tpu_custom_call" | custom-call | flops 37748736 | bytes 94371840 | tf_op jit(solution)/shard_map/pallas_call | solution.py:932
  (91 shorter events, 18.5 us)
Async XLA Ops:
  7.2 42.9 %all-gather.10.cloned.1.call-start = ((), (), s32[]{:S(2)}) async-start(), calls=%async_computation.1 | async-start | bytes 3145728 | tf_op jit(solution)/shard_map/all_gather | solution.py:1033
  10.0 40.1 %all-gather.8.cloned.1.call-start = ((), (), s32[]{:S(2)}) async-start(), calls=%async_computation | async-start | bytes 9437184 | tf_op jit(solution)/shard_map/all_gather | solution.py:1031
  15.0 56.4 %all-gather.12.cloned.1.call-start = ((), (), s32[]{:S(2)}) async-start(), calls=%async_computation.2 | async-start | bytes 14155776 | tf_op jit(solution)/shard_map/all_gather | solution.py:1035
  21.4 72.3 %all-gather.14.cloned.1.call-start = ((), (), s32[]{:S(2)}) async-start(), calls=%async_computation.3 | async-start | bytes 14155776 | tf_op jit(solution)/shard_map/all_gather | solution.py:1036
  27.9 90.9 %all-gather.16.cloned.1.call-start = ((), (), s32[]{:S(2)}) async-start(), calls=%async_computation.4 | async-start | bytes 14155776 | tf_op jit(solution)/shard_map/all_gather | solution.py:1037
  34.7 6.6 copy-start.9
  34.7 8.0 %copy-start.13 = (f32[512]{0:T(512)S(1)}, f32[512]{0:T(512)}, u32[]{:S(2)}) copy-start(f32[512]{0:T(512)} %param.24) | copy-start | bytes 6148
  34.7 10.4 %copy-start.14 = (f32[512]{0:T(512)S(1)}, f32[512]{0:T(512)}, u32[]{:S(2)}) copy-start(f32[512]{0:T(512)} %param.28) | copy-start | bytes 6148
  34.7 12.8 %copy-start.11 = (f32[3,512]{1,0:T(4,128)S(1)}, f32[3,512]{1,0:T(4,128)}, u32[]{:S(2)}) copy-start(f32[3,512]{1,0:T(4,128)} %param.26) | copy-start | bytes 18436
  35.6 14.5 %collective-permute-start = (bf16[16,1024]{1,0:T(8,128)(2,1)S(1)}, bf16[16,1024]{1,0:T(8,128)(2,1)S(1)}, u32[]{:S(2)}, u32[]{:S(2)}) collective-permute-start(bf16[16,1024]{1,0:T(8,128)(2,1)S(1)} %slice_bitcast_fusion), channel_id=1, source_target_pairs={{0,2},{2,4},{4,6},{1,3},{3,5},{5,7},{8,10},{10,12},{12,14},{9,11},... | collective-permute-start | bytes 98312 | tf_op jit(solution)/shard_map/ppermute | solution.py:25
  50.1 0.6 copy-start.17
  208.9 5.8 collective-permute-start.1
  214.6 0.6 copy-start.8
  234.8 2.8 copy-start
  246.3 409.9 %collective-permute-start.6 = (bf16[2304,1024]{1,0:T(8,128)(2,1)}, bf16[2304,1024]{1,0:T(8,128)(2,1)}, u32[]{:S(2)}, u32[]{:S(2)}) collective-permute-start(bf16[2304,1024]{1,0:T(8,128)(2,1)} %shard_map.331.refs_12_.base_own), channel_id=1, source_target_pairs={{0,1},{1,0},{2,3},{3,2},{4,5},{5,4},{6,7},{7,6},{8,9},{9,8},{10,11... | collective-permute-start | bytes 14155784 | tf_op jit(solution)/shard_map/ppermute | solution.py:552
  246.3 18.5 %slice-start = ((s8[6291456]{0:T(1024)(128)(4,1)}), s8[4194304]{0:T(1024)(128)(4,1)S(1)}, s32[]{:S(2)}) async-start(s8[6291456]{0:T(1024)(128)(4,1)} %bitcast.30), calls=%async_computation.5 | async-start | bytes 8388608
  255.3 9.5 %slice-start.1 = ((s8[6291456]{0:T(1024)(128)(4,1)}), s8[2097152]{0:T(1024)(128)(4,1)S(1)}, s32[]{:S(2)}) async-start(s8[6291456]{0:T(1024)(128)(4,1)} %bitcast.30), calls=%async_computation.6 | async-start | bytes 4194304
  264.2 6.3 copy-start.7
  264.2 409.8 %collective-permute-start.4 = (bf16[512,4608]{1,0:T(8,128)(2,1)}, bf16[512,4608]{1,0:T(8,128)(2,1)}, u32[]{:S(2)}, u32[]{:S(2)}) collective-permute-start(bf16[512,4608]{1,0:T(8,128)(2,1)} %shard_map.329.refs_10_.refs_2_), channel_id=1, source_target_pairs={{0,1},{1,0},{2,3},{3,2},{4,5},{5,4},{6,7},{7,6},{8,9},{9,8},{10,11... | collective-permute-start | bytes 14155784 | tf_op jit(solution)/shard_map/ppermute | solution.py:552
  264.7 409.3 %collective-permute-start.5 = (bf16[512,4608]{1,0:T(8,128)(2,1)}, bf16[512,4608]{1,0:T(8,128)(2,1)}, u32[]{:S(2)}, u32[]{:S(2)}) collective-permute-start(bf16[512,4608]{1,0:T(8,128)(2,1)} %shard_map.330.refs_11_.refs_7_), channel_id=1, source_target_pairs={{0,1},{1,0},{2,3},{3,2},{4,5},{5,4},{6,7},{7,6},{8,9},{9,8},{10,11... | collective-permute-start | bytes 14155784 | tf_op jit(solution)/shard_map/ppermute | solution.py:552
  270.0 373.6 %collective-permute-start.2 = (bf16[512,3072]{1,0:T(8,128)(2,1)}, bf16[512,3072]{1,0:T(8,128)(2,1)}, u32[]{:S(2)}, u32[]{:S(2)}) collective-permute-start(bf16[512,3072]{1,0:T(8,128)(2,1)} %shard_map.332.refs_13_.refs_2_), channel_id=1, source_target_pairs={{0,1},{1,0},{2,3},{3,2},{4,5},{5,4},{6,7},{7,6},{8,9},{9,8},{10,11... | collective-permute-start | bytes 9437192 | tf_op jit(solution)/shard_map/ppermute | solution.py:552
  274.0 2.8 copy-start.1
  276.8 1.6 copy-start.5
  278.4 1.6 copy-start.6
  280.3 16.1 %copy-start.2 = (bf16[512,1024]{1,0:T(8,128)(2,1)}, bf16[512,1024]{1,0:T(8,128)(2,1)S(1)}, u32[]{:S(2)}) copy-start(bf16[512,1024]{1,0:T(8,128)(2,1)S(1)} %shard_map.333.refs_14_.refs_2_) | copy-start | bytes 3145732
  280.3 356.2 %collective-permute-start.3 = (bf16[512,1024]{1,0:T(8,128)(2,1)S(1)}, bf16[512,1024]{1,0:T(8,128)(2,1)}, u32[]{:S(2)}, u32[]{:S(2)}) collective-permute-start(bf16[512,1024]{1,0:T(8,128)(2,1)S(1)} %shard_map.333.refs_14_.refs_2_), channel_id=1, source_target_pairs={{0,1},{1,0},{2,3},{3,2},{4,5},{5,4},{6,7},{7,6},{8,9},{9,8},{10,11... | collective-permute-start | bytes 3145736 | tf_op jit(solution)/shard_map/ppermute | solution.py:552
  280.4 14.5 %copy-start.12 = (f32[8,1024]{1,0:T(8,128)S(1)}, f32[8,1024]{1,0:T(8,128)}, u32[]{:S(2)}) copy-start(f32[8,1024]{1,0:T(8,128)} %get-tuple-element.79) | copy-start | bytes 98308
  296.4 338.1 %copy-start.15 = (f32[512]{0:T(512)S(1)}, f32[512]{0:T(512)}, u32[]{:S(2)}) copy-start(f32[512]{0:T(512)} %param.36) | copy-start | bytes 6148
  296.4 338.1 %copy-start.16 = (f32[512]{0:T(512)S(1)}, f32[512]{0:T(512)}, u32[]{:S(2)}) copy-start(f32[512]{0:T(512)} %param.32) | copy-start | bytes 6148
  296.4 338.7 %copy-start.10 = (f32[3,512]{1,0:T(4,128)S(1)}, f32[3,512]{1,0:T(4,128)}, u32[]{:S(2)}) copy-start(f32[3,512]{1,0:T(4,128)} %param.34) | copy-start | bytes 18436
  636.4 1.2 copy-start.3
  637.7 1.6 copy-start.4
Sparse Core Ops, SparseCore 0:
  10.1 13.2 all-gather.9
  25.6 17.9 all-gather.7
  45.7 23.0 all-gather.11
  70.7 23.0 all-gather.13
  95.7 23.0 all-gather.15

commit v3 on v2

--- a/solution.py
+++ b/solution.py
@@ -496,9 +496,10 @@
     return outs[: len(wholes)], outs[-2], outs[-1]
 
 
-def feed_kernel(step, n2, e, wg, wu, wd, out, back, act, gate_back, up_back):
+def feed_kernel(step, n2, e, wg, wu, wd, out, back, act, gate_back, up_back, et):
     @pl.when(pl.program_id(0) == 0)
     def _():
+        et[...] = e[...].T
         out[...] = jnp.zeros_like(out)
         back[...] = jnp.zeros_like(back)
 
@@ -524,6 +525,7 @@
 
 def feed(n2, e, gate_matrix, up_matrix, down_matrix, tiles):
     rows, width = n2.shape
+    assert rows == width
     cols = gate_matrix.shape[1] // tiles
     whole = pl.BlockSpec((rows, width), lambda i: (0, 0), pipeline_mode=pl.Buffered(1))
     tile = pl.BlockSpec((rows, cols), lambda i: (0, i))
@@ -533,9 +535,10 @@
         in_specs=[whole, whole]
         + [pl.BlockSpec((width, cols), lambda i: (0, i))] * 2
         + [pl.BlockSpec((cols, width), lambda i: (i, 0))],
-        out_specs=[whole, whole, tile, tile, tile],
+        out_specs=[whole, whole, tile, tile, tile, whole],
         out_shape=[jax.ShapeDtypeStruct((rows, width), jnp.float32)] * 2
-        + [jax.ShapeDtypeStruct((rows, tiles * cols), jnp.bfloat16)] * 3,
+        + [jax.ShapeDtypeStruct((rows, tiles * cols), jnp.bfloat16)] * 3
+        + [jax.ShapeDtypeStruct((width, rows), jnp.bfloat16)],
         cost_estimate=pl.CostEstimate(
             flops=12 * rows * width * cols * tiles,
             bytes_accessed=70 * 1024 * 1024,
@@ -569,74 +572,278 @@
     return moved
 
 
+STEPS = 4
+
+
 def mixer_kernel(
-    x_ref, edge_ref, masks, gain_one, gain_two, taps, w_in, w_out, proj, conv, hid, n1t, zt, n2, n2t, carry
+    x_ref,
+    x_all,
+    masks,
+    pack,
+    in_master,
+    out_master,
+    gate_master,
+    up_master,
+    down_master,
+    proj,
+    conv,
+    hid,
+    n1t,
+    zt,
+    n2,
+    n2t,
+    gains,
+    in_whole,
+    out_whole,
+    gate_whole,
+    up_whole,
+    down_whole,
+    carry,
+    edge,
+    pack_in,
+    w_in,
+    w_out,
+    in_stage,
+    out_stage,
+    gate_stage,
+    up_stage,
+    down_stage,
+    gate_low,
+    up_low,
+    down_low,
+    load_sem,
+    send,
+    recv,
+    keep_sem,
+    part_load,
+    part_send,
+    part_recv,
+    part_keep,
 ):
     width = x_ref.shape[1]
+    half = width // 2
     low = jnp.bfloat16
-
-    def project(values, first, count):
+    step = pl.program_id(0)
+    group = lax.axis_index("dp")
+    place = lax.axis_index("seq")
+    core = lax.axis_index("shard")
+    places = lax.axis_size("seq")
+    sibling = (group, place, 1 - core)
+    after = (group, lax.rem(place + 1, places), core)
+    before = (group, lax.rem(place + places - 1, places), core)
+
+    def remote(source, target, k, device):
+        return pltpu.make_async_remote_copy(
+            src_ref=source,
+            dst_ref=target,
+            send_sem=send.at[k],
+            recv_sem=recv.at[k],
+            device_id=device,
+            device_id_type=MESH,
+        )
+
+    def own_rows(rows, start=0, count=None):
+        return pl.ds(pl.multiple_of(core * rows + start, 16), rows if count is None else count)
+
+    def cast(target, target_row, source, source_row, rows):
+        block = 16
+
+        def body(i, carry_):
+            put = pl.ds(pl.multiple_of(target_row + i * block, block), block)
+            get = pl.ds(pl.multiple_of(source_row + i * block, block), block)
+            target[put, :] = source[get, :].astype(low)
+            return carry_
+
+        lax.fori_loop(0, rows // block, body, 0)
+
+    stages = (gate_stage, up_stage, down_stage)
+    masters = (gate_master, up_master, down_master)
+    wholes = (gate_whole, up_whole, down_whole)
+    lows = (gate_low, up_low, down_low)
+
+    def part_in(m, i):
+        rows = stages[m].shape[0]
+        return pltpu.make_async_copy(
+            masters[m].at[pl.ds(pl.multiple_of(i * rows, 16), rows)], stages[m], part_load.at[m]
+        )
+
+    def part_rows(m, i):
+        rows = stages[m].shape[0]
+        return pl.ds(pl.multiple_of(core * (STEPS * rows) + i * rows, 16), rows)
+
+    def part_out(m, i):
+        slot = lax.rem(i, 2)
+        return pltpu.make_async_remote_copy(
+            src_ref=lows[m].at[slot],
+            dst_ref=wholes[m].at[part_rows(m, i)],
+            send_sem=part_send.at[i, m],
+            recv_sem=part_recv.at[i, m],
+            device_id=sibling,
+            device_id_type=MESH,
+        )
+
+    def part_own(m, i):
+        slot = lax.rem(i, 2)
+        return pltpu.make_async_copy(
+            lows[m].at[slot], wholes[m].at[part_rows(m, i)], part_keep.at[i, m]
+        )
+
+    quarter = half // 2
+    copies = []
+    for k in range(2):
+        rows = own_rows(half, k * quarter, quarter)
+        copies.append(remote(w_in.at[rows], w_in.at[rows], k, sibling))
+    rows = own_rows(half)
+    copies.append(remote(w_out.at[rows], w_out.at[rows], 2, sibling))
+    copies.append(remote(pack, pack_in, 3, sibling))
+    to_after = remote(x_all.at[pl.ds(x_all.shape[0] - 16, 16)], edge, 4, after)
+    in_loads = [
+        pltpu.make_async_copy(
+            in_master.at[pl.ds(k * quarter, quarter)],
+            in_stage.at[pl.ds(k * quarter, quarter)],
+            load_sem.at[k],
+        )
+        for k in range(2)
+    ]
+    out_load = pltpu.make_async_copy(out_master, out_stage, load_sem.at[2])
+    keeps = [
+        pltpu.make_async_copy(w_in, in_whole, keep_sem.at[0]),
+        pltpu.make_async_copy(w_out, out_whole, keep_sem.at[1]),
+    ]
+
+    def project(values, first, count=1):
         return kernel_dot(values, w_in[:, first * width : (first + count) * width])
 
     def normed(values):
-        return (values * scale_of(values) * gain_one[...]).astype(low)
-
-    @pl.when(pl.program_id(0) == 0)
+        return (values * scale_of(values) * gains[0:1, :]).astype(low)
+
+    @pl.when(step == 0)
     def _():
-        edge = normed(edge_ref[...].astype(jnp.float32))
-        mixed = project(edge, 0, 1) * project(edge, 2, 1)
+        for load in (*in_loads, out_load):
+            load.start()
+        for m in range(3):
+            part_in(m, 0).start()
+        barrier = pltpu.get_barrier_semaphore()
+        for device in (sibling, after, before):
+            pl.semaphore_signal(barrier, inc=1, device_id=device, device_id_type=MESH)
+        pl.semaphore_wait(barrier, 3)
+        copies[3].start()
+
+        @pl.when(place < places - 1)
+        def _():
+            to_after.start()
+
+        for k in range(2):
+            in_loads[k].wait()
+            cast(w_in, core * half + k * quarter, in_stage, k * quarter, quarter)
+            copies[k].start()
+        out_load.wait()
+        cast(w_out, core * half, out_stage, 0, half)
+        copies[2].start()
+
+        @pl.when(place == 0)
+        def _():
+            edge[...] = jnp.zeros_like(edge)
+
+        @pl.when(place > 0)
+        def _():
+            to_after.wait_recv()
+
+        @pl.when(place < places - 1)
+        def _():
+            to_after.wait_send()
+
+        for copy in copies:
+            copy.wait()
+        gains[:, pl.ds(pl.multiple_of(core * half, half), half)] = pack[...]
+        gains[:, pl.ds(pl.multiple_of((1 - core) * half, half), half)] = pack_in[...]
+        for copy in keeps:
+            copy.start()
+        rows = normed(edge[...].astype(jnp.float32))
+        mixed = project(rows, 0) * project(rows, 2)
         carry[...] = mixed[8:, :]
 
-    x = x_ref[...].astype(jnp.float32)
-    first = normed(x)
-    n1t[...] = first.T
-    gate_b, gate_c, values = project(first, 0, 1), project(first, 1, 1), project(first, 2, 1)
-    proj[:, :width] = gate_b
-    proj[:, width : 2 * width] = gate_c
-    proj[:, 2 * width :] = values
-    mixed = gate_b * values
-    edge = carry[...]
-    convolved = (
-        taps[2:3, :] * mixed
-        + taps[1:2, :] * masks[:, 0:1] * shifted(mixed, edge, -1)
-        + taps[0:1, :] * masks[:, 1:2] * shifted(mixed, edge, -2)
-    )
-    carry[...] = mixed[mixed.shape[0] - 8 :, :]
-    conv[...] = convolved
-    mixer_out = (gate_c * convolved).astype(low)
-    zt[...] = mixer_out.T
-    hidden = x + kernel_dot(mixer_out, w_out[...])
-    hid[...] = hidden
-    second = (hidden * scale_of(hidden) * gain_two[...]).astype(low)
-    n2[...] = second
-    n2t[...] = second.T
+    @pl.when(step > 0)
+    def _():
+        i = step - 1
+
+        @pl.when(i >= 2)
+        def _():
+            for m in range(3):
+                part_out(m, i - 2).wait_send()
+                part_own(m, i - 2).wait()
+
+        for m in range(3):
+            part_in(m, i).wait()
+            cast(lows[m].at[lax.rem(i, 2)], 0, stages[m], 0, stages[m].shape[0])
+            part_out(m, i).start()
+            part_own(m, i).start()
+
+        @pl.when(i + 1 < STEPS)
+        def _():
+            for m in range(3):
+                part_in(m, i + 1).start()
+
+        x = x_ref[...].astype(jnp.float32)
+        first = normed(x)
+        n1t[...] = first.T
+        gate_b, gate_c, values = project(first, 0), project(first, 1), project(first, 2)
+        proj[:, :width] = gate_b
+        proj[:, width : 2 * width] = gate_c
+        proj[:, 2 * width :] = values
+        mixed = gate_b * values
+        beside = carry[...]
+        convolved = (
+            gains[4:5, :] * mixed
+            + gains[3:4, :] * masks[:, 0:1] * shifted(mixed, beside, -1)
+            + gains[2:3, :] * masks[:, 1:2] * shifted(mixed, beside, -2)
+        )
+        carry[...] = mixed[mixed.shape[0] - 8 :, :]
+        conv[...] = convolved
+        mixer_out = (gate_c * convolved).astype(low)
+        zt[...] = mixer_out.T
+        hidden = x + kernel_dot(mixer_out, w_out[...])
+        hid[...] = hidden
+        second = (hidden * scale_of(hidden) * gains[1:2, :]).astype(low)
+        n2[...] = second
+        n2t[...] = second.T
+
+    @pl.when(step == STEPS)
+    def _():
+        for copy in keeps:
+            copy.wait()
+        for i in range(STEPS):
+            for m in range(3):
+                if i >= STEPS - 2:
+                    part_out(m, i).wait_send()
+                    part_own(m, i).wait()
+                part_out(m, i).wait_recv()
 
 
 def resident(shape):
     return pl.BlockSpec(shape, lambda i: (0,) * len(shape), pipeline_mode=pl.Buffered(1))
 
 
-def mixer(x, edge, masks, gain_one, gain_two, taps, w_in, w_out):
+def mixer(x, masks, pack, masters):
     rows, width = x.shape
-    step = rows // 4
-    tile = lambda cols: pl.BlockSpec((step, cols), lambda i: (i, 0))
-    turned = pl.BlockSpec((width, step), lambda i: (0, i))
+    step = rows // STEPS
+    at = lambda i: jnp.maximum(i - 1, 0)
+    tile = lambda cols: pl.BlockSpec((step, cols), lambda i: (at(i), 0))
+    turned = pl.BlockSpec((width, step), lambda i: (0, at(i)))
     low, full = jnp.bfloat16, jnp.float32
     shape = jax.ShapeDtypeStruct
+    in_master, out_master = masters[:2]
+    large = masters[2:]
+    whole = [shape((2 * m.shape[0], m.shape[1]), low) for m in masters]
+    parts = [(m.shape[0] // STEPS, m.shape[1]) for m in large]
+    semaphore = pltpu.SemaphoreType.DMA
     return pl.pallas_call(
         mixer_kernel,
-        grid=(4,),
-        in_specs=[
-            tile(width),
-            resident(edge.shape),
-            tile(masks.shape[1]),
-            resident(gain_one.shape),
-            resident(gain_two.shape),
-            resident(taps.shape),
-            resident(w_in.shape),
-            resident(w_out.shape),
-        ],
-        out_specs=[tile(3 * width), tile(width), tile(width), turned, turned, tile(width), turned],
+        grid=(STEPS + 1,),
+        in_specs=[tile(width), ANY, tile(masks.shape[1]), resident(pack.shape)] + [ANY] * 5,
+        out_specs=[tile(3 * width), tile(width), tile(width), turned, turned, tile(width), turned]
+        + [resident((8, width))]
+        + [ANY] * 5,
         out_shape=[
             shape((rows, 3 * width), full),
             shape((rows, width), full),
@@ -645,13 +852,34 @@
             shape((width, rows), low),
             shape((rows, width), low),
             shape((width, rows), low),
+            shape((8, width), full),
+        ]
+        + whole,
+        scratch_shapes=[
+            pltpu.VMEM((8, width), full),
+            pltpu.VMEM((16, width), low),
+            pltpu.VMEM(pack.shape, full),
+            pltpu.VMEM(whole[0].shape, low),
+            pltpu.VMEM(whole[1].shape, low),
+            pltpu.VMEM(in_master.shape, full),
+            pltpu.VMEM(out_master.shape, full),
+        ]
+        + [pltpu.VMEM(part, full) for part in parts]
+        + [pltpu.VMEM((2, *part), low) for part in parts]
+        + [
+            semaphore((3,)),
+            semaphore((5,)),
+            semaphore((5,)),
+            semaphore((2,)),
+            semaphore((3,)),
+            semaphore((STEPS, 3)),
+            semaphore((STEPS, 3)),
+            semaphore((STEPS, 3)),
         ],
-        scratch_shapes=[pltpu.VMEM((8, width), full)],
-        compiler_params=pltpu.CompilerParams(vmem_limit_bytes=56 * 1024 * 1024),
-        cost_estimate=pl.CostEstimate(
-            flops=8 * rows * width * width, bytes_accessed=48 * rows * width, transcendentals=0
+        compiler_params=pltpu.CompilerParams(
+            collective_id=1, has_side_effects=True, vmem_limit_bytes=60 * 1024 * 1024
         ),
-    )(x, edge, masks, gain_one, gain_two, taps, w_in, w_out)
+    )(x, x, masks, pack, *masters)
 
 
 def out_back_kernel(parts, *refs):
@@ -1026,24 +1254,6 @@
         moment_up,
         moment_down,
     )
-    whole = (
-        lax.all_gather(norm_one.astype(jnp.bfloat16), "shard", axis=0, tiled=True),
-        lax.all_gather(in_weight.astype(jnp.bfloat16), "shard", axis=0, tiled=True),
-        lax.all_gather(conv_weight.astype(jnp.bfloat16), "shard", axis=1, tiled=True),
-        lax.all_gather(out_weight.astype(jnp.bfloat16), "shard", axis=0, tiled=True),
-        lax.all_gather(norm_two.astype(jnp.bfloat16), "shard", axis=0, tiled=True),
-        lax.all_gather(gate_weight.astype(jnp.bfloat16), "shard", axis=0, tiled=True),
-        lax.all_gather(up_weight.astype(jnp.bfloat16), "shard", axis=0, tiled=True),
-        lax.all_gather(down_weight.astype(jnp.bfloat16), "shard", axis=0, tiled=True),
-    )
-    gain_one = whole[0].astype(jnp.float32)
-    in_matrix = whole[1]
-    conv_taps = whole[2].astype(jnp.float32)
-    out_matrix = whole[3]
-    gain_two = whole[4].astype(jnp.float32)
-    gate_matrix = whole[5]
-    up_matrix = whole[6]
-    down_matrix = whole[7]
     seq_count, span, model_width = tokens.shape
     row_count = seq_count * span
     x = tokens.reshape(row_count, model_width)
@@ -1062,13 +1272,27 @@
         ],
         1,
     ).astype(jnp.float32)
-    edge = from_behind(x[row_count - 16 :, :], "seq", 1)
-    gain_one_row, gain_two_row = gain_one[None], gain_two[None]
-    proj, convolved, hidden, n1t, zt, n2, n2t = mixer(
-        x, edge, masks, gain_one_row, gain_two_row, conv_taps, in_matrix, out_matrix
-    )
-    et = e.T
-    feed_out, feed_back, act, gate_back, up_back = feed(
+    pack = jnp.concatenate(
+        [norm_one[None], norm_two[None], conv_weight, jnp.zeros((3, norm_one.size))], 0
+    )
+    pack = pack.astype(jnp.bfloat16).astype(jnp.float32)
+    (
+        proj,
+        convolved,
+        hidden,
+        n1t,
+        zt,
+        n2,
+        n2t,
+        gains,
+        in_matrix,
+        out_matrix,
+        gate_matrix,
+        up_matrix,
+        down_matrix,
+    ) = mixer(x, masks, pack, (in_weight, out_weight, gate_weight, up_weight, down_weight))
+    gain_one_row, gain_two_row, conv_taps = gains[0:1], gains[1:2], gains[2:5]
+    feed_out, feed_back, act, gate_back, up_back, et = feed(
         n2, e, gate_matrix, up_matrix, down_matrix, 2 * FEED_PARTS
     )
     block_out, hidden_grad, gc_grad, conv_out_grad, gain_two_grad, out_keep, out_give = out_back(
@@ -1115,7 +1339,7 @@
         small,
         [base[place] for place in (5, 6, 7, 1, 3)],
     )
-    param_count = sum((member.size for member in whole))
+    param_count = 2 * sum((member.size for member in masters))
     clip_level = CLIP_RATIO * math.sqrt(param_count)
     grad_norm = jnp.sqrt(jnp.sum(squares) + jnp.sum(small_sum * small_sum))
     clip_factor = clip_level / jnp.maximum(grad_norm, clip_level)

time: 718 us -> 647 us (0.901)
  waiting for transfers between devices: 50.5 us -> 2.44 us
  other arithmetic: 36.3 us -> 10.1 us
  Pallas kernels: 576 us -> 600 us
  between operations: 18 us -> 5.08 us
    all_gather x5 -> x0, waiting for transfers between devices: 47.4 us -> none  [the longest x1 25 us: local_fast(): lax.all_gather(down_weight.astype(jnp.bfloat16), 'shard', axis=0, tiled=T...]
    convert_element_type x9 -> x1, other arithmetic: 27.8 us -> 0.68 us  [local_fast(): pack = pack.astype(jnp.bfloat16).astype(jnp.float32)]
    pallas_call x1, Pallas kernels: 20.7 us -> 42.8 us  [mixer(): pl.pallas_call(mixer_kernel, grid=(STEPS + 1,), in_specs=[tile(width), AN...]
    unnamed x43 -> x30, local copies, waits for them, and re-layouts: 15.4 us -> 12.2 us
  transfers between devices with their start and end apart: 12 -> 6, of which waited for: 3 -> 1; matrix products, arithmetic and copies ran while one was open for 5% -> 1% of each run, Pallas kernels for 60% -> 64%
where the time goes in v3:
time: 647 us; the launch traced here: 638 us
  Pallas kernels  600 us (93%)
  local copies, waits for them, and re-layouts  17.8 us (3%)
  other arithmetic  10.1 us (2%)
    pallas_call x1, Pallas kernels, finish(): pl.pallas_call(functools.partial(finish_kernel, tuple(chunks), parts, len...  333 us
    pallas_call x1, Pallas kernels, feed(): pl.pallas_call(functools.partial(feed_kernel, rows // 2), grid=(tiles,),...  72.4 us
    pallas_call x3, Pallas kernels, update_rows(): pl.pallas_call(update_kernel, grid_spec=pltpu.PrefetchScalarGridSpec(num_...  49.1 us
    pallas_call x1, Pallas kernels, mixer(): pl.pallas_call(mixer_kernel, grid=(STEPS + 1,), in_specs=[tile(width), AN...  42.8 us
    pallas_call x5, Pallas kernels, base_of(): pl.pallas_call(skip_last(base_kernel, 3, len(order)), grid=(4,), in_specs...  32.3 us
    pallas_call x1, Pallas kernels, conv_back(): pl.pallas_call(skip_last(conv_back_kernel, 8, len(order)), grid=(4,), in_...  19.5 us
    pallas_call x1, Pallas kernels, out_back(): pl.pallas_call(skip_last(functools.partial(out_back_kernel, len(outs)), i...  18.1 us
    pallas_call x1, Pallas kernels, update_down(): pl.pallas_call(update_down_kernel, grid_spec=pltpu.PrefetchScalarGridSpec...  17.8 us
  transfers between devices with their start and end apart: 6, of which 1 were waited for; matrix products, arithmetic and copies ran while one was open for 1% of the time, Pallas kernels for 64%

profile of v3, /device:TPU:0, one launch (start us, length us, event | category | flops | bytes accessed | tf_op | source)
XLA Modules:
  0.0 637.8 jit_solution(5144796948566550452)
XLA Ops:
  0.7 0.8 concatenate.10
  2.0 0.8 convert_element_type.10.masks.refs_4_
  5.7 42.8 %shard_map.324 = (f32[1024,3072]{1,0:T(8,128)}, f32[1024,1024]{1,0:T(8,128)}, f32[1024,1024]{1,0:T(8,128)}, bf16[1024,1024]{1,0:T(8,128)(2,1)}, bf16[1024,1024]{...) custom-call(bf16[1024,1024]{1,0:T(8,128)(2,1)} %bitcast.23, ...), custom_call_target="tpu_custom_call" | custom-call | tf_op jit(solution)/shard_map/pallas_call | solution.py:840
  48.5 1.4 fusion.1
  49.9 72.4 %shard_map.325 = (f32[1024,1024]{1,0:T(8,128)}, f32[1024,1024]{1,0:T(8,128)}, bf16[1024,4608]{1,0:T(8,128)(2,1)}, bf16[1024,4608]{1,0:T(8,128)(2,1)}, bf16[1024,...) custom-call(bf16[1024,1024]{1,0:T(8,128)(2,1)} %get-tuple-element.69.n2, bf16[1024,1024]{1,0:T(8,128)(2,1)} %bitcast.26, ...), custom_call_target="tpu_custom_call" | custom-call | flops 57982058496 | bytes 73400320 | tf_op jit(solution)/shard_map/pallas_call | solution.py:532
  122.3 18.1 %shard_map.326 = (bf16[1024,1024]{1,0:T(8,128)(2,1)}, f32[1024,1024]{1,0:T(8,128)}, bf16[1024,1024]{1,0:T(8,128)(2,1)}, f32[1024,1024]{1,0:T(8,128)}, f32[8,1024...) custom-call(f32[1024,1024]{1,0:T(8,128)} %get-tuple-element.63.refs_0_, ...), custom_call_target="tpu_custom_call" | custom-call | flops 4294967296 | bytes 50331648 | tf_op jit(solution)/shard_map/pallas_call | solution.py:945
  140.4 0.8 slice.31
  141.2 1.5 collective-permute-start
  144.6 2.4 collective-permute-done.refs_5_
  147.6 19.5 %shard_map.327 = (bf16[1024,3072]{1,0:T(8,128)(2,1)}, f32[8,1024]{1,0:T(8,128)}, bf16[512,3072]{1,0:T(8,128)(2,1)}, bf16[512,3072]{1,0:T(8,128)(2,1)}) custom-call(f32[1024,1024]{1,0:T(8,128)} %get-tuple-element.76.refs_0_, bf16[1024,1024]{1,0:T(8,128)(2,1)} %get-tuple-element.77.refs_1_, f32[1024,3072]{1,0:T(8,128)} %get-tuple-element.65.refs_2_.refs_3_, ...), custom_call_target="tpu_custom_call" | custom-call | flops 6442450944 | bytes 33554432 | tf_op jit(solution)/shard_map/pallas_call | solution.py:1024
  167.2 2.8 copy-done
  169.9 8.7 %shard_map.331.refs_12_.base_own = bf16[2304,1024]{1,0:T(8,128)(2,1)} custom-call(f32[1]{0:T(128)} %bitcast.8.refs_0_, f32[2304,1024]{1,0:T(8,128)} %refs_1_.7, f32[2304,1024]{1,0:T(8,128)} %moment.1, bf16[1024,3072]{1,0:T(8,128)(2,1)S(1)} %copy-done), custom_call_target="tpu_custom_call" | custom-call | flops 7077888 | bytes 23592960 | tf_op jit(solution)/shard_map/pallas_call | solution.py:1107
  178.7 8.9 %shard_map.329.refs_10_.refs_2_ = bf16[512,4608]{1,0:T(8,128)(2,1)} custom-call(f32[1]{0:T(128)} %bitcast.8.refs_0_, f32[512,4608]{1,0:T(8,128)} %refs_1_.5, f32[512,4608]{1,0:T(8,128)} %refs_4_.5, bf16[1024,3072]{1,0:T(8,128)(2,1)S(1)} %copy-done), custom_call_target="tpu_custom_call" | custom-call | flops 7077888 | bytes 23592960 | tf_op jit(solution)/shard_map/pallas_call | solution.py:1107
  187.6 8.9 %shard_map.330.refs_11_.refs_7_ = bf16[512,4608]{1,0:T(8,128)(2,1)} custom-call(f32[1]{0:T(128)} %bitcast.8.refs_0_, f32[512,4608]{1,0:T(8,128)} %refs_1_.6, f32[512,4608]{1,0:T(8,128)} %refs_9_.1, bf16[1024,3072]{1,0:T(8,128)(2,1)S(1)} %copy-done), custom_call_target="tpu_custom_call" | custom-call | flops 7077888 | bytes 23592960 | tf_op jit(solution)/shard_map/pallas_call | solution.py:1107
  197.1 5.2 shard_map.332.refs_13_.refs_2_
  202.8 0.8 slice.36
  203.7 2.8 copy-done.1
  206.5 1.6 copy-done.5
  208.1 1.6 copy-done.6
  210.2 14.5 %shard_map.328 = (bf16[1024,1024]{1,0:T(8,128)(2,1)}, f32[8,1024]{1,0:T(8,128)}) custom-call(bf16[1024,3072]{1,0:T(8,128)(2,1)} %get-tuple-element.79.refs_0_.refs_3_, bf16[1024,3072]{1,0:T(8,128)(2,1)} %get-tuple-element.80.refs_1_, bf16[1024,1024]{1,0:T(8,128)(2,1)} %bitcast.25, f32[1024,1024]{1,0:T(8,128)} %get-tuple-element.81.refs_3_, ...), custom_call_target="tpu_custom_call" | custom-call | flops 6442450944 | bytes 20971520 | tf_op jit(solution)/shard_map/pallas_call | solution.py:1074
  224.8 0.8 slice.34
  226.2 333.2 %shard_map.334 = (bf16[1024,1024]{1,0:T(8,128)(2,1)}, bf16[1024,3072]{1,0:T(8,128)(2,1)}, bf16[18432,768]{1,0:T(8,128)(2,1)}, f32[8,1024]{1,0:T(8,128)}, f32[8,128]{1,0:T(8,128)}) custom-call(bf16[512,1024]{1,0:T(8,128)(2,1)} %get-tuple-element.83.refs_0_, bf16[512,1024]{1,0:T(8,128)(2,1)} %get-tuple-element.84.refs_1_, ...), custom_call_target="tpu_custom_call" | custom-call | tf_op jit(solution)/shard_map/pallas_call | solution.py:460
  559.5 1.3 reduce_sum.18
  560.8 1.4 multiply_reduce_fusion
  563.6 0.9 dynamic-slice_multiply_fusion.1
  565.1 1.4 fusion
  566.5 1.2 copy-done.3
  567.7 1.6 copy-done.4
  569.3 4.4 shard_map.336
  573.6 12.6 %shard_map.335 = (bf16[1024,3072]{1,0:T(8,128)(2,1)}, f32[512,3072]{1,0:T(8,128)}) custom-call(s32[3]{0:T(128)S(1)} %pad_add_fusion.1.bits, f32[2]{0:T(128)S(1)} %pad_maximum_fusion.scalars, bf16[1024,3072]{1,0:T(8,128)(2,1)} %get-tuple-element.97.refs_0_.refs_1_, bf16[1024,3072]{1,0:T(8,128)(2,1)} %get-tuple-element.97.refs_0_.refs_1_, ...), custom_call_target="tpu_custom_call" | custom-call | flops 12582912 | bytes 31457280 | tf_op jit(solution)/shard_map/pallas_call | solution.py:1160
  586.2 17.8 %shard_map.338 = (bf16[2,2304,1024]{2,1,0:T(8,128)(2,1)}, f32[2304,1024]{1,0:T(8,128)}) custom-call(s32[3]{0:T(128)S(1)} %pad_add_fusion.1.bits, f32[2]{0:T(128)S(1)} %pad_maximum_fusion.scalars, bf16[18432,768]{1,0:T(8,128)(2,1)} %get-tuple-element.101.refs_0_.refs_1_.refs_5_.refs_6_.own.other, ...), custom_call_target="tpu_custom_call" | custom-call | flops 18874368 | bytes 47185920 | tf_op jit(solution)/shard_map/pallas_call | solution.py:1187
  604.1 32.2 %shard_map.337 = (bf16[1024,4608]{1,0:T(8,128)(2,1)}, f32[512,4608]{1,0:T(8,128)}, bf16[1024,4608]{1,0:T(8,128)(2,1)}, f32[512,4608]{1,0:T(8,128)}) custom-call(s32[3]{0:T(128)S(1)} %pad_add_fusion.1.bits, f32[2]{0:T(128)S(1)} %pad_maximum_fusion.scalars, bf16[18432,768]{1,0:T(8,128)(2,1)} %get-tuple-element.101.refs_0_.refs_1_.refs_5_.refs_6_.own.other, ...), custom_call_target="tpu_custom_call" | custom-call | flops 37748736 | bytes 94371840 | tf_op jit(solution)/shard_map/pallas_call | solution.py:1160
  (56 shorter events, 7.6 us)
Async XLA Ops:
  122.3 20.4 %copy-start.8 = (f32[8,1024]{1,0:T(8,128)S(1)}, f32[8,1024]{1,0:T(8,128)}, u32[]{:S(2)}) copy-start(f32[8,1024]{1,0:T(8,128)} %get-tuple-element.66) | copy-start | bytes 98308
  141.2 5.8 collective-permute-start
  147.0 0.6 copy-start.7
  167.1 2.8 copy-start
  178.7 407.5 %collective-permute-start.5 = (bf16[2304,1024]{1,0:T(8,128)(2,1)}, bf16[2304,1024]{1,0:T(8,128)(2,1)}, u32[]{:S(2)}, u32[]{:S(2)}) collective-permute-start(bf16[2304,1024]{1,0:T(8,128)(2,1)} %shard_map.331.refs_12_.base_own), channel_id=1, source_target_pairs={{0,1},{1,0},{2,3},{3,2},{4,5},{5,4},{6,7},{7,6},{8,9},{9,8},{10,11... | collective-permute-start | bytes 14155784 | tf_op jit(solution)/shard_map/ppermute | solution.py:555
  178.7 18.4 %slice-start = ((s8[6291456]{0:T(1024)(128)(4,1)}), s8[4194304]{0:T(1024)(128)(4,1)S(1)}, s32[]{:S(2)}) async-start(s8[6291456]{0:T(1024)(128)(4,1)} %bitcast.21), calls=%async_computation | async-start | bytes 8388608
  187.6 9.4 %slice-start.1 = ((s8[6291456]{0:T(1024)(128)(4,1)}), s8[2097152]{0:T(1024)(128)(4,1)S(1)}, s32[]{:S(2)}) async-start(s8[6291456]{0:T(1024)(128)(4,1)} %bitcast.21), calls=%async_computation.1 | async-start | bytes 4194304
  196.5 407.5 %collective-permute-start.3 = (bf16[512,4608]{1,0:T(8,128)(2,1)}, bf16[512,4608]{1,0:T(8,128)(2,1)}, u32[]{:S(2)}, u32[]{:S(2)}) collective-permute-start(bf16[512,4608]{1,0:T(8,128)(2,1)} %shard_map.329.refs_10_.refs_2_), channel_id=1, source_target_pairs={{0,1},{1,0},{2,3},{3,2},{4,5},{5,4},{6,7},{7,6},{8,9},{9,8},{10,11... | collective-permute-start | bytes 14155784 | tf_op jit(solution)/shard_map/ppermute | solution.py:555
  197.0 407.0 %collective-permute-start.4 = (bf16[512,4608]{1,0:T(8,128)(2,1)}, bf16[512,4608]{1,0:T(8,128)(2,1)}, u32[]{:S(2)}, u32[]{:S(2)}) collective-permute-start(bf16[512,4608]{1,0:T(8,128)(2,1)} %shard_map.330.refs_11_.refs_7_), channel_id=1, source_target_pairs={{0,1},{1,0},{2,3},{3,2},{4,5},{5,4},{6,7},{7,6},{8,9},{9,8},{10,11... | collective-permute-start | bytes 14155784 | tf_op jit(solution)/shard_map/ppermute | solution.py:555
  202.3 371.4 %collective-permute-start.1 = (bf16[512,3072]{1,0:T(8,128)(2,1)}, bf16[512,3072]{1,0:T(8,128)(2,1)}, u32[]{:S(2)}, u32[]{:S(2)}) collective-permute-start(bf16[512,3072]{1,0:T(8,128)(2,1)} %shard_map.332.refs_13_.refs_2_), channel_id=1, source_target_pairs={{0,1},{1,0},{2,3},{3,2},{4,5},{5,4},{6,7},{7,6},{8,9},{9,8},{10,11... | collective-permute-start | bytes 9437192 | tf_op jit(solution)/shard_map/ppermute | solution.py:555
  203.7 2.8 copy-start.1
  206.5 1.6 copy-start.5
  208.1 1.6 copy-start.6
  210.1 16.1 %copy-start.2 = (bf16[512,1024]{1,0:T(8,128)(2,1)}, bf16[512,1024]{1,0:T(8,128)(2,1)S(1)}, u32[]{:S(2)}) copy-start(bf16[512,1024]{1,0:T(8,128)(2,1)S(1)} %shard_map.333.refs_14_.refs_2_) | copy-start | bytes 3145732
  210.1 356.3 %collective-permute-start.2 = (bf16[512,1024]{1,0:T(8,128)(2,1)S(1)}, bf16[512,1024]{1,0:T(8,128)(2,1)}, u32[]{:S(2)}, u32[]{:S(2)}) collective-permute-start(bf16[512,1024]{1,0:T(8,128)(2,1)S(1)} %shard_map.333.refs_14_.refs_2_), channel_id=1, source_target_pairs={{0,1},{1,0},{2,3},{3,2},{4,5},{5,4},{6,7},{7,6},{8,9},{9,8},{10,11... | collective-permute-start | bytes 3145736 | tf_op jit(solution)/shard_map/ppermute | solution.py:555
  210.2 14.5 %copy-start.10 = (f32[8,1024]{1,0:T(8,128)S(1)}, f32[8,1024]{1,0:T(8,128)}, u32[]{:S(2)}) copy-start(f32[8,1024]{1,0:T(8,128)} %get-tuple-element.93) | copy-start | bytes 98308
  226.2 338.2 %copy-start.11 = (f32[512]{0:T(512)S(1)}, f32[512]{0:T(512)}, u32[]{:S(2)}) copy-start(f32[512]{0:T(512)} %param.36) | copy-start | bytes 6148
  226.2 338.2 %copy-start.12 = (f32[512]{0:T(512)S(1)}, f32[512]{0:T(512)}, u32[]{:S(2)}) copy-start(f32[512]{0:T(512)} %param.32) | copy-start | bytes 6148
  226.2 338.8 %copy-start.9 = (f32[3,512]{1,0:T(4,128)S(1)}, f32[3,512]{1,0:T(4,128)}, u32[]{:S(2)}) copy-start(f32[3,512]{1,0:T(4,128)} %param.34) | copy-start | bytes 18436
  566.5 1.2 copy-start.3
  567.7 1.6 copy-start.4

commit v4 on v3

--- a/solution.py
+++ b/solution.py
@@ -79,26 +79,47 @@
 INTO_VMEM = pl.BlockSpec(memory_space=pltpu.VMEM)
 ROWS_DOT = (((1,), (0,)), ((), ()))
 BACK_DOT = (((1,), (1,)), ((), ()))
-KEEP_SLOTS, GOT_SLOTS, GIVE_SLOTS = 5, 3, 2
+KEEP_SLOTS, GOT_SLOTS, TILE_ROWS = 3, 2, 128
 
 
 def kernel_dot(left, right, dims=ROWS_DOT):
     return lax.dot_general(left, right, dims, preferred_element_type=jnp.float32)
 
 
-def finish_kernel(chunks, parts, wholes_count, unused, *refs):
+def finish_kernel(chunks, parts, wholes_count, *refs):
     count = len(chunks)
-    out_keep, out_give, in_keep, in_give = refs[:4]
-    n2t, et, gate_back, up_back, act, small = refs[4:10]
-    refs = refs[10 + unused :]
+    (
+        n2t,
+        et,
+        n1t,
+        masks,
+        gains,
+        rate,
+        gate_back,
+        up_back,
+        act,
+        hidden,
+        convolved,
+        proj,
+        e,
+        back,
+        zt,
+        x,
+        w_in,
+        w_out,
+    ) = refs[:18]
+    masters, moments = refs[18:23], refs[23:28]
+    refs = refs[28:]
     whole_refs = refs[:wholes_count]
-    small_out, square_out = refs[wholes_count : wholes_count + 2]
-    rest = refs[wholes_count + 2 :]
-    plain = sum(1 for chunk in chunks if chunk[0] != "feed")
-    plain_keep, plain_got = rest[:plain], rest[plain : 2 * plain]
-    rest = rest[2 * plain :]
-    keep_ring, got_ring, give_ring, tiles = rest[:4]
-    rest = rest[4:]
+    small_out, square_out, input_grad, hidden_grad, gc_grad, conv_grad, dp = refs[
+        wholes_count : wholes_count + 7
+    ]
+    refs = refs[wholes_count + 7 :]
+    bases, bases_other = refs[:5], refs[5:10]
+    rest = refs[10:]
+    out_keep, out_give, out_got = rest[:3]
+    keep_ring, got_ring, give_buffer, tiles, edge = rest[3:8]
+    rest = rest[8:]
     first_in = rest[:count]
     pieces = rest[count : 2 * count]
     done = rest[2 * count : 3 * count]
@@ -114,6 +135,10 @@
         own_sem,
         load_sem,
         tile_sem,
+        base_send,
+        base_recv,
+        edge_send,
+        edge_recv,
         credit,
     ) = rest[4 * count + 2 :]
 
@@ -140,17 +165,16 @@
     def unit_of(c):
         return chunks[c][2] // 8
 
-    def feed_index(c):
-        return c - plain
+    ringed = [c for c in range(count) if chunks[c][0] == "feed"]
 
     def is_feed(c):
         return chunks[c][0] == "feed"
 
     def keep_of(c):
-        return keep_ring.at[feed_index(c) % KEEP_SLOTS] if is_feed(c) else plain_keep[c]
+        return keep_ring.at[ringed.index(c) % KEEP_SLOTS] if is_feed(c) else out_keep
 
     def got_of(c):
-        return got_ring.at[feed_index(c) % GOT_SLOTS] if is_feed(c) else plain_got[c]
+        return got_ring.at[ringed.index(c) % GOT_SLOTS] if is_feed(c) else out_got
 
     def remote(source, target, c, k, device):
         return pltpu.make_async_remote_copy(
@@ -210,16 +234,7 @@
         )
 
     def over_core(c):
-        if is_feed(c):
-            return remote(give_ring.at[feed_index(c) % GIVE_SLOTS], got_of(c), c, 0, sibling)
-        name, start, rows = chunks[c][0], chunks[c][6], chunks[c][2]
-        source = out_give if name == "out" else in_give
-        return remote(source.at[pl.ds(start, rows)], got_of(c), c, 0, sibling)
-
-    def load_keep(c):
-        name, start, rows = chunks[c][0], chunks[c][6], chunks[c][2]
-        source = out_keep if name == "out" else in_keep
-        return pltpu.make_async_copy(source.at[pl.ds(start, rows)], plain_keep[c], load_sem.at[c])
+        return remote(give_buffer if is_feed(c) else out_give, got_of(c), c, 0, sibling)
 
     def over_first(c, h):
         unit = unit_of(c)
@@ -266,19 +281,25 @@
     def load_tile(c, half):
         part, kind = chunks[c][1]
         cols = tiles.shape[2]
-        source = (gate_back, up_back, act)[kind]
+        place_of = 2 * part + half if kind == 3 else half * parts + part
+        source = (gate_back, up_back, act, dp)[kind]
         return pltpu.make_async_copy(
-            source.at[:, pl.ds((half * parts + part) * cols, cols)], tiles.at[half], tile_sem.at[half]
+            source.at[:, pl.ds(place_of * cols, cols)], tiles.at[half], tile_sem.at[half]
         )
+
+    def next_tiles(c):
+        if c + 1 < count and is_feed(c + 1):
+            for half in range(2):
+                load_tile(c + 1, half).start()
 
     def produce(c):
         if not is_feed(c):
             over_core(c).start()
-            load_keep(c).start()
+            next_tiles(c)
             return
-        index = feed_index(c)
+        index = ringed.index(c)
         kind = chunks[c][1][1]
-        keep, give = keep_of(c), give_ring.at[index % GIVE_SLOTS]
+        keep = keep_of(c)
         rows = n2t.shape[0] // 2
         for half in range(2):
             load_tile(c, half).wait()
@@ -286,26 +307,23 @@
         @pl.loop(0, 2)
         def _(r):
             target = aligned(r * rows, rows)
-            for ref, side in ((keep, core), (give, 1 - core)):
-                if kind < 2:
-                    block = kernel_dot(n2t[aligned(side * rows, rows), :], tiles[r])
+            for ref, side in ((keep, core), (give_buffer, 1 - core)):
+                if kind == 2:
+                    block = kernel_dot(et[target, :], tiles[side])
                 else:
-                    block = kernel_dot(et[target, :], tiles[side])
+                    left = n1t if kind == 3 else n2t
+                    block = kernel_dot(left[aligned(side * rows, rows), :], tiles[r])
                 ref[target, :] = block.astype(jnp.bfloat16)
 
-        if c + 1 < count:
-            for half in range(2):
-                load_tile(c + 1, half).start()
+        next_tiles(c)
         if index >= GOT_SLOTS:
             pl.semaphore_wait(credit, 1)
         over_core(c).start()
 
     def sum_core(c):
-        if not is_feed(c):
-            load_keep(c).wait()
         over_core(c).wait()
         add_into(keep_of(c), 0, keep_of(c), 0, got_of(c), 0, chunks[c][2])
-        if is_feed(c) and c + GOT_SLOTS < count:
+        if is_feed(c) and ringed.index(c) + GOT_SLOTS < len(ringed):
             pl.semaphore_signal(credit, inc=1, device_id=sibling, device_id_type=MESH)
         for h in range(2):
             over_first(c, h).start()
@@ -403,24 +421,187 @@
             device_id_type=MESH,
         )
 
-    small_out[...] = small[...]
+    width = n2t.shape[0]
+    low, full = jnp.bfloat16, jnp.float32
+    blocks = x.shape[0] // TILE_ROWS
+    gain_one, gain_two = gains[0:1, :], gains[1:2, :]
+    tile = lambda cols, k=0: pl.BlockSpec((TILE_ROWS, cols), lambda i: (i, k))
+    turned = lambda cols, k=0: pl.BlockSpec((TILE_ROWS, cols), lambda i: (blocks - 1 - i, k))
+    to_before = pltpu.make_async_remote_copy(
+        src_ref=conv_grad.at[pl.ds(0, 8)],
+        dst_ref=edge,
+        send_sem=edge_send,
+        recv_sem=edge_recv,
+        device_id=(group, lax.rem(place + 3, 4), core),
+        device_id_type=MESH,
+    )
+
+    def run_out_back():
+        def scope(total, w_out_here):
+            load = pltpu.make_async_copy(w_out, w_out_here, load_sem)
+            load.start()
+            total[...] = jnp.zeros_like(total)
+            load.wait()
+
+            def body(h_ref, c_ref, gc_ref, e_ref, back_ref, zt_ref, dh_ref, dgc_ref, dc_ref):
+                values = h_ref[...]
+                upstream = back_ref[...]
+                scale = scale_of(values)
+                inner = jnp.mean(values * gain_two * upstream, axis=-1, keepdims=True)
+                grad = (
+                    e_ref[...].astype(full)
+                    + scale * gain_two * upstream
+                    - values * (scale * scale * scale * inner)
+                )
+                dh_ref[...] = grad
+                rounded = grad.astype(low)
+                small_out[4:5, :] += jnp.sum(upstream * values * scale, axis=0, keepdims=True)
+                mixer_grad = kernel_dot(rounded, w_out_here[...], BACK_DOT)
+                dgc_ref[...] = (mixer_grad * c_ref[...]).astype(low)
+                dc_ref[...] = mixer_grad * gc_ref[...]
+                total[...] += kernel_dot(zt_ref[...], rounded)
+
+            pltpu.emit_pipeline(
+                body,
+                grid=(blocks,),
+                in_specs=[tile(width), tile(width), tile(width, 1), tile(width), tile(width)]
+                + [pl.BlockSpec((width, TILE_ROWS), lambda i: (0, i))],
+                out_specs=[tile(width)] * 3,
+            )(hidden, convolved, proj, e, back, zt, hidden_grad, gc_grad, conv_grad)
+            rows = width // 2
+            for target, side in ((out_keep, core), (out_give, 1 - core)):
+                target[...] = total[aligned(side * rows, rows), :].astype(low)
+
+        pl.run_scoped(scope, pltpu.VMEM((width, width), full), pltpu.VMEM((width, width), low))
+
+        @pl.when(place > 0)
+        def _():
+            to_before.start()
+
+    def run_conv_back():
+        @pl.when(place == 3)
+        def _():
+            edge[...] = jnp.zeros_like(edge)
+
+        @pl.when(place < 3)
+        def _():
+            to_before.wait_recv()
+
+        @pl.when(place > 0)
+        def _():
+            to_before.wait_send()
+
+        def body(dc_ref, dgc_ref, gb_ref, v_ref, masks_ref, dp_ref):
+            grad = dc_ref[...]
+            beside = edge[...]
+            next_one = masks_ref[:, 2:3] * shifted(grad, beside, 1)
+            next_two = masks_ref[:, 3:4] * shifted(grad, beside, 2)
+            edge[...] = grad[:8, :]
+            gate_b, values = gb_ref[...], v_ref[...]
+            mixed = gate_b * values
+            for row, term in ((1, next_two), (2, next_one), (3, grad)):
+                small_out[row : row + 1, :] += jnp.sum(term * mixed, axis=0, keepdims=True)
+            mixed_grad = (
+                gains[4:5, :] * grad + gains[3:4, :] * next_one + gains[2:3, :] * next_two
+            )
+            dp_ref[:, :width] = (mixed_grad * values).astype(low)
+            dp_ref[:, width : 2 * width] = dgc_ref[...]
+            dp_ref[:, 2 * width :] = (mixed_grad * gate_b).astype(low)
+
+        pltpu.emit_pipeline(
+            body,
+            grid=(blocks,),
+            in_specs=[
+                turned(width),
+                turned(width),
+                turned(width),
+                turned(width, 2),
+                turned(masks.shape[1]),
+            ],
+            out_specs=[turned(3 * width)],
+        )(conv_grad, gc_grad, proj, proj, masks, dp)
+
+    def run_in_back():
+        def scope(w_in_here):
+            load = pltpu.make_async_copy(w_in, w_in_here, load_sem)
+            load.start()
+            load.wait()
+
+            def body(dp_ref, x_ref, dh_ref, grad_ref):
+                upstream = kernel_dot(dp_ref[...], w_in_here[...], BACK_DOT)
+                values = x_ref[...].astype(full)
+                scale = scale_of(values)
+                inner = jnp.mean(values * gain_one * upstream, axis=-1, keepdims=True)
+                grad_ref[...] = (
+                    dh_ref[...]
+                    + scale * gain_one * upstream
+                    - values * (scale * scale * scale * inner)
+                ).astype(low)
+                small_out[0:1, :] += jnp.sum(upstream * values * scale, axis=0, keepdims=True)
+
+            pltpu.emit_pipeline(
+                body,
+                grid=(blocks,),
+                in_specs=[tile(3 * width), tile(width), tile(width)],
+                out_specs=[tile(width)],
+            )(dp, x, hidden_grad, input_grad)
+
+        pl.run_scoped(scope, pltpu.VMEM(w_in.shape, low))
+
+    def base_copy(n):
+        return pltpu.make_async_remote_copy(
+            src_ref=bases[n],
+            dst_ref=bases_other[n],
+            send_sem=base_send.at[n],
+            recv_sem=base_recv.at[n],
+            device_id=sibling,
+            device_id_type=MESH,
+        )
+
+    def run_base(n):
+        rows, cols = masters[n].shape
+        step = 128 if cols <= 1024 else 32
+        decay = 1.0 - rate[0] * WEIGHT_DECAY
+        slope = rate[0] * MOMENTUM_BETA
+
+        def body(master, moment, base):
+            base[...] = (master[...] * decay - slope * moment[...]).astype(low)
+
+        block = pl.BlockSpec((step, cols), lambda i: (i, 0))
+        pltpu.emit_pipeline(
+            body, grid=(rows // step,), in_specs=[block, block], out_specs=[block]
+        )(masters[n], moments[n], bases[n])
+        base_copy(n).start()
+
+    work = {
+        3: [run_out_back],
+        4: [run_conv_back],
+        5: [run_in_back],
+        6: [functools.partial(run_base, 2)],
+        7: [functools.partial(run_base, 3)],
+        8: [functools.partial(run_base, 4)],
+        9: [functools.partial(run_base, 0), functools.partial(run_base, 1)],
+    }
+    small_from, squares_from = 8, count + 3
+
+    small_out[...] = jnp.zeros_like(small_out)
     square_out[...] = jnp.zeros_like(square_out)
     for half in range(2):
-        load_tile(plain, half).start()
-    small_copy(0).start()
+        load_tile(0, half).start()
 
     def at(step, action):
         if 0 <= step < count:
             action(step)
 
-    squares_from = count + 3
     for t in range(count + 7):
         at(t, produce)
-        if t < 5:
-            small_copy(t).wait()
-            small_out[...] += small_in[t]
-            if t < 4:
-                small_copy(t + 1).start()
+        if small_from <= t <= small_from + 5:
+            k = t - small_from
+            if k >= 1:
+                small_copy(k - 1).wait()
+                small_out[...] += small_in[k - 1]
+            if k < 5:
+                small_copy(k).start()
         at(t - 1, sum_first)
         at(t - 2, sum_second)
         at(t - 3, sum_middle)
@@ -435,49 +616,67 @@
         at(t, sum_core)
         at(t - 2, sum_end)
         at(t - 4, forward)
+        for item in work.get(t, ()):
+            item()
     for c in range(count):
         drain(c)
-
-
-def finish(out_sides, in_sides, n2t, et, gate_back, up_back, act, parts, small, order):
-    width = n2t.shape[0]
+    for n in range(5):
+        base_copy(n).wait()
+
+
+def finish(feed_ins, mixer_ins, masters, moments, parts):
+    n2t, et, gate_back, up_back, act, back = feed_ins
+    n1t, zt, hidden, convolved, proj, masks, gains, e, x, w_in, w_out, rate = mixer_ins
+    rows, width = x.shape
     half = width // 2
     cols = gate_back.shape[1] // (2 * parts)
-    in_cols = in_sides[0].shape[1]
-    chunks = [("out", None, half, 0, 0, half, 0, width)]
-    chunks += [("in", None, half // 2, 1, t * half // 2, half, t * half // 2, in_cols) for t in range(2)]
+    in_cols = w_in.shape[1]
+    chunks = []
     for part in range(parts):
         for kind in range(3):
             first = (part * 3 + kind) * 2 * width
             chunks.append(("feed", (part, kind), width, 2, first, width, 0, cols))
-    count, plain = len(chunks), 3
-    low = jnp.bfloat16
+    chunks.append(("out", None, half, 0, 0, half, 0, width))
+    in_parts = in_cols // (2 * cols)
+    for part in range(in_parts):
+        chunks.append(("feed", (part, 3), width, 1, part * 2 * width, width, 0, cols))
+    count = len(chunks)
+    low, full = jnp.bfloat16, jnp.float32
+    shape = jax.ShapeDtypeStruct
     semaphore = pltpu.SemaphoreType.DMA
-    wholes = [(width, width), (width, in_cols), (parts * 3 * 2 * width, cols)]
+    wholes = [(width, width), (in_parts * 2 * width, cols), (parts * 3 * 2 * width, cols)]
     eighths = [(chunk[2] // 8, chunk[7]) for chunk in chunks]
-    plain_shapes = [(chunk[2], chunk[7]) for chunk in chunks[:plain]]
-    pair = [pltpu.VMEM((2 * rows, c), low) for rows, c in eighths]
+    pair = [pltpu.VMEM((2 * r, c), low) for r, c in eighths]
     outs = pl.pallas_call(
-        functools.partial(finish_kernel, tuple(chunks), parts, len(wholes), len(order)),
-        out_shape=[jax.ShapeDtypeStruct(shape, low) for shape in wholes]
+        functools.partial(finish_kernel, tuple(chunks), parts, len(wholes)),
+        out_shape=[shape(whole, low) for whole in wholes]
         + [
-            jax.ShapeDtypeStruct((8, small.shape[1]), jnp.float32),
-            jax.ShapeDtypeStruct((8, 128), jnp.float32),
-        ],
-        in_specs=[ANY] * 4 + [INTO_VMEM] * 2 + [ANY] * 3 + [INTO_VMEM] + [ANY] * len(order),
-        out_specs=[ANY] * len(wholes) + [INTO_VMEM] * 2,
-        scratch_shapes=[pltpu.VMEM(shape, low) for shape in plain_shapes] * 2
+            shape((8, width), full),
+            shape((8, 128), full),
+            shape((rows, width), low),
+            shape((rows, width), full),
+            shape((rows, width), low),
+            shape((rows, width), full),
+            shape((rows, in_cols), low),
+        ]
+        + [shape(master.shape, low) for master in masters] * 2,
+        in_specs=[INTO_VMEM] * 3
+        + [ANY, INTO_VMEM, pl.BlockSpec(memory_space=pltpu.SMEM)]
+        + [ANY] * (12 + 2 * len(masters)),
+        out_specs=[ANY] * len(wholes) + [INTO_VMEM] * 2 + [ANY] * (5 + 2 * len(masters)),
+        scratch_shapes=[pltpu.VMEM((half, width), low)] * 3
         + [
             pltpu.VMEM((KEEP_SLOTS, width, cols), low),
             pltpu.VMEM((GOT_SLOTS, width, cols), low),
-            pltpu.VMEM((GIVE_SLOTS, width, cols), low),
-            pltpu.VMEM((2, act.shape[0], cols), low),
+            pltpu.VMEM((width, cols), low),
+            pltpu.VMEM((2, rows, cols), low),
+            pltpu.VMEM((8, width), full),
         ]
-        + [pltpu.VMEM((4 * rows, c), low) for rows, c in eighths]
+        + [pltpu.VMEM((4 * r, c), low) for r, c in eighths]
         + pair * 3
         + [
-            pltpu.VMEM((5, 8, small.shape[1]), jnp.float32),
-            pltpu.VMEM((3, 8, 128), jnp.float32),
+            pltpu.VMEM((5, 8, width), full),
+            pltpu.VMEM((3, 8, 128), full),
             semaphore((count, 22)),
             semaphore((count, 22)),
             semaphore((5,)),
@@ -485,22 +684,47 @@
             semaphore((3,)),
             semaphore((3,)),
             semaphore((count, 2)),
-            semaphore((plain,)),
+            semaphore,
             semaphore((2,)),
+            semaphore((5,)),
+            semaphore((5,)),
+            semaphore,
+            semaphore,
             pltpu.SemaphoreType.REGULAR,
         ],
         compiler_params=pltpu.CompilerParams(
             collective_id=0, has_side_effects=True, vmem_limit_bytes=62 * 1024 * 1024
         ),
-    )(*out_sides, *in_sides, n2t, et, gate_back, up_back, act, small, *order)
-    return outs[: len(wholes)], outs[-2], outs[-1]
-
-
-def feed_kernel(step, n2, e, wg, wu, wd, out, back, act, gate_back, up_back, et):
+    )(
+        n2t,
+        et,
+        n1t,
+        masks,
+        gains,
+        rate,
+        gate_back,
+        up_back,
+        act,
+        hidden,
+        convolved,
+        proj,
+        e,
+        back,
+        zt,
+        x,
+        w_in,
+        w_out,
+        *masters,
+        *moments,
+    )
+    return outs[:3], outs[3], outs[4], outs[5], outs[10:15], outs[15:20]
+
+
+def feed_kernel(step, n2, e, hidden, wg, wu, wd, block_out, back, act, gate_back, up_back, et, out):
     @pl.when(pl.program_id(0) == 0)
     def _():
         et[...] = e[...].T
-        out[...] = jnp.zeros_like(out)
+        out[...] = hidden[...]
         back[...] = jnp.zeros_like(back)
 
     @pl.loop(0, n2.shape[0] // step)
@@ -522,8 +746,12 @@
             low_up, wu[...], BACK_DOT
         )
 
-
-def feed(n2, e, gate_matrix, up_matrix, down_matrix, tiles):
+    @pl.when(pl.program_id(0) == pl.num_programs(0) - 1)
+    def _():
+        block_out[...] = out[...].astype(jnp.bfloat16)
+
+
+def feed(n2, e, hidden, gate_matrix, up_matrix, down_matrix, tiles):
     rows, width = n2.shape
     assert rows == width
     cols = gate_matrix.shape[1] // tiles
@@ -532,27 +760,24 @@
     return pl.pallas_call(
         functools.partial(feed_kernel, rows // 2),
         grid=(tiles,),
-        in_specs=[whole, whole]
+        in_specs=[whole, whole, whole]
         + [pl.BlockSpec((width, cols), lambda i: (0, i))] * 2
         + [pl.BlockSpec((cols, width), lambda i: (i, 0))],
         out_specs=[whole, whole, tile, tile, tile, whole],
-        out_shape=[jax.ShapeDtypeStruct((rows, width), jnp.float32)] * 2
+        out_shape=[
+            jax.ShapeDtypeStruct((rows, width), jnp.bfloat16),
+            jax.ShapeDtypeStruct((rows, width), jnp.float32),
+        ]
         + [jax.ShapeDtypeStruct((rows, tiles * cols), jnp.bfloat16)] * 3
         + [jax.ShapeDtypeStruct((width, rows), jnp.bfloat16)],
+        scratch_shapes=[pltpu.VMEM((rows, width), jnp.float32)],
         cost_estimate=pl.CostEstimate(
             flops=12 * rows * width * cols * tiles,
             bytes_accessed=70 * 1024 * 1024,
             transcendentals=rows * cols * tiles,
         ),
         compiler_params=pltpu.CompilerParams(vmem_limit_bytes=56 * 1024 * 1024),
-    )(n2, e, gate_matrix, up_matrix, down_matrix)
-
-
-CORE_ROUTE = ((0, 1), (1, 0))
-
-
-def over_core(give):
-    return lax.ppermute(give, "shard", CORE_ROUTE)
+    )(n2, e, hidden, gate_matrix, up_matrix, down_matrix)
 
 
 def scale_of(values):
@@ -882,241 +1107,6 @@
     )(x, x, masks, pack, *masters)
 
 
-def out_back_kernel(parts, *refs):
-    h_ref, c_ref, gc_ref, e_ref, gain_two, w_out, zt = refs[:7]
-    outs, backs = refs[7 : 7 + parts], refs[7 + parts : 7 + 2 * parts]
-    block_out, hidden_grad, gc_grad, conv_grad, gain_grad, keep, give, total = refs[-8:]
-    step = pl.program_id(0)
-    core = lax.axis_index("shard")
-    hidden = h_ref[...]
-    gain = gain_two[...]
-    summed = hidden
-    for ref in outs:
-        summed = summed + ref[...]
-    block_out[...] = summed.astype(jnp.bfloat16)
-    upstream = backs[0][...]
-    for ref in backs[1:]:
-        upstream = upstream + ref[...]
-    scale = scale_of(hidden)
-    inner = jnp.mean(hidden * gain * upstream, axis=-1, keepdims=True)
-    grad = (
-        e_ref[...].astype(jnp.float32)
-        + scale * gain * upstream
-        - hidden * (scale * scale * scale * inner)
-    )
-    hidden_grad[...] = grad
-    low = grad.astype(jnp.bfloat16)
-    share = jnp.sum(upstream * hidden * scale, axis=0, keepdims=True)
-    mixer_grad = kernel_dot(low, w_out[...], BACK_DOT)
-    gc_grad[...] = (mixer_grad * c_ref[...]).astype(jnp.bfloat16)
-    conv_grad[...] = mixer_grad * gc_ref[...]
-
-    @pl.when(step == 0)
-    def _():
-        total[...] = jnp.zeros_like(total)
-        gain_grad[...] = jnp.zeros_like(gain_grad)
-
-    gain_grad[0:1, :] += share
-    total[...] += kernel_dot(zt[...], low)
-
-    @pl.when(step == pl.num_programs(0) - 1)
-    def _():
-        rows = total.shape[0] // 2
-        for target, side in ((keep, core), (give, 1 - core)):
-            target[...] = total[pl.ds(pl.multiple_of(side * rows, rows), rows), :].astype(
-                jnp.bfloat16
-            )
-
-
-def skip_last(kernel, inputs, extra):
-    def wrapped(*refs):
-        return kernel(*refs[:inputs], *refs[inputs + extra :])
-
-    return wrapped
-
-
-def out_back(hidden, convolved, proj, e, gain_two, w_out, zt, outs, backs, order):
-    rows, width = hidden.shape
-    step = rows // 4
-    tile = pl.BlockSpec((step, width), lambda i: (i, 0))
-    low, full = jnp.bfloat16, jnp.float32
-    shape = jax.ShapeDtypeStruct
-    inputs = 7 + len(outs) + len(backs)
-    return pl.pallas_call(
-        skip_last(functools.partial(out_back_kernel, len(outs)), inputs, len(order)),
-        grid=(4,),
-        in_specs=[
-            tile,
-            tile,
-            pl.BlockSpec((step, width), lambda i: (i, 1)),
-            tile,
-            resident(gain_two.shape),
-            resident(w_out.shape),
-            pl.BlockSpec((width, step), lambda i: (0, i)),
-        ]
-        + [tile] * (len(outs) + len(backs))
-        + [ANY] * len(order),
-        out_specs=[tile] * 4 + [resident((8, width))] + [resident((width // 2, width))] * 2,
-        out_shape=[
-            shape((rows, width), low),
-            shape((rows, width), full),
-            shape((rows, width), low),
-            shape((rows, width), full),
-            shape((8, width), full),
-            shape((width // 2, width), low),
-            shape((width // 2, width), low),
-        ],
-        scratch_shapes=[pltpu.VMEM((width, width), full)],
-        compiler_params=pltpu.CompilerParams(vmem_limit_bytes=56 * 1024 * 1024),
-        cost_estimate=pl.CostEstimate(
-            flops=4 * rows * width * width, bytes_accessed=48 * rows * width, transcendentals=0
-        ),
-    )(hidden, convolved, proj, e, gain_two, w_out, zt, *outs, *backs, *order)
-
-
-def conv_back_kernel(
-    dc_ref, dgc, gb_ref, v_ref, masks, edge_ref, taps, n1t, dp_ref, taps_grad, keep, give, carry, all_dp
-):
-    step = pl.program_id(0)
-    last = pl.num_programs(0) - 1
-    core = lax.axis_index("shard")
-    rows, width = dc_ref.shape
-    low = jnp.bfloat16
-
-    @pl.when(step == 0)
-    def _():
-        carry[...] = edge_ref[...]
-        taps_grad[...] = jnp.zeros_like(taps_grad)
-
-    grad = dc_ref[...]
-    edge = carry[...]
-    next_one = masks[:, 2:3] * shifted(grad, edge, 1)
-    next_two = masks[:, 3:4] * shifted(grad, edge, 2)
-    carry[...] = grad[:8, :]
-    gate_b, values = gb_ref[...], v_ref[...]
-    mixed = gate_b * values
-    for row, term in ((0, next_two), (1, next_one), (2, grad)):
-        taps_grad[row : row + 1, :] += jnp.sum(term * mixed, axis=0, keepdims=True)
-    mixed_grad = taps[2:3, :] * grad + taps[1:2, :] * next_one + taps[0:1, :] * next_two
-    place = pl.ds(pl.multiple_of((last - step) * rows, rows), rows)
-    for k, block in enumerate(
-        ((mixed_grad * values).astype(low), dgc[...], (mixed_grad * gate_b).astype(low))
-    ):
-        dp_ref[:, k * width : (k + 1) * width] = block
-        all_dp[place, k * width : (k + 1) * width] = block
-
-    @pl.when(step == last)
-    def _():
-        half = width // 2
-        for target, side in ((keep, core), (give, 1 - core)):
-            left = n1t[pl.ds(pl.multiple_of(side * half, half), half), :]
-            for k in range(3):
-                cols = slice(k * width, (k + 1) * width)
-                target[:, cols] = kernel_dot(left, all_dp[:, cols]).astype(low)
-
-
-def conv_back(conv_grad, gc_grad, proj, masks, edge, taps, n1t, order):
-    rows, width = conv_grad.shape
-    step = rows // 4
-    tile = lambda cols, k=0: pl.BlockSpec((step, cols), lambda i: (3 - i, k))
-    low, full = jnp.bfloat16, jnp.float32
-    shape = jax.ShapeDtypeStruct
-    return pl.pallas_call(
-        skip_last(conv_back_kernel, 8, len(order)),
-        grid=(4,),
-        in_specs=[
-            tile(width),
-            tile(width),
-            tile(width, 0),
-            tile(width, 2),
-            tile(masks.shape[1]),
-            resident(edge.shape),
-            resident(taps.shape),
-            resident(n1t.shape),
-        ]
-        + [ANY] * len(order),
-        out_specs=[tile(3 * width), resident((8, width))] + [resident((width // 2, 3 * width))] * 2,
-        out_shape=[
-            shape((rows, 3 * width), low),
-            shape((8, width), full),
-            shape((width // 2, 3 * width), low),
-            shape((width // 2, 3 * width), low),
-        ],
-        scratch_shapes=[pltpu.VMEM((8, width), full), pltpu.VMEM((rows, 3 * width), low)],
-        compiler_params=pltpu.CompilerParams(vmem_limit_bytes=56 * 1024 * 1024),
-        cost_estimate=pl.CostEstimate(
-            flops=6 * rows * width * width, bytes_accessed=32 * rows * width, transcendentals=0
-        ),
-    )(conv_grad, gc_grad, proj, proj, masks, edge, taps, n1t, *order)
-
-
-def in_back_kernel(dp_ref, w_in, x_ref, grad_ref, gain_one, input_grad, gain_grad):
-    upstream = kernel_dot(dp_ref[...], w_in[...], BACK_DOT)
-    x = x_ref[...].astype(jnp.float32)
-    gain = gain_one[...]
-    scale = scale_of(x)
-    inner = jnp.mean(x * gain * upstream, axis=-1, keepdims=True)
-    input_grad[...] = (
-        grad_ref[...] + scale * gain * upstream - x * (scale * scale * scale * inner)
-    ).astype(jnp.bfloat16)
-
-    @pl.when(pl.program_id(0) == 0)
-    def _():
-        gain_grad[...] = jnp.zeros_like(gain_grad)
-
-    gain_grad[0:1, :] += jnp.sum(upstream * x * scale, axis=0, keepdims=True)
-
-
-def in_back(dp, w_in, x, hidden_grad, gain_one, order):
-    rows, width = x.shape
-    step = rows // 4
-    tile = lambda cols: pl.BlockSpec((step, cols), lambda i: (i, 0))
-    return pl.pallas_call(
-        skip_last(in_back_kernel, 5, len(order)),
-        grid=(4,),
-        in_specs=[
-            tile(3 * width),
-            resident(w_in.shape),
-            tile(width),
-            tile(width),
-            resident(gain_one.shape),
-        ]
-        + [ANY] * len(order),
-        out_specs=[tile(width), resident((8, width))],
-        out_shape=[
-            jax.ShapeDtypeStruct((rows, width), jnp.bfloat16),
-            jax.ShapeDtypeStruct((8, width), jnp.float32),
-        ],
-        compiler_params=pltpu.CompilerParams(vmem_limit_bytes=56 * 1024 * 1024),
-        cost_estimate=pl.CostEstimate(
-            flops=6 * rows * width * width, bytes_accessed=20 * rows * width, transcendentals=0
-        ),
-    )(dp, w_in, x, hidden_grad, gain_one, *order)
-
-
-def base_kernel(rate, master, moment, base):
-    base[...] = (
-        master[...] * (1.0 - rate[0] * WEIGHT_DECAY) - (rate[0] * MOMENTUM_BETA) * moment[...]
-    ).astype(jnp.bfloat16)
-
-
-def base_of(rate, master, moment, order):
-    rows, cols = master.shape
-    step = rows // 4
-    tile = pl.BlockSpec((step, cols), lambda i: (i, 0))
-    return pl.pallas_call(
-        skip_last(base_kernel, 3, len(order)),
-        grid=(4,),
-        in_specs=[pl.BlockSpec(memory_space=pltpu.SMEM), tile, tile] + [ANY] * len(order),
-        out_specs=tile,
-        out_shape=jax.ShapeDtypeStruct((rows, cols), jnp.bfloat16),
-        compiler_params=pltpu.CompilerParams(vmem_limit_bytes=40 * 1024 * 1024),
-        cost_estimate=pl.CostEstimate(
-            flops=3 * rows * cols, bytes_accessed=10 * rows * cols, transcendentals=0
-        ),
-    )(rate, master, moment, *order)
-
-
 def update_kernel(bits, scalars, *refs):
     core = bits[2]
     clip, scale = scalars[0], scalars[1]
@@ -1291,54 +1281,36 @@
         up_matrix,
         down_matrix,
     ) = mixer(x, masks, pack, (in_weight, out_weight, gate_weight, up_weight, down_weight))
-    gain_one_row, gain_two_row, conv_taps = gains[0:1], gains[1:2], gains[2:5]
-    feed_out, feed_back, act, gate_back, up_back, et = feed(
-        n2, e, gate_matrix, up_matrix, down_matrix, 2 * FEED_PARTS
-    )
-    block_out, hidden_grad, gc_grad, conv_out_grad, gain_two_grad, out_keep, out_give = out_back(
-        hidden,
-        convolved,
-        proj,
-        e,
-        gain_two_row,
-        out_matrix,
-        zt,
-        [feed_out],
-        [feed_back],
-        [],
-    )
-    after_edge = from_behind(conv_out_grad[:8, :], "seq", -1)
-    proj_back, taps_grad, in_keep, in_give = conv_back(
-        conv_out_grad, gc_grad, proj, masks, after_edge, conv_taps, n1t, []
-    )
-    input_grad, gain_one_grad = in_back(
-        proj_back, in_matrix, x, hidden_grad, gain_one_row, []
+    block_out, back, act, gate_back, up_back, et = feed(
+        n2, e, hidden, gate_matrix, up_matrix, down_matrix, 2 * FEED_PARTS
     )
     rate_now = learn_rate * jnp.minimum(1.0, (step_number + 1).astype(jnp.float32) / WARMUP)
-    rate = rate_now.reshape(1)
-    base, base_other = {}, {}
-    for place in (5, 6, 7, 1, 3):
-        base[place] = base_of(rate, masters[place], moments[place], [proj_back])
-        base_other[place] = over_core(base[place])
+    large = (1, 3, 5, 6, 7)
+    wholes, small_sum, squares, input_grad, bases, bases_other = finish(
+        (n2t, et, gate_back, up_back, act, back),
+        (
+            n1t,
+            zt,
+            hidden,
+            convolved,
+            proj,
+            masks,
+            gains,
+            e,
+            x,
+            in_matrix,
+            out_matrix,
+            rate_now.reshape(1),
+        ),
+        [masters[place] for place in large],
+        [moments[place] for place in large],
+        FEED_PARTS,
+    )
+    base = dict(zip(large, bases))
+    base_other = dict(zip(large, bases_other))
+    cols = gate_matrix.shape[1] // (2 * FEED_PARTS)
     input_grad = input_grad.reshape(tokens.shape)
     block_out = block_out.reshape(tokens.shape)
-    small = jnp.concatenate(
-        [gain_one_grad[:1], taps_grad[:3], gain_two_grad[:1], jnp.zeros((3, model_width))], 0
-    )
-    hidden_units = gate_matrix.shape[1]
-    cols = hidden_units // (2 * FEED_PARTS)
-    wholes, small_sum, squares = finish(
-        (out_keep, out_give),
-        (in_keep, in_give),
-        n2t,
-        et,
-        gate_back,
-        up_back,
-        act,
-        FEED_PARTS,
-        small,
-        [base[place] for place in (5, 6, 7, 1, 3)],
-    )
     param_count = 2 * sum((member.size for member in masters))
     clip_level = CLIP_RATIO * math.sqrt(param_count)
     grad_norm = jnp.sqrt(jnp.sum(squares) + jnp.sum(small_sum * small_sum))
@@ -1382,7 +1354,20 @@
         bits, scalars, wholes[2], FEED_PARTS, base[7], base_other[7], moments[7]
     )
     new_weight[1], new_moment[1] = update_rows(
-        bits, scalars, (6,), (half, half), [plain_matrix(1, wholes[1])]
+        bits,
+        scalars,
+        (in_matrix.shape[1] // narrow // 4, 2, 2),
+        (half, narrow),
+        [
+            (
+                wholes[1],
+                lambda side, k, i, t: (k * 4 + side * 2 + i, t),
+                lambda k, i, t: (k * 2 + i) * 2 + t,
+                base[1],
+                base_other[1],
+                moments[1],
+            )
+        ],
     )
     small_own = lax.dynamic_slice_in_dim(small_sum, core * half, half, 1)
     for place, gradient in ((0, small_own[0]), (2, small_own[1:4]), (4, small_own[4])):

time: 647 us -> 598 us (0.924)
  Pallas kernels: 600 us -> 564 us
  local copies, waits for them, and re-layouts: 17.8 us -> 8.04 us
    pallas_call x8 -> x0, Pallas kernels: 84.4 us -> none  [the longest x5 32.3 us: base_of(): pl.pallas_call(skip_last(base_kernel, 3, len(order)), grid=(4,), in_specs...]
    pallas_call x1, Pallas kernels: 333 us -> 383 us  [finish(): pl.pallas_call(functools.partial(finish_kernel, tuple(chunks), parts, len...]
  transfers between devices with their start and end apart: 6 -> 0, of which waited for: 1 -> 0; matrix products, arithmetic and copies ran while one was open for 1% -> 0% of each run, Pallas kernels for 64% -> 0%
where the time goes in v4:
time: 598 us; the launch traced here: 587 us
  Pallas kernels  564 us (94%)
  other arithmetic  9.39 us (2%)
  local copies, waits for them, and re-layouts  8.04 us (1%)
    pallas_call x1, Pallas kernels, finish(): pl.pallas_call(functools.partial(finish_kernel, tuple(chunks), parts, len...  383 us
    pallas_call x1, Pallas kernels, feed(): pl.pallas_call(functools.partial(feed_kernel, rows // 2), grid=(tiles,),...  73.2 us
    pallas_call x3, Pallas kernels, update_rows(): pl.pallas_call(update_kernel, grid_spec=pltpu.PrefetchScalarGridSpec(num_...  48.9 us
    pallas_call x1, Pallas kernels, mixer(): pl.pallas_call(mixer_kernel, grid=(STEPS + 1,), in_specs=[tile(width), AN...  42.8 us
    pallas_call x1, Pallas kernels, update_down(): pl.pallas_call(update_down_kernel, grid_spec=pltpu.PrefetchScalarGridSpec...  17 us

profile of v4, /device:TPU:0, one launch (start us, length us, event | category | flops | bytes accessed | tf_op | source)
XLA Modules:
  0.0 586.9 jit_solution(2359687459566237013)
XLA Ops:
  0.7 0.8 concatenate.7
  1.5 0.1 compare_bitcast_fusion.3
  1.7 0.3 copy.41
  2.0 0.8 convert_element_type.10.masks.refs_3_
  2.8 0.7 convert.15
  3.5 0.7 convert.14
  4.2 0.7 convert.13
  4.9 0.1 pad.8.clone
  5.0 0.7 maximum_convert_fusion.pack
  5.7 42.8 %shard_map.324 = (f32[1024,3072]{1,0:T(8,128)}, f32[1024,1024]{1,0:T(8,128)}, f32[1024,1024]{1,0:T(8,128)}, bf16[1024,1024]{1,0:T(8,128)(2,1)}, bf16[1024,1024]{...) custom-call(bf16[1024,1024]{1,0:T(8,128)(2,1)} %bitcast.23, ...), custom_call_target="tpu_custom_call" | custom-call | tf_op jit(solution)/shard_map/pallas_call | solution.py:1065
  48.4 73.2 %shard_map.325 = (bf16[1024,1024]{1,0:T(8,128)(2,1)}, f32[1024,1024]{1,0:T(8,128)}, bf16[1024,4608]{1,0:T(8,128)(2,1)}, bf16[1024,4608]{1,0:T(8,128)(2,1)}, bf16...) custom-call(bf16[1024,1024]{1,0:T(8,128)(2,1)} %get-tuple-element.61.n2, bf16[1024,1024]{1,0:T(8,128)(2,1)} %bitcast.26, ...), custom_call_target="tpu_custom_call" | custom-call | flops 57982058496 | bytes 73400320 | tf_op jit(solution)/shard_map/pallas_call | solution.py:760
  123.0 0.0 copy-start.7
  123.0 0.0 copy-start.8
  123.0 382.5 %shard_map.326 = (bf16[1024,1024]{1,0:T(8,128)(2,1)}, bf16[4096,768]{1,0:T(8,128)(2,1)}, bf16[18432,768]{1,0:T(8,128)(2,1)}, f32[8,1024]{1,0:T(8,128)}, f32[8,12...) custom-call(bf16[1024,1024]{1,0:T(8,128)(2,1)} %get-tuple-element.67, ...), custom_call_target="tpu_custom_call" | custom-call | tf_op jit(solution)/shard_map/pallas_call | solution.py:650
  505.5 1.3 reduce_sum.18
  506.8 1.4 multiply_reduce_fusion
  509.6 0.9 dynamic-slice_multiply_fusion.1
  510.4 0.0 copy-done.7
  510.4 0.0 copy-done.8
  510.4 0.6 multiply_add_fusion
  511.0 0.1 pad_add_fusion.1.bits
  511.1 0.1 pad_maximum_fusion.scalars
  511.2 1.9 copy-done.2
  513.1 13.1 %shard_map.327 = (bf16[1024,3072]{1,0:T(8,128)(2,1)}, f32[512,3072]{1,0:T(8,128)}) custom-call(s32[3]{0:T(128)S(1)} %pad_add_fusion.1.bits, f32[2]{0:T(128)S(1)} %pad_maximum_fusion.scalars, bf16[4096,768]{1,0:T(8,128)(2,1)} %get-tuple-element.83.refs_0_.refs_1_, bf16[4096,768]{1,0:T(8,128)(2,1)} %get-tuple-element.83.refs_0_.refs_1_, ...), custom_call_target="tpu_custom_call" | custom-call | flops 12582912 | bytes 31457280 | tf_op jit(solution)/shard_map/pallas_call | solution.py:1150
  526.2 1.4 fusion
  527.6 0.0 copy-done.3
  527.6 1.2 copy-done.4
  528.9 4.6 shard_map.328
  533.4 2.3 copy-done.1
  535.8 31.1 %shard_map.329 = (bf16[1024,4608]{1,0:T(8,128)(2,1)}, f32[512,4608]{1,0:T(8,128)}, bf16[1024,4608]{1,0:T(8,128)(2,1)}, f32[512,4608]{1,0:T(8,128)}) custom-call(s32[3]{0:T(128)S(1)} %pad_add_fusion.1.bits, f32[2]{0:T(128)S(1)} %pad_maximum_fusion.scalars, bf16[18432,768]{1,0:T(8,128)(2,1)} %get-tuple-element.91.refs_0_.refs_1_.refs_5_.refs_6_.own.other, ...), custom_call_target="tpu_custom_call" | custom-call | flops 37748736 | bytes 94371840 | tf_op jit(solution)/shard_map/pallas_call | solution.py:1150
  567.0 17.0 %shard_map.330 = (bf16[2,2304,1024]{2,1,0:T(8,128)(2,1)}, f32[2304,1024]{1,0:T(8,128)}) custom-call(s32[3]{0:T(128)S(1)} %pad_add_fusion.1.bits, f32[2]{0:T(128)S(1)} %pad_maximum_fusion.scalars, bf16[18432,768]{1,0:T(8,128)(2,1)} %get-tuple-element.91.refs_0_.refs_1_.refs_5_.refs_6_.own.other, ...), custom_call_target="tpu_custom_call" | custom-call | flops 18874368 | bytes 47185920 | tf_op jit(solution)/shard_map/pallas_call | solution.py:1177
  584.0 1.3 copy.45
  (20 shorter events, 0.1 us)
Async XLA Ops:
  123.0 387.5 %copy-start.7 = (f32[512]{0:T(512)S(1)}, f32[512]{0:T(512)}, u32[]{:S(2)}) copy-start(f32[512]{0:T(512)} %param.36) | copy-start | bytes 6148
  123.0 387.4 %copy-start.8 = (f32[512]{0:T(512)S(1)}, f32[512]{0:T(512)}, u32[]{:S(2)}) copy-start(f32[512]{0:T(512)} %param.32) | copy-start | bytes 6148
  511.2 1.9 copy-start.2
  513.1 13.1 %copy-start.6 = (f32[3,512]{1,0:T(4,128)S(1)}, f32[3,512]{1,0:T(4,128)}, u32[]{:S(2)}) copy-start(f32[3,512]{1,0:T(4,128)} %param.34) | copy-start | bytes 18436
  513.1 14.6 %copy-start = (bf16[1024,1024]{1,0:T(8,128)(2,1)S(1)}, bf16[1024,1024]{1,0:T(8,128)(2,1)}, u32[]{:S(2)}) copy-start(bf16[1024,1024]{1,0:T(8,128)(2,1)} %get-tuple-element.87.refs_0_.refs_1_) | copy-start | bytes 6291460
  513.1 14.6 %copy-start.3 = (bf16[512,1024]{1,0:T(8,128)(2,1)S(1)}, bf16[512,1024]{1,0:T(8,128)(2,1)}, u32[]{:S(2)}) copy-start(bf16[512,1024]{1,0:T(8,128)(2,1)} %get-tuple-element.88.refs_2_) | copy-start | bytes 3145732
  527.6 1.2 copy-start.4
  528.9 38.1 %slice-start = ((s8[4718592]{0:T(1024)(128)(4,1)}), s8[4194304]{0:T(1024)(128)(4,1)S(1)}, s32[]{:S(2)}) async-start(s8[4718592]{0:T(1024)(128)(4,1)} %bitcast.21), calls=%async_computation | async-start | bytes 8388608
  533.4 2.3 copy-start.1
  535.8 31.2 %slice-start.1 = ((s8[4718592]{0:T(1024)(128)(4,1)}), s8[524288]{0:T(1024)(128)(4,1)S(1)}, s32[]{:S(2)}) async-start(s8[4718592]{0:T(1024)(128)(4,1)} %bitcast.21), calls=%async_computation.1 | async-start | bytes 1048576
  567.0 17.0 %copy-start.5 = (bf16[1024,1024]{1,0:T(8,128)(2,1)S(1)}, bf16[1024,1024]{1,0:T(8,128)(2,1)}, u32[]{:S(2)}) copy-start(bf16[1024,1024]{1,0:T(8,128)(2,1)} %get-tuple-element.80) | copy-start | bytes 6291460

commit v5 on v4

--- a/solution.py
+++ b/solution.py
@@ -574,15 +574,15 @@
         base_copy(n).start()
 
     work = {
-        3: [run_out_back],
-        4: [run_conv_back],
-        5: [run_in_back],
-        6: [functools.partial(run_base, 2)],
-        7: [functools.partial(run_base, 3)],
-        8: [functools.partial(run_base, 4)],
-        9: [functools.partial(run_base, 0), functools.partial(run_base, 1)],
+        2: [run_out_back],
+        3: [run_conv_back],
+        4: [run_in_back],
+        5: [functools.partial(run_base, 2)],
+        6: [functools.partial(run_base, 3)],
+        7: [functools.partial(run_base, 4)],
+        8: [functools.partial(run_base, 0), functools.partial(run_base, 1)],
     }
-    small_from, squares_from = 8, count + 3
+    small_from, squares_from = 6, count + 3
 
     small_out[...] = jnp.zeros_like(small_out)
     square_out[...] = jnp.zeros_like(square_out)
@@ -595,6 +595,8 @@
 
     for t in range(count + 7):
         at(t, produce)
+        at(t - 4, forward)
+        at(t, sum_core)
         if small_from <= t <= small_from + 5:
             k = t - small_from
             if k >= 1:
@@ -613,11 +615,9 @@
             if k < 3:
                 square_copy(k).start()
         at(t - 5, last_hop)
-        at(t, sum_core)
-        at(t - 2, sum_end)
-        at(t - 4, forward)
         for item in work.get(t, ()):
             item()
+        at(t - 2, sum_end)
     for c in range(count):
         drain(c)
     for n in range(5):

time: 598 us -> 584 us (0.977)
  Pallas kernels: 564 us -> 550 us
    pallas_call x1, Pallas kernels: 383 us -> 368 us  [finish(): pl.pallas_call(functools.partial(finish_kernel, tuple(chunks), parts, len...]
where the time goes in v5:
time: 584 us; the launch traced here: 572 us
  Pallas kernels  550 us (94%)
  other arithmetic  9.39 us (2%)
  local copies, waits for them, and re-layouts  8.04 us (1%)
    pallas_call x1, Pallas kernels, finish(): pl.pallas_call(functools.partial(finish_kernel, tuple(chunks), parts, len...  368 us
    pallas_call x1, Pallas kernels, feed(): pl.pallas_call(functools.partial(feed_kernel, rows // 2), grid=(tiles,),...  73.2 us
    pallas_call x3, Pallas kernels, update_rows(): pl.pallas_call(update_kernel, grid_spec=pltpu.PrefetchScalarGridSpec(num_...  48.9 us
    pallas_call x1, Pallas kernels, mixer(): pl.pallas_call(mixer_kernel, grid=(STEPS + 1,), in_specs=[tile(width), AN...  42.8 us
    pallas_call x1, Pallas kernels, update_down(): pl.pallas_call(update_down_kernel, grid_spec=pltpu.PrefetchScalarGridSpec...  17 us

profile of v5, /device:TPU:0, one launch (start us, length us, event | category | flops | bytes accessed | tf_op | source)
XLA Modules:
  0.0 572.5 jit_solution(7199888381386344600)
XLA Ops:
  0.7 0.8 concatenate.7
  1.5 0.1 compare_bitcast_fusion.3
  1.7 0.3 copy.41
  2.0 0.8 convert_element_type.10.masks.refs_3_
  2.8 0.7 convert.15
  3.5 0.7 convert.14
  4.2 0.7 convert.13
  4.9 0.1 pad.8.clone
  5.0 0.7 maximum_convert_fusion.pack
  5.7 42.8 %shard_map.324 = (f32[1024,3072]{1,0:T(8,128)}, f32[1024,1024]{1,0:T(8,128)}, f32[1024,1024]{1,0:T(8,128)}, bf16[1024,1024]{1,0:T(8,128)(2,1)}, bf16[1024,1024]{...) custom-call(bf16[1024,1024]{1,0:T(8,128)(2,1)} %bitcast.23, ...), custom_call_target="tpu_custom_call" | custom-call | tf_op jit(solution)/shard_map/pallas_call | solution.py:1065
  48.4 73.2 %shard_map.325 = (bf16[1024,1024]{1,0:T(8,128)(2,1)}, f32[1024,1024]{1,0:T(8,128)}, bf16[1024,4608]{1,0:T(8,128)(2,1)}, bf16[1024,4608]{1,0:T(8,128)(2,1)}, bf16...) custom-call(bf16[1024,1024]{1,0:T(8,128)(2,1)} %get-tuple-element.61.n2, bf16[1024,1024]{1,0:T(8,128)(2,1)} %bitcast.26, ...), custom_call_target="tpu_custom_call" | custom-call | flops 57982058496 | bytes 73400320 | tf_op jit(solution)/shard_map/pallas_call | solution.py:760
  123.0 0.0 copy-start.7
  123.0 0.0 copy-start.8
  123.0 368.1 %shard_map.326 = (bf16[1024,1024]{1,0:T(8,128)(2,1)}, bf16[4096,768]{1,0:T(8,128)(2,1)}, bf16[18432,768]{1,0:T(8,128)(2,1)}, f32[8,1024]{1,0:T(8,128)}, f32[8,12...) custom-call(bf16[1024,1024]{1,0:T(8,128)(2,1)} %get-tuple-element.67, ...), custom_call_target="tpu_custom_call" | custom-call | tf_op jit(solution)/shard_map/pallas_call | solution.py:650
  491.1 1.3 reduce_sum.18
  492.4 1.4 multiply_reduce_fusion
  495.2 0.9 dynamic-slice_multiply_fusion.1
  496.0 0.0 copy-done.7
  496.0 0.0 copy-done.8
  496.0 0.6 multiply_add_fusion
  496.6 0.1 pad_add_fusion.1.bits
  496.7 0.1 pad_maximum_fusion.scalars
  496.8 1.9 copy-done.2
  498.7 13.1 %shard_map.327 = (bf16[1024,3072]{1,0:T(8,128)(2,1)}, f32[512,3072]{1,0:T(8,128)}) custom-call(s32[3]{0:T(128)S(1)} %pad_add_fusion.1.bits, f32[2]{0:T(128)S(1)} %pad_maximum_fusion.scalars, bf16[4096,768]{1,0:T(8,128)(2,1)} %get-tuple-element.83.refs_0_.refs_1_, bf16[4096,768]{1,0:T(8,128)(2,1)} %get-tuple-element.83.refs_0_.refs_1_, ...), custom_call_target="tpu_custom_call" | custom-call | flops 12582912 | bytes 31457280 | tf_op jit(solution)/shard_map/pallas_call | solution.py:1150
  511.8 1.4 fusion
  513.2 0.0 copy-done.3
  513.2 1.2 copy-done.4
  514.5 4.6 shard_map.328
  519.0 2.3 copy-done.1
  521.4 31.1 %shard_map.329 = (bf16[1024,4608]{1,0:T(8,128)(2,1)}, f32[512,4608]{1,0:T(8,128)}, bf16[1024,4608]{1,0:T(8,128)(2,1)}, f32[512,4608]{1,0:T(8,128)}) custom-call(s32[3]{0:T(128)S(1)} %pad_add_fusion.1.bits, f32[2]{0:T(128)S(1)} %pad_maximum_fusion.scalars, bf16[18432,768]{1,0:T(8,128)(2,1)} %get-tuple-element.91.refs_0_.refs_1_.refs_5_.refs_6_.own.other, ...), custom_call_target="tpu_custom_call" | custom-call | flops 37748736 | bytes 94371840 | tf_op jit(solution)/shard_map/pallas_call | solution.py:1150
  552.6 17.0 %shard_map.330 = (bf16[2,2304,1024]{2,1,0:T(8,128)(2,1)}, f32[2304,1024]{1,0:T(8,128)}) custom-call(s32[3]{0:T(128)S(1)} %pad_add_fusion.1.bits, f32[2]{0:T(128)S(1)} %pad_maximum_fusion.scalars, bf16[18432,768]{1,0:T(8,128)(2,1)} %get-tuple-element.91.refs_0_.refs_1_.refs_5_.refs_6_.own.other, ...), custom_call_target="tpu_custom_call" | custom-call | flops 18874368 | bytes 47185920 | tf_op jit(solution)/shard_map/pallas_call | solution.py:1177
  569.6 1.3 copy.45
  (20 shorter events, 0.1 us)
Async XLA Ops:
  123.0 373.1 %copy-start.7 = (f32[512]{0:T(512)S(1)}, f32[512]{0:T(512)}, u32[]{:S(2)}) copy-start(f32[512]{0:T(512)} %param.36) | copy-start | bytes 6148
  123.0 373.0 %copy-start.8 = (f32[512]{0:T(512)S(1)}, f32[512]{0:T(512)}, u32[]{:S(2)}) copy-start(f32[512]{0:T(512)} %param.32) | copy-start | bytes 6148
  496.8 1.9 copy-start.2
  498.7 13.1 %copy-start.6 = (f32[3,512]{1,0:T(4,128)S(1)}, f32[3,512]{1,0:T(4,128)}, u32[]{:S(2)}) copy-start(f32[3,512]{1,0:T(4,128)} %param.34) | copy-start | bytes 18436
  498.7 14.6 %copy-start = (bf16[1024,1024]{1,0:T(8,128)(2,1)S(1)}, bf16[1024,1024]{1,0:T(8,128)(2,1)}, u32[]{:S(2)}) copy-start(bf16[1024,1024]{1,0:T(8,128)(2,1)} %get-tuple-element.87.refs_0_.refs_1_) | copy-start | bytes 6291460
  498.7 14.6 %copy-start.3 = (bf16[512,1024]{1,0:T(8,128)(2,1)S(1)}, bf16[512,1024]{1,0:T(8,128)(2,1)}, u32[]{:S(2)}) copy-start(bf16[512,1024]{1,0:T(8,128)(2,1)} %get-tuple-element.88.refs_2_) | copy-start | bytes 3145732
  513.2 1.2 copy-start.4
  514.4 38.1 %slice-start = ((s8[4718592]{0:T(1024)(128)(4,1)}), s8[4194304]{0:T(1024)(128)(4,1)S(1)}, s32[]{:S(2)}) async-start(s8[4718592]{0:T(1024)(128)(4,1)} %bitcast.21), calls=%async_computation | async-start | bytes 8388608
  519.0 2.3 copy-start.1
  521.4 31.2 %slice-start.1 = ((s8[4718592]{0:T(1024)(128)(4,1)}), s8[524288]{0:T(1024)(128)(4,1)S(1)}, s32[]{:S(2)}) async-start(s8[4718592]{0:T(1024)(128)(4,1)} %bitcast.21), calls=%async_computation.1 | async-start | bytes 1048576
  552.5 17.0 %copy-start.5 = (bf16[1024,1024]{1,0:T(8,128)(2,1)S(1)}, bf16[1024,1024]{1,0:T(8,128)(2,1)}, u32[]{:S(2)}) copy-start(bf16[1024,1024]{1,0:T(8,128)(2,1)} %get-tuple-element.80) | copy-start | bytes 6291460

commit v6 on v5

--- a/solution.py
+++ b/solution.py
@@ -86,7 +86,7 @@
     return lax.dot_general(left, right, dims, preferred_element_type=jnp.float32)
 
 
-def finish_kernel(chunks, parts, wholes_count, *refs):
+def finish_kernel(chunks, parts, wholes_count, clip_level, *refs):
     count = len(chunks)
     (
         n2t,
@@ -115,8 +115,8 @@
         wholes_count : wholes_count + 7
     ]
     refs = refs[wholes_count + 7 :]
-    bases, bases_other = refs[:5], refs[5:10]
-    rest = refs[10:]
+    bases, bases_other, scalars = refs[:5], refs[5:10], refs[10]
+    rest = refs[11:]
     out_keep, out_give, out_got = rest[:3]
     keep_ring, got_ring, give_buffer, tiles, edge = rest[3:8]
     rest = rest[8:]
@@ -210,10 +210,7 @@
     def add_into(target, target_row, one, one_row, two, two_row, rows):
         def body(i, carry):
             at = lambda start: aligned(start + i * 16, 16)
-            total = one[at(one_row), :].astype(jnp.float32) + two[at(two_row), :].astype(
-                jnp.float32
-            )
-            target[at(target_row), :] = total.astype(jnp.bfloat16)
+            target[at(target_row), :] = one[at(one_row), :] + two[at(two_row), :]
             return carry
 
         lax.fori_loop(0, rows // 16, body, 0)
@@ -618,13 +615,20 @@
         for item in work.get(t, ()):
             item()
         at(t - 2, sum_end)
+    grads = small_out[...]
+    total = jnp.sum(square_out[...], keepdims=True) + jnp.sum(grads * grads, keepdims=True)
+    norm = jnp.sqrt(total)
+    clip = clip_level / jnp.maximum(norm, clip_level)
+    scalars[...] = jnp.zeros_like(scalars)
+    for row, value in enumerate((clip, rate[0] * clip, norm)):
+        scalars[row : row + 1, :] = jnp.broadcast_to(value, (1, 128))
     for c in range(count):
         drain(c)
     for n in range(5):
         base_copy(n).wait()
 
 
-def finish(feed_ins, mixer_ins, masters, moments, parts):
+def finish(feed_ins, mixer_ins, masters, moments, clip_level, parts):
     n2t, et, gate_back, up_back, act, back = feed_ins
     n1t, zt, hidden, convolved, proj, masks, gains, e, x, w_in, w_out, rate = mixer_ins
     rows, width = x.shape
@@ -648,7 +652,7 @@
     eighths = [(chunk[2] // 8, chunk[7]) for chunk in chunks]
     pair = [pltpu.VMEM((2 * r, c), low) for r, c in eighths]
     outs = pl.pallas_call(
-        functools.partial(finish_kernel, tuple(chunks), parts, len(wholes)),
+        functools.partial(finish_kernel, tuple(chunks), parts, len(wholes), clip_level),
         out_shape=[shape(whole, low) for whole in wholes]
         + [
             shape((8, width), full),
@@ -659,11 +663,15 @@
             shape((rows, width), full),
             shape((rows, in_cols), low),
         ]
-        + [shape(master.shape, low) for master in masters] * 2,
+        + [shape(master.shape, low) for master in masters] * 2
+        + [shape((8, 128), full)],
         in_specs=[INTO_VMEM] * 3
         + [ANY, INTO_VMEM, pl.BlockSpec(memory_space=pltpu.SMEM)]
         + [ANY] * (12 + 2 * len(masters)),
-        out_specs=[ANY] * len(wholes) + [INTO_VMEM] * 2 + [ANY] * (5 + 2 * len(masters)),
+        out_specs=[ANY] * len(wholes)
+        + [INTO_VMEM] * 2
+        + [ANY] * (5 + 2 * len(masters))
+        + [INTO_VMEM],
         scratch_shapes=[pltpu.VMEM((half, width), low)] * 3
         + [
             pltpu.VMEM((KEEP_SLOTS, width, cols), low),
@@ -717,7 +725,7 @@
         *masters,
         *moments,
     )
-    return outs[:3], outs[3], outs[4], outs[5], outs[10:15], outs[15:20]
+    return outs[:3], outs[3], outs[5], outs[10:15], outs[15:20], outs[20]
 
 
 def feed_kernel(step, n2, e, hidden, wg, wu, wd, block_out, back, act, gate_back, up_back, et, out):
@@ -1109,7 +1117,7 @@
 
 def update_kernel(bits, scalars, *refs):
     core = bits[2]
-    clip, scale = scalars[0], scalars[1]
+    clip, scale = scalars[0:1, 0:1], scalars[1:2, 0:1]
     count = len(refs) // 7
     for n in range(count):
         own, other, base_own, base_other, moment = refs[5 * n : 5 * n + 5]
@@ -1146,7 +1154,7 @@
             jax.ShapeDtypeStruct((rows, cols), jnp.float32),
         ]
         operands += [gradient, gradient, base, base_other, moment]
-    in_specs = [pl.BlockSpec(memory_space=pltpu.SMEM)] + in_specs
+    in_specs = [INTO_VMEM] + in_specs
     return pl.pallas_call(
         update_kernel,
         grid_spec=pltpu.PrefetchScalarGridSpec(
@@ -1160,7 +1168,7 @@
 
 def update_down_kernel(bits, scalars, own, other, base_own, base_other, moment, weight, new_moment):
     core = bits[2]
-    clip, scale = scalars[0], scalars[1]
+    clip, scale = scalars[0:1, 0:1], scalars[1:2, 0:1]
     gradient = own[...].astype(jnp.float32).T
     new_moment[...] = MOMENTUM_BETA * moment[...] + clip * gradient
     weight[core] = (base_own[...].astype(jnp.float32) - scale * gradient).astype(jnp.bfloat16)
@@ -1180,7 +1188,7 @@
             num_scalar_prefetch=1,
             grid=(parts, subs),
             in_specs=[
-                pl.BlockSpec(memory_space=pltpu.SMEM),
+                INTO_VMEM,
                 pl.BlockSpec((width, step), lambda k, t, b: ((k * 3 + 2) * 2 + b[2], t)),
                 pl.BlockSpec((width, step), lambda k, t, b: ((k * 3 + 2) * 2 + 1 - b[2], t)),
                 row,
@@ -1286,7 +1294,9 @@
     )
     rate_now = learn_rate * jnp.minimum(1.0, (step_number + 1).astype(jnp.float32) / WARMUP)
     large = (1, 3, 5, 6, 7)
-    wholes, small_sum, squares, input_grad, bases, bases_other = finish(
+    param_count = 2 * sum((member.size for member in masters))
+    clip_level = CLIP_RATIO * math.sqrt(param_count)
+    wholes, small_sum, input_grad, bases, bases_other, scalars = finish(
         (n2t, et, gate_back, up_back, act, back),
         (
             n1t,
@@ -1304,6 +1314,7 @@
         ),
         [masters[place] for place in large],
         [moments[place] for place in large],
+        clip_level,
         FEED_PARTS,
     )
     base = dict(zip(large, bases))
@@ -1311,11 +1322,7 @@
     cols = gate_matrix.shape[1] // (2 * FEED_PARTS)
     input_grad = input_grad.reshape(tokens.shape)
     block_out = block_out.reshape(tokens.shape)
-    param_count = 2 * sum((member.size for member in masters))
-    clip_level = CLIP_RATIO * math.sqrt(param_count)
-    grad_norm = jnp.sqrt(jnp.sum(squares) + jnp.sum(small_sum * small_sum))
-    clip_factor = clip_level / jnp.maximum(grad_norm, clip_level)
-    scalars = jnp.stack([clip_factor, rate_now * clip_factor])
+    clip_factor, grad_norm = scalars[0, 0], scalars[2, 0]
     half = model_width // 2
     narrow = cols // 2
 

time: 584 us -> 581 us (level)
  no operation moved by 1% of the time
where the time goes in v6:
time: 581 us; the launch traced here: 570 us
  Pallas kernels  550 us (95%)
  local copies, waits for them, and re-layouts  9.99 us (2%)
  other arithmetic  7.96 us (1%)
    pallas_call x1, Pallas kernels, finish(): pl.pallas_call(functools.partial(finish_kernel, tuple(chunks), parts, len...  365 us
    pallas_call x1, Pallas kernels, feed(): pl.pallas_call(functools.partial(feed_kernel, rows // 2), grid=(tiles,),...  73.2 us
    pallas_call x3, Pallas kernels, update_rows(): pl.pallas_call(update_kernel, grid_spec=pltpu.PrefetchScalarGridSpec(num_...  51.4 us
    pallas_call x1, Pallas kernels, mixer(): pl.pallas_call(mixer_kernel, grid=(STEPS + 1,), in_specs=[tile(width), AN...  42.7 us
    pallas_call x1, Pallas kernels, update_down(): pl.pallas_call(update_down_kernel, grid_spec=pltpu.PrefetchScalarGridSpec...  17 us

profile of v6, /device:TPU:0, one launch (start us, length us, event | category | flops | bytes accessed | tf_op | source)
XLA Modules:
  0.0 570.0 jit_solution(11747272143194082041)
XLA Ops:
  0.7 0.8 concatenate.7
  1.5 0.1 compare_bitcast_fusion.3
  1.7 0.3 copy.41
  2.0 0.8 convert_element_type.10.masks.refs_3_
  2.8 0.7 convert.15
  3.5 0.7 convert.14
  4.2 0.7 convert.13
  4.9 0.1 pad.6.clone
  5.0 0.7 maximum_convert_fusion.pack
  5.7 42.7 %shard_map.324 = (f32[1024,3072]{1,0:T(8,128)}, f32[1024,1024]{1,0:T(8,128)}, f32[1024,1024]{1,0:T(8,128)}, bf16[1024,1024]{1,0:T(8,128)(2,1)}, bf16[1024,1024]{...) custom-call(bf16[1024,1024]{1,0:T(8,128)(2,1)} %bitcast.23, ...), custom_call_target="tpu_custom_call" | custom-call | tf_op jit(solution)/shard_map/pallas_call | solution.py:1073
  48.4 73.2 %shard_map.325 = (bf16[1024,1024]{1,0:T(8,128)(2,1)}, f32[1024,1024]{1,0:T(8,128)}, bf16[1024,4608]{1,0:T(8,128)(2,1)}, bf16[1024,4608]{1,0:T(8,128)(2,1)}, bf16...) custom-call(bf16[1024,1024]{1,0:T(8,128)(2,1)} %get-tuple-element.61.n2, bf16[1024,1024]{1,0:T(8,128)(2,1)} %bitcast.26, ...), custom_call_target="tpu_custom_call" | custom-call | flops 57982058496 | bytes 73400320 | tf_op jit(solution)/shard_map/pallas_call | solution.py:768
  123.0 0.0 copy-start.9
  123.0 0.0 copy-start.10
  123.0 365.1 %shard_map.326 = (bf16[1024,1024]{1,0:T(8,128)(2,1)}, bf16[4096,768]{1,0:T(8,128)(2,1)}, bf16[18432,768]{1,0:T(8,128)(2,1)}, f32[8,1024]{1,0:T(8,128)}, f32[8,12...) custom-call(bf16[1024,1024]{1,0:T(8,128)(2,1)} %get-tuple-element.67, ...), custom_call_target="tpu_custom_call" | custom-call | tf_op jit(solution)/shard_map/pallas_call | solution.py:654
  488.1 1.3 fusion.1
  489.4 1.5 dynamic-slice_multiply_fusion.1
  490.9 0.6 multiply_add_fusion
  491.5 0.1 pad_add_fusion.1.bits
  491.6 1.9 copy-done.2
  493.5 0.7 copy-done.5
  494.2 14.1 %shard_map.327 = (bf16[1024,3072]{1,0:T(8,128)(2,1)}, f32[512,3072]{1,0:T(8,128)}) custom-call(s32[3]{0:T(128)S(1)} %pad_add_fusion.1.bits, f32[8,128]{1,0:T(8,128)S(1)} %copy-done.5, bf16[4096,768]{1,0:T(8,128)(2,1)} %get-tuple-element.83.refs_0_.refs_1_, bf16[4096,768]{1,0:T(8,128)(2,1)} %get-tuple-element.83.refs_0_.refs_1_, ...), custom_call_target="tpu_custom_call" | custom-call | flops 12582912 | bytes 31457280 | tf_op jit(solution)/shard_map/pallas_call | solution.py:1158
  508.3 2.0 fusion
  510.3 0.0 copy-done.3
  510.3 1.2 copy-done.4
  511.5 5.2 shard_map.328
  516.7 2.3 copy-done.1
  519.1 32.1 %shard_map.329 = (bf16[1024,4608]{1,0:T(8,128)(2,1)}, f32[512,4608]{1,0:T(8,128)}, bf16[1024,4608]{1,0:T(8,128)(2,1)}, f32[512,4608]{1,0:T(8,128)}) custom-call(s32[3]{0:T(128)S(1)} %pad_add_fusion.1.bits, f32[8,128]{1,0:T(8,128)S(1)} %copy-done.6, bf16[18432,768]{1,0:T(8,128)(2,1)} %get-tuple-element.91.refs_0_.refs_1_.refs_5_.refs_6_.own.other, ...), custom_call_target="tpu_custom_call" | custom-call | flops 37748736 | bytes 94371840 | tf_op jit(solution)/shard_map/pallas_call | solution.py:1158
  551.2 0.0 slice-done
  551.2 0.0 slice-done.1
  551.3 0.0 copy-start.7
  551.3 17.0 %shard_map.330 = (bf16[2,2304,1024]{2,1,0:T(8,128)(2,1)}, f32[2304,1024]{1,0:T(8,128)}) custom-call(s32[3]{0:T(128)S(1)} %pad_add_fusion.1.bits, f32[8,128]{1,0:T(8,128)S(1)} %copy-done.6, bf16[18432,768]{1,0:T(8,128)(2,1)} %get-tuple-element.91.refs_0_.refs_1_.refs_5_.refs_6_.own.other, ...), custom_call_target="tpu_custom_call" | custom-call | flops 18874368 | bytes 47185920 | tf_op jit(solution)/shard_map/pallas_call | solution.py:1185
  568.3 1.3 copy.45
  (22 shorter events, 0.1 us)
Async XLA Ops:
  123.0 368.0 %copy-start.9 = (f32[512]{0:T(512)S(1)}, f32[512]{0:T(512)}, u32[]{:S(2)}) copy-start(f32[512]{0:T(512)} %param.36) | copy-start | bytes 6148
  123.0 368.0 %copy-start.10 = (f32[512]{0:T(512)S(1)}, f32[512]{0:T(512)}, u32[]{:S(2)}) copy-start(f32[512]{0:T(512)} %param.32) | copy-start | bytes 6148
  491.6 1.9 copy-start.2
  493.5 0.7 copy-start.5
  494.2 14.1 %copy-start.8 = (f32[3,512]{1,0:T(4,128)S(1)}, f32[3,512]{1,0:T(4,128)}, u32[]{:S(2)}) copy-start(f32[3,512]{1,0:T(4,128)} %param.34) | copy-start | bytes 18436
  494.2 16.2 %copy-start = (bf16[1024,1024]{1,0:T(8,128)(2,1)S(1)}, bf16[1024,1024]{1,0:T(8,128)(2,1)}, u32[]{:S(2)}) copy-start(bf16[1024,1024]{1,0:T(8,128)(2,1)} %get-tuple-element.87.refs_0_.refs_1_) | copy-start | bytes 6291460
  494.2 16.2 %copy-start.3 = (bf16[512,1024]{1,0:T(8,128)(2,1)S(1)}, bf16[512,1024]{1,0:T(8,128)(2,1)}, u32[]{:S(2)}) copy-start(bf16[512,1024]{1,0:T(8,128)(2,1)} %get-tuple-element.88.refs_2_) | copy-start | bytes 3145732
  494.2 16.2 %copy-start.6 = (f32[8,128]{1,0:T(8,128)S(1)}, f32[8,128]{1,0:T(8,128)}, u32[]{:S(2)}) copy-start(f32[8,128]{1,0:T(8,128)} %get-tuple-element.81.scalars) | copy-start | bytes 12292
  510.3 1.2 copy-start.4
  511.5 39.7 %slice-start = ((s8[4718592]{0:T(1024)(128)(4,1)}), s8[4194304]{0:T(1024)(128)(4,1)S(1)}, s32[]{:S(2)}) async-start(s8[4718592]{0:T(1024)(128)(4,1)} %bitcast.21), calls=%async_computation | async-start | bytes 8388608
  516.7 2.3 copy-start.1
  519.1 32.2 %slice-start.1 = ((s8[4718592]{0:T(1024)(128)(4,1)}), s8[524288]{0:T(1024)(128)(4,1)S(1)}, s32[]{:S(2)}) async-start(s8[4718592]{0:T(1024)(128)(4,1)} %bitcast.21), calls=%async_computation.1 | async-start | bytes 1048576
  551.3 17.0 %copy-start.7 = (bf16[1024,1024]{1,0:T(8,128)(2,1)S(1)}, bf16[1024,1024]{1,0:T(8,128)(2,1)}, u32[]{:S(2)}) copy-start(bf16[1024,1024]{1,0:T(8,128)(2,1)} %get-tuple-element.80) | copy-start | bytes 6291460
